TPU v7x, 1024 devices: a whole 4x8x16 slice. The times are simulated.
1024 devices in a mesh: node: 64 (over y, x, core), local: 16 (over z).
Axes of the slice: x: 4, y: 8, z: 16, core: 2. Of those that a mesh axis runs over, the one named last changes fastest.
Arguments:
- d_out: bfloat16 [4096, 6144], P('local', 'node'), may hold values from -2.5 to 2.5
- node_ids: int32 [4096, 4], P('local'), may hold values from 0 to 63, as said below
- gates: float32 [64, 16, 32, 2], P('node'), may hold values from 0.1 to 1
- hidden: bfloat16 [64, 16, 32, 2, 1024], P('node', None, None, None, 'local'), may hold values from -2.5 to 2.5
- w_down: bfloat16 [128, 1024, 6144], P('node', 'local'), may hold values from -0.1875 to 0.1875
Outputs:
- d_hidden: bfloat16 [64, 16, 32, 2, 1024], P('node', None, None, None, 'local')
- d_down: bfloat16 [128, 1024, 6144], P('node', 'local')
- d_gates: float32 [4096, 4, 2], P('local')
Inputs may be any that keep to these rules, and one draw needn't show every extreme that they name: `node_ids`: each token names 4 different node groups. Within the 256 tokens of one shard, every node group is named by at most 32 tokens, and some node group by exactly 32.
All inputs are finite; a program needn't handle non-finite values.
Results may differ from a plain program's by a relative error of at most 0.0049.
Values may be sent and summed in bfloat16 or wider, within the bound.
No kernel may reach another device: no remote copies, remote signals or barrier semaphores. Data moves between devices by JAX's collectives and lax.ppermute only.
A program may use at most 64 MiB of HBM per device.

v0:
```python
import jax
import jax.numpy as jnp
from jax import lax
from jax.sharding import PartitionSpec as P


def expert_work(gathered, w_down, saved, gating):
    upward = jnp.einsum("erd,efd->ref", gathered, w_down, preferred_element_type=jnp.float32)
    weighted = (gating[:, :, None] * jnp.swapaxes(gathered, 0, 1).astype(jnp.float32)).astype(
        jnp.bfloat16
    )
    grad_h = (gating[:, :, None] * upward).astype(jnp.bfloat16)
    partial_value = jnp.sum(saved.astype(jnp.float32) * upward, axis=-1)
    grad_w = jnp.einsum("ref,red->efd", saved, weighted, preferred_element_type=jnp.float32)
    return (grad_h, grad_w.astype(jnp.bfloat16), partial_value)


def per_device(d_out, node_ids, gates, hidden, w_down):
    tok_count = node_ids.shape[0]
    node_count = lax.axis_size("node")
    local_count = lax.axis_size("local")
    capacity = gates.shape[2]
    per_dev = gates.shape[3]
    width = d_out.shape[1] * node_count
    slice_ff = hidden.shape[4]
    node_range = jnp.arange(node_count, dtype=jnp.int32)
    slot_range = jnp.arange(capacity, dtype=jnp.int32)
    picked = node_ids[:, :, None] == node_range[None, None, :]
    member = jnp.any(picked, axis=1).astype(jnp.int32)
    before = jnp.cumsum(member, axis=0) - member
    placed = (member[:, :, None] == 1) & (before[:, :, None] == slot_range[None, None, :])
    placer = placed.reshape(tok_count, node_count * capacity).T.astype(jnp.bfloat16)
    packed = jnp.dot(placer, d_out, preferred_element_type=jnp.float32).astype(jnp.bfloat16)
    packed = packed.reshape(node_count, capacity, d_out.shape[1])
    saved = hidden.reshape(local_count * capacity, per_dev, slice_ff)
    gating = gates.reshape(local_count * capacity, per_dev)
    doubled = jnp.broadcast_to(packed[:, None], (node_count, per_dev, capacity, d_out.shape[1]))
    arrived = lax.all_to_all(doubled, "node", split_axis=0, concat_axis=3, tiled=True).reshape(
        per_dev, capacity, width
    )
    gathered = lax.all_gather(arrived, "local", axis=1, tiled=True)
    grad_h, grad_w, partial_value = expert_work(gathered, w_down, saved, gating)
    d_hidden = grad_h.reshape(1, local_count, capacity, per_dev, slice_ff)
    own_sums = lax.psum_scatter(
        partial_value.reshape(local_count, capacity, per_dev),
        "local",
        scatter_dimension=0,
        tiled=True,
    )
    table = lax.all_gather(own_sums, "node", axis=0, tiled=True)
    slot_pick = jnp.sum(picked.astype(jnp.int32) * before[:, None, :], axis=2)
    lookup = picked[:, :, :, None] & (
        slot_pick[:, :, None, None] == slot_range[None, None, None, :]
    )
    lookup = lookup.astype(jnp.float32).reshape(
        tok_count * node_ids.shape[1], node_count * capacity
    )
    d_gates = jnp.dot(
        lookup,
        table.reshape(node_count * capacity, per_dev),
        precision=lax.Precision.HIGHEST,
        preferred_element_type=jnp.float32,
    )
    return (d_hidden, grad_w, d_gates.reshape(tok_count, node_ids.shape[1], per_dev))


def solution(mesh):
    return jax.shard_map(
        per_device,
        mesh=mesh,
        in_specs=(
            P("local", "node"),
            P("local", None),
            P("node", None, None, None),
            P("node", None, None, None, "local"),
            P("node", "local", None),
        ),
        out_specs=(
            P("node", None, None, None, "local"),
            P("node", "local", None),
            P("local", None, None),
        ),
        check_vma=False,
    )
```

profile of v0, /device:TPU:1, one launch (start us, length us, event | category | flops | bytes accessed | tf_op | source)
XLA Modules:
  0.0 332.1 jit_solution(4206204688020891643)
XLA Ops:
  7.3 0.8 iota_compare_fusion
  8.2 0.6 reduce-window.6
  8.8 0.2 slice_reduce_fusion
  9.0 0.1 convert_subtract_fusion
  9.1 0.5 fusion.14
  9.7 1.3 convolution_convert_fusion
  10.9 0.3 copy.27
  11.2 0.2 broadcast_in_dim.5
  11.4 45.7 %all_to_all.15 = bf16[64,2,32,96]{3,2,1,0:T(8,128)(2,1)S(1)} all-to-all(bf16[64,2,32,96]{3,2,1,0:T(8,128)(2,1)S(1)} %broadcast_in_dim.5), channel_id=1, replica_groups=mesh['node'=64,'local'=16] {'node'}, dimensions={0} | all-to-all | bytes 1572864 | tf_op jit(solution)/shard_map/all_to_all | solution.py:38
  57.1 0.7 copy.28
  57.8 2.3 reshape.66
  60.2 0.1 mul.29
  60.3 0.1 copy.32
  60.4 1.3 dynamic-slice
  61.8 148.2 %all-gather.2.cloned.1.call-done = bf16[2,512,6144]{2,1,0:T(8,128)(2,1)} async-done(((bf16[2,32,6144]{2,1,0:T(8,128)(2,1)}), bf16[2,512,6144]{2,1,0:T(8,128)(2,1)}) %all-gather.2.cloned.1.call-update) | async-done | bytes 12582928 | tf_op jit(solution)/shard_map/all_gather | solution.py:41
  210.0 8.5 %multiply_reduce_fusion = (f32[512,2]{0,1:T(2,128)S(1)}, bf16[512,2,64]{0,2,1:T(8,128)(2,1)S(1)}) fusion(bf16[512,2,64]{0,2,1:T(8,128)(2,1)S(1)} %copy.32, f32[512,2]{0,1:T(2,128)S(1)} %mul.29, bf16[2,512,6144]{2,1,0:T(8,128)(2,1)} %all-gather.2.cloned.1.call-done, bf16[2,64,6144]{2,1,0:T(8,128)(2,1)S(1)} %copy-done), kind=kOutput, calls=%fused_computation.15 | convolution fusion | flops 805633024 | bytes 14426112 | tf_op jit(solution)/shard_map/erd,efd->ref/dot_general | solution.py:8
  218.7 40.3 %all-reduce = f32[16,32,2]{1,2,0:T(2,128)S(1)} all-reduce(f32[16,32,2]{1,2,0:T(2,128)S(1)} %copy.33), channel_id=2, replica_groups=mesh['node'=64,'local'=16] {'local'}, use_global_device_ids=true, to_apply=%region_5.6.clone | all-reduce | flops 1024 | bytes 8192
  259.0 0.6 constant_dynamic-slice_fusion
  259.6 53.1 %all_gather.7 = f32[64,32,2]{1,2,0:T(2,128)S(1)} all-gather(f32[1,32,2]{1,2,0:T(2,128)S(1)} %constant_dynamic-slice_fusion), channel_id=1, replica_groups=mesh['node'=64,'local'=16] {'node'}, dimensions={0}, use_global_device_ids=true | all-gather | bytes 16640 | tf_op jit(solution)/shard_map/all_gather | solution.py:50
  312.7 0.1 copy.34
  312.8 0.2 copy.29
  313.0 1.0 copy.35
  314.0 2.8 fusion.15
  316.8 8.5 %fusion.9 = bf16[2,64,6144]{2,1,0:T(8,128)(2,1)} fusion(bf16[512,2,64]{2,0,1:T(8,128)(2,1)S(1)} %bitcast.65, bf16[2,512,6144]{2,1,0:T(8,128)(2,1)} %all-gather.2.cloned.1.call-done, f32[512,2]{0,1:T(2,128)S(1)} %mul.29), kind=kOutput, calls=%fused_computation.7 | convolution fusion | flops 824967168 | bytes 14290944 | tf_op jit(solution)/shard_map/ref,red->efd/dot_general | solution.py:14
  (22 shorter events, 0.4 us)
Async XLA Ops:
  7.2 202.9 %copy-start = (bf16[2,64,6144]{2,1,0:T(8,128)(2,1)S(1)}, bf16[2,64,6144]{2,1,0:T(8,128)(2,1)}, u32[]{:S(2)}) copy-start(bf16[2,64,6144]{2,1,0:T(8,128)(2,1)} %param.9) | copy-start | bytes 4718596
  7.2 202.9 %all-gather.2.cloned.1.call-start = ((), (), s32[]{:S(2)}) async-start(), calls=%async_computation.1 | async-start | bytes 13369344 | tf_op jit(solution)/shard_map/all_gather | solution.py:41
  11.4 48.7 %copy-start.2 = (f32[1,16,32,2]{2,3,1,0:T(2,128)S(1)}, f32[1,16,32,2]{2,3,1,0:T(2,128)}, u32[]{:S(2)}) copy-start(f32[1,16,32,2]{2,3,1,0:T(2,128)} %param.7) | copy-start | bytes 12292
  11.4 48.8 %copy-start.1 = (bf16[1,16,32,2,64]{4,3,2,1,0:T(2,128)(2,1)S(1)}, bf16[1,16,32,2,64]{4,3,2,1,0:T(2,128)(2,1)}, u32[]{:S(2)}) copy-start(bf16[1,16,32,2,64]{4,3,2,1,0:T(2,128)(2,1)} %param.8) | copy-start | bytes 393220
  57.1 4.6 %copy-start.3 = (s32[256,4]{0,1:T(4,128)S(1)}, s32[256,4]{0,1:T(4,128)}, u32[]{:S(2)}) copy-start(s32[256,4]{0,1:T(4,128)} %param.6) | copy-start | bytes 12292
Sparse Core Ops, SparseCore 0:
  60.3 149.7 all-gather.1
where the time goes:
time: 333 us; the launch traced here: 332 us
  waiting for transfers between devices  148 us (44%)
  blocking collectives  139 us (42%)
  matrix products  21.1 us (6%)
  between operations  14.2 us (4%)
  local copies, waits for them, and re-layouts  7.23 us (2%)
    all_gather x1, waiting for transfers between devices, per_device(): gathered = lax.all_gather(arrived, 'local', axis=1, tiled=True)  148 us
    all_gather x1, blocking collectives, per_device(): table = lax.all_gather(own_sums, 'node', axis=0, tiled=True)  53.1 us
    all_to_all x1, blocking collectives, per_device(): lax.all_to_all(doubled, 'node', split_axis=0, concat_axis=3, tiled=True)  45.7 us
    unnamed x1, blocking collectives  40.3 us
    dot_general x1, matrix products, expert_work(): jnp.einsum('erd,efd->ref', gathered, w_down, preferred_element_type=jnp.f...  8.52 us
    dot_general x1, matrix products, expert_work(): jnp.einsum('ref,red->efd', saved, weighted, preferred_element_type=jnp.fl...  8.52 us
  transfers between devices with their start and end apart: 1, of which 1 were waited for; matrix products, arithmetic and copies ran while one was open for 0% of the time, Pallas kernels for 0%

commit v1 on v0

v1 whole, which is shorter than its diff:
```python
import functools

import jax
import jax.numpy as jnp
from jax import lax
from jax.experimental import pallas as pl
from jax.experimental.pallas import tpu as pltpu
from jax.sharding import PartitionSpec as P

BF = jnp.bfloat16
F32 = jnp.float32


def dot(a, b, dims=(((1,), (0,)), ((), ()))):
    return lax.dot_general(a, b, dims, preferred_element_type=F32)


def pack_kernel(ids_ref, rows_ref, out_ref):
    groups, toks = ids_ref.shape
    nodes, cap, cols = out_ref.shape
    node = lax.broadcasted_iota(jnp.int32, (nodes, toks), 0)
    member = node == ids_ref[0:1, :]
    for k in range(1, groups):
        member = member | (node == ids_ref[k : k + 1, :])
    earlier = lax.broadcasted_iota(jnp.int32, (toks, toks), 0) < lax.broadcasted_iota(
        jnp.int32, (toks, toks), 1
    )
    before = dot(
        jnp.where(member, 1.0, 0.0).astype(BF), jnp.where(earlier, 1.0, 0.0).astype(BF)
    )
    code = jnp.where(member, before, -1.0).astype(jnp.int32)
    slot = lax.broadcasted_iota(jnp.int32, (nodes, cap, toks), 1)
    placed = jnp.where(code[:, None, :] == slot, 1.0, 0.0).astype(BF)
    out = dot(placed.reshape(nodes * cap, toks), rows_ref[...])
    out_ref[...] = out.astype(BF).reshape(nodes, cap, cols)


def pack(ids, rows, nodes, cap):
    return pl.pallas_call(
        pack_kernel,
        out_shape=jax.ShapeDtypeStruct((nodes, cap, rows.shape[1]), BF),
        compiler_params=pltpu.CompilerParams(vmem_limit_bytes=32 * 1024 * 1024),
        name="pack",
    )(ids, rows)


def up_kernel(rows_ref, w_ref, saved_ref, gate_ref, dh_ref, part_ref, acc_ref):
    step = pl.program_id(0)

    @pl.when(step == 0)
    def _():
        acc_ref[...] = jnp.zeros_like(acc_ref)

    acc_ref[...] += dot(rows_ref[...], w_ref[...], (((1,), (1,)), ((), ())))

    @pl.when(step == pl.num_programs(0) - 1)
    def _():
        up = acc_ref[...]
        dh_ref[...] = (gate_ref[...] * up).astype(BF)
        prod = saved_ref[...].astype(F32) * up
        count, per_dev, cap = part_ref.shape
        width = prod.shape[1] // per_dev
        pick = jnp.where(
            lax.broadcasted_iota(jnp.int32, (8, prod.shape[1]), 0)
            == lax.broadcasted_iota(jnp.int32, (8, prod.shape[1]), 1) // width,
            1.0,
            0.0,
        )
        for at in range(count):
            sums = lax.dot_general(
                pick,
                prod[at * cap : (at + 1) * cap],
                (((1,), (1,)), ((), ())),
                precision=lax.Precision.HIGHEST,
                preferred_element_type=F32,
            )
            part_ref[at] = sums[:per_dev]


def up(rows, w, saved, gate, count, per_dev, tile):
    slots, width = rows.shape
    units = w.shape[0]
    whole = lambda i: (0, 0)
    return pl.pallas_call(
        up_kernel,
        grid=(width // tile,),
        in_specs=[
            pl.BlockSpec((slots, tile), lambda i: (0, i)),
            pl.BlockSpec((units, tile), lambda i: (0, i)),
            pl.BlockSpec((slots, units), whole),
            pl.BlockSpec((slots, units), whole),
        ],
        out_specs=[
            pl.BlockSpec((slots, units), whole),
            pl.BlockSpec((count, per_dev, slots // count), lambda i: (0, 0, 0)),
        ],
        out_shape=[
            jax.ShapeDtypeStruct((slots, units), BF),
            jax.ShapeDtypeStruct((count, per_dev, slots // count), F32),
        ],
        scratch_shapes=[pltpu.VMEM((slots, units), F32)],
        compiler_params=pltpu.CompilerParams(vmem_limit_bytes=32 * 1024 * 1024),
        cost_estimate=pl.CostEstimate(
            flops=2 * slots * units * width,
            bytes_accessed=2 * (slots + units) * width,
            transcendentals=0,
        ),
        name="up",
    )(rows, w, saved, gate)


def down_kernel(hi_ref, lo_ref, rows_ref, out_ref):
    rows = rows_ref[...]
    out_ref[...] = (dot(hi_ref[...], rows) + dot(lo_ref[...], rows)).astype(BF)


def down(hi, lo, rows, tile):
    slots, width = rows.shape
    units = hi.shape[0]
    whole = lambda i: (0, 0)
    return pl.pallas_call(
        down_kernel,
        grid=(width // tile,),
        in_specs=[
            pl.BlockSpec((units, slots), whole),
            pl.BlockSpec((units, slots), whole),
            pl.BlockSpec((slots, tile), lambda i: (0, i)),
        ],
        out_specs=pl.BlockSpec((units, tile), lambda i: (0, i)),
        out_shape=jax.ShapeDtypeStruct((units, width), BF),
        compiler_params=pltpu.CompilerParams(vmem_limit_bytes=32 * 1024 * 1024),
        cost_estimate=pl.CostEstimate(
            flops=4 * slots * units * width,
            bytes_accessed=2 * (slots + units) * width,
            transcendentals=0,
        ),
        name="down",
    )(hi, lo, rows)


def look_kernel(ids_ref, slot_ref, table_ref, out_ref):
    toks, groups = ids_ref.shape
    nodes, wide = table_ref.shape
    per_dev = out_ref.shape[1] // groups
    cap = wide // per_dev
    table = table_ref[...]
    node = lax.broadcasted_iota(jnp.int32, (toks, nodes), 1)
    lane = lax.broadcasted_iota(jnp.int32, (toks, wide), 1)
    found = []
    for k in range(groups):
        hot = jnp.where(ids_ref[:, k : k + 1] == node, 1.0, 0.0)
        line = lax.dot_general(
            hot,
            table,
            (((1,), (0,)), ((), ())),
            precision=lax.Precision.HIGHEST,
            preferred_element_type=F32,
        )
        for j in range(per_dev):
            mine = lane == slot_ref[:, k : k + 1] + j * cap
            found.append(jnp.sum(jnp.where(mine, line, 0.0), axis=1, keepdims=True))
    out_ref[...] = jnp.concatenate(found, axis=1)


def look(ids, slot, table, per_dev):
    return pl.pallas_call(
        look_kernel,
        out_shape=jax.ShapeDtypeStruct((ids.shape[0], ids.shape[1] * per_dev), F32),
        compiler_params=pltpu.CompilerParams(vmem_limit_bytes=32 * 1024 * 1024),
        name="look",
    )(ids, slot, table)


def slots_of(ids, nodes):
    picked = ids[:, :, None] == jnp.arange(nodes, dtype=jnp.int32)[None, None, :]
    member = jnp.any(picked, axis=1).astype(jnp.int32)
    before = jnp.cumsum(member, axis=0) - member
    return jnp.sum(picked.astype(jnp.int32) * before[:, None, :], axis=2)


def largest_tile(width, most):
    return max(t for t in range(128, most + 1, 128) if width % t == 0)


def per_device(d_out, node_ids, gates, hidden, w_down):
    nodes = lax.axis_size("node")
    local = lax.axis_size("local")
    cap, per_dev = gates.shape[2:]
    units = hidden.shape[4]
    width = d_out.shape[1] * nodes
    tile = largest_tile(width, 1024)

    packed = pack(node_ids.T, d_out, nodes, cap)
    arrived = lax.all_to_all(packed, "node", split_axis=0, concat_axis=2, tiled=True)
    arrived = arrived.reshape(cap, width)
    rows = lax.all_gather(arrived, "local", axis=0, tiled=True)

    slot = slots_of(node_ids, nodes)
    saved = hidden.reshape(local * cap, per_dev * units)
    gate = jnp.broadcast_to(
        gates.reshape(local * cap, per_dev, 1), (local * cap, per_dev, units)
    ).reshape(local * cap, per_dev * units)
    scaled = (saved.astype(F32) * gate).T
    hi = scaled.astype(BF)
    lo = (scaled - hi.astype(F32)).astype(BF)

    w = w_down.reshape(per_dev * units, width)
    grad_h, part = up(rows, w, saved, gate, local, per_dev, tile)
    got = lax.all_to_all(part, "local", split_axis=0, concat_axis=0, tiled=True)
    own = jnp.sum(got, axis=0)
    table = lax.all_to_all(
        jnp.broadcast_to(own[None], (nodes, per_dev, cap)),
        "node",
        split_axis=0,
        concat_axis=0,
        tiled=True,
    )
    grad_w = down(hi, lo, rows, tile)
    d_gates = look(node_ids, slot, table.reshape(nodes, per_dev * cap), per_dev)
    return (
        grad_h.reshape(1, local, cap, per_dev, units),
        grad_w.reshape(per_dev, units, width),
        d_gates.reshape(node_ids.shape + (per_dev,)),
    )


def solution(mesh):
    return jax.shard_map(
        per_device,
        mesh=mesh,
        in_specs=(
            P("local", "node"),
            P("local", None),
            P("node", None, None, None),
            P("node", None, None, None, "local"),
            P("node", "local", None),
        ),
        out_specs=(
            P("node", None, None, None, "local"),
            P("node", "local", None),
            P("local", None, None),
        ),
        check_vma=False,
    )
```

time: 333 us -> 191 us (0.57)
  blocking collectives: 139 us -> 35.2 us
  waiting for transfers between devices: 148 us -> 96.6 us
  matrix products: 21.1 us -> 0 us
  starting transfers between devices: 0.04 us -> 20.9 us
  Pallas kernels: 0 us -> 10.9 us
  local copies, waits for them, and re-layouts: 7.23 us -> 12.1 us
    all_gather x1, waiting for transfers between devices: 148 us -> 83.6 us  [per_device(): rows = lax.all_gather(arrived, 'local', axis=0, tiled=True)]
    all_gather x1 -> x0, blocking collectives: 53.1 us -> none  [per_device(): table = lax.all_gather(own_sums, 'node', axis=0, tiled=True)]
    unnamed x1 -> x0, blocking collectives: 40.3 us -> none
    dot_general x4 -> x0, matrix products: 21.1 us -> none  [the longest x1 8.52 us: expert_work(): jnp.einsum('erd,efd->ref', gathered, w_down, preferred_element_type=jnp.f...]
    all_to_all x0 -> x2, starting transfers between devices: none -> 20.9 us  [the longest x1 11.8 us: per_device(): lax.all_to_all(jnp.broadcast_to(own[None], (nodes, per_dev, cap)), 'node'...]
    all_to_all x0 -> x2, waiting for transfers between devices: none -> 13.1 us  [the longest x1 10.9 us: per_device(): got = lax.all_to_all(part, 'local', split_axis=0, concat_axis=0, tiled=True)]
    pallas_call x0 -> x4, Pallas kernels: none -> 10.9 us  [the longest x1 4.38 us: up(): pl.pallas_call(up_kernel, grid=(width // tile,), in_specs=[pl.BlockSpec((...]
    all_to_all x1, blocking collectives: 45.7 us -> 35.2 us  [per_device(): lax.all_to_all(packed, 'node', split_axis=0, concat_axis=2, tiled=True)]
  transfers between devices with their start and end apart: 1 -> 3, of which waited for: 1 -> 3; matrix products, arithmetic and copies ran while one was open for 0% -> 1% of each run, Pallas kernels for 0% -> 2%
where the time goes in v1:
time: 191 us
  waiting for transfers between devices  96.6 us (51%)
  blocking collectives  35.2 us (18%)
  starting transfers between devices  20.9 us (11%)
  between operations  14.2 us (7%)
  local copies, waits for them, and re-layouts  12.1 us (6%)
  Pallas kernels  10.9 us (6%)
    all_gather x1, waiting for transfers between devices, per_device(): rows = lax.all_gather(arrived, 'local', axis=0, tiled=True)  83.6 us
    all_to_all x1, blocking collectives, per_device(): lax.all_to_all(packed, 'node', split_axis=0, concat_axis=2, tiled=True)  35.2 us
    all_to_all x1, starting transfers between devices, per_device(): lax.all_to_all(jnp.broadcast_to(own[None], (nodes, per_dev, cap)), 'node'...  11.8 us
    all_to_all x1, waiting for transfers between devices, per_device(): got = lax.all_to_all(part, 'local', split_axis=0, concat_axis=0, tiled=True)  10.9 us
    all_to_all x1, starting transfers between devices, per_device(): got = lax.all_to_all(part, 'local', split_axis=0, concat_axis=0, tiled=True)  9.08 us
    unnamed x17, local copies, waits for them, and re-layouts  7.31 us
    pallas_call x1, Pallas kernels, up(): pl.pallas_call(up_kernel, grid=(width // tile,), in_specs=[pl.BlockSpec((...  4.38 us
    pallas_call x1, Pallas kernels, down(): pl.pallas_call(down_kernel, grid=(width // tile,), in_specs=[pl.BlockSpec...  4.23 us
  transfers between devices with their start and end apart: 3, of which 3 were waited for; matrix products, arithmetic and copies ran while one was open for 1% of the time, Pallas kernels for 2%

profile of v1, /device:TPU:1, one launch (start us, length us, event | category | flops | bytes accessed | tf_op | source)
XLA Modules:
  0.0 191.0 jit_solution(9573780562728527943)
XLA Ops:
  7.2 0.9 copy.41.rows_ref
  8.1 0.7 copy-done.3
  8.8 0.6 pack.1
  9.4 35.2 %all_to_all.25 = bf16[64,32,96]{2,1,0:T(8,128)(2,1)S(1)} all-to-all(bf16[64,32,96]{2,1,0:T(8,128)(2,1)S(1)} %pack.1), channel_id=1, replica_groups=mesh['node'=64,'local'=16] {'node'}, dimensions={0} | all-to-all | bytes 786432 | tf_op jit(solution)/shard_map/all_to_all | solution.py:194
  44.6 0.2 copy.42
  44.9 1.5 reshape.47
  46.6 0.1 reshape.49.saved_ref
  46.9 0.6 reduce-window.6
  47.5 0.2 slice_reduce_fusion
  47.8 83.6 %all-gather.2.cloned.1.call-done.rows_ref = bf16[512,6144]{1,0:T(8,128)(2,1)} async-done(((bf16[32,6144]{1,0:T(8,128)(2,1)}), bf16[512,6144]{1,0:T(8,128)(2,1)}) %all-gather.2.cloned.1.call-update) | async-done | bytes 6291472 | tf_op jit(solution)/shard_map/all_gather | solution.py:196
  131.4 2.8 %copy-done = bf16[512,6144]{1,0:T(8,128)(2,1)S(1)} copy-done((bf16[512,6144]{1,0:T(8,128)(2,1)S(1)}, bf16[512,6144]{1,0:T(8,128)(2,1)}, u32[]{:S(2)}) %copy-start) | copy-done | bytes 6291480
  134.1 4.4 %up.1 = (bf16[512,128]{1,0:T(8,128)(2,1)S(1)}, f32[16,2,32]{2,1,0:T(2,128)}) custom-call(bf16[512,6144]{1,0:T(8,128)(2,1)S(1)} %copy-done, bf16[128,6144]{1,0:T(8,128)(2,1)S(1)} %bitcast.44, bf16[512,128]{1,0:T(8,128)(2,1)S(1)} %reshape.49.saved_ref, f32[512,128]{1,0:T(8,128)S(1)} %copy.44.gate_ref), custom_call_target="tpu_custom_call" | custom-call | flops 805306368 | bytes 7864320 | tf_op jit(solution)/shard_map/up/pallas_call | solution.py:84
  138.5 9.1 %all-to-all-start.1 = ((f32[16,2,32]{2,1,0:T(2,128)}), f32[16,2,32]{2,1,0:T(2,128)S(1)}, u32[]{:S(2)}, u32[]{:S(2)}) async-start(f32[16,2,32]{2,1,0:T(2,128)} %get-tuple-element.6), calls=%async_computation.1 | async-start | bytes 32768 | tf_op jit(solution)/shard_map/all_to_all | solution.py:209
  147.7 0.1 copy.49.ids_ref
  148.0 0.1 copy.50.slot_ref
  148.1 10.9 %all-to-all-done.1 = f32[16,2,32]{2,1,0:T(2,128)S(1)} async-done(((f32[16,2,32]{2,1,0:T(2,128)}), f32[16,2,32]{2,1,0:T(2,128)S(1)}, u32[]{:S(2)}, u32[]{:S(2)}) %all-to-all-start.1) | async-done | bytes 4128 | tf_op jit(solution)/shard_map/all_to_all | solution.py:209
  159.0 0.6 broadcast_in_dim.8
  159.7 11.8 %all-to-all-start.2 = ((f32[64,2,32]{2,1,0:T(2,128)}), f32[64,2,32]{2,1,0:T(2,128)S(1)}, u32[]{:S(2)}, u32[]{:S(2)}) async-start(f32[64,2,32]{2,1,0:T(2,128)} %broadcast_in_dim.8), calls=%async_computation.2 | async-start | bytes 131072 | tf_op jit(solution)/shard_map/all_to_all | solution.py:211
  171.5 2.8 %copy-done.1 = bf16[512,6144]{1,0:T(8,128)(2,1)S(1)} copy-done((bf16[512,6144]{1,0:T(8,128)(2,1)S(1)}, bf16[512,6144]{1,0:T(8,128)(2,1)}, u32[]{:S(2)}) %copy-start.1) | copy-done | bytes 6291480
  174.3 4.2 %down.1 = bf16[128,6144]{1,0:T(8,128)(2,1)} custom-call(bf16[128,512]{1,0:T(8,128)(2,1)S(1)} %bitcast_convert_fusion.hi_ref, bf16[128,512]{1,0:T(8,128)(2,1)S(1)} %fusion.lo_ref, bf16[512,6144]{1,0:T(8,128)(2,1)S(1)} %copy-done.1), custom_call_target="tpu_custom_call" | custom-call | flops 1610612736 | bytes 7864320 | tf_op jit(solution)/shard_map/down/pallas_call | solution.py:121
  178.5 0.8 reshape.51
  179.3 2.2 %all-to-all-done.2 = f32[64,2,32]{2,1,0:T(2,128)S(1)} async-done(((f32[64,2,32]{2,1,0:T(2,128)}), f32[64,2,32]{2,1,0:T(2,128)S(1)}, u32[]{:S(2)}, u32[]{:S(2)}) %all-to-all-start.2) | async-done | bytes 16416 | tf_op jit(solution)/shard_map/all_to_all | solution.py:211
  181.7 1.7 look.1
  183.5 0.6 reshape.56
  (30 shorter events, 0.9 us)
Async XLA Ops:
  7.2 124.2 %all-gather.2.cloned.1.call-start = ((), (), s32[]{:S(2)}) async-start(), calls=%async_computation.3 | async-start | bytes 6684672 | tf_op jit(solution)/shard_map/all_gather | solution.py:196
  8.1 0.7 copy-start.3
  9.4 37.0 %copy-start.6 = (f32[1,16,32,2]{2,3,1,0:T(2,128)S(1)}, f32[1,16,32,2]{2,3,1,0:T(2,128)}, u32[]{:S(2)}) copy-start(f32[1,16,32,2]{2,3,1,0:T(2,128)} %param.7) | copy-start | bytes 12292
  44.6 2.0 %copy-start.5 = (bf16[1,16,32,2,64]{4,3,2,1,0:T(2,128)(2,1)S(1)}, bf16[1,16,32,2,64]{4,3,2,1,0:T(2,128)(2,1)}, u32[]{:S(2)}) copy-start(bf16[1,16,32,2,64]{4,3,2,1,0:T(2,128)(2,1)} %param.8) | copy-start | bytes 393220
  44.6 2.1 %copy-start.4 = (s32[256,4]{0,1:T(4,128)S(1)}, s32[256,4]{0,1:T(4,128)}, u32[]{:S(2)}) copy-start(s32[256,4]{0,1:T(4,128)} %param.6) | copy-start | bytes 12292
  44.9 86.5 %copy-start.2 = (bf16[2,64,6144]{2,1,0:T(8,128)(2,1)S(1)}, bf16[2,64,6144]{2,1,0:T(8,128)(2,1)}, u32[]{:S(2)}) copy-start(bf16[2,64,6144]{2,1,0:T(8,128)(2,1)} %param.9) | copy-start | bytes 4718596
  131.4 2.8 %copy-start = (bf16[512,6144]{1,0:T(8,128)(2,1)S(1)}, bf16[512,6144]{1,0:T(8,128)(2,1)}, u32[]{:S(2)}) copy-start(bf16[512,6144]{1,0:T(8,128)(2,1)} %all-gather.2.cloned.1.call-done.rows_ref) | copy-start | bytes 18874372
  138.5 20.5 %all-to-all-start.1 = ((f32[16,2,32]{2,1,0:T(2,128)}), f32[16,2,32]{2,1,0:T(2,128)S(1)}, u32[]{:S(2)}, u32[]{:S(2)}) async-start(f32[16,2,32]{2,1,0:T(2,128)} %get-tuple-element.6), calls=%async_computation.1 | async-start | bytes 32768 | tf_op jit(solution)/shard_map/all_to_all | solution.py:209
  159.7 21.9 %all-to-all-start.2 = ((f32[64,2,32]{2,1,0:T(2,128)}), f32[64,2,32]{2,1,0:T(2,128)S(1)}, u32[]{:S(2)}, u32[]{:S(2)}) async-start(f32[64,2,32]{2,1,0:T(2,128)} %broadcast_in_dim.8), calls=%async_computation.2 | async-start | bytes 131072 | tf_op jit(solution)/shard_map/all_to_all | solution.py:211
  171.5 2.8 %copy-start.1 = (bf16[512,6144]{1,0:T(8,128)(2,1)S(1)}, bf16[512,6144]{1,0:T(8,128)(2,1)}, u32[]{:S(2)}) copy-start(bf16[512,6144]{1,0:T(8,128)(2,1)} %all-gather.2.cloned.1.call-done.rows_ref) | copy-start | bytes 18874372
Sparse Core Ops, SparseCore 0:
  46.5 84.8 all-gather.1

commit v2 on v1

v2 whole, which is shorter than its diff:
```python
import functools

import jax
import jax.numpy as jnp
from jax import lax
from jax.experimental import pallas as pl
from jax.experimental.pallas import tpu as pltpu
from jax.sharding import PartitionSpec as P

BF = jnp.bfloat16
F32 = jnp.float32
VMEM = 16 * 1024 * 1024


def dot(a, b, dims=(((1,), (0,)), ((), ()))):
    return lax.dot_general(a, b, dims, preferred_element_type=F32)


def pack_kernel(ids_ref, rows_ref, out_ref, slot_ref):
    groups, toks = ids_ref.shape
    nodes, cap, cols = out_ref.shape
    node = lax.broadcasted_iota(jnp.int32, (nodes, toks), 0)
    picked = [node == ids_ref[k : k + 1, :] for k in range(groups)]
    member = picked[0]
    for k in range(1, groups):
        member = member | picked[k]
    earlier = lax.broadcasted_iota(jnp.int32, (toks, toks), 0) < lax.broadcasted_iota(
        jnp.int32, (toks, toks), 1
    )
    before = dot(
        jnp.where(member, 1.0, 0.0).astype(BF), jnp.where(earlier, 1.0, 0.0).astype(BF)
    )
    code = jnp.where(member, before, -1.0).astype(jnp.int32)
    slot = lax.broadcasted_iota(jnp.int32, (nodes, cap, toks), 1)
    placed = jnp.where(code[:, None, :] == slot, 1.0, 0.0).astype(BF)
    out = dot(placed.reshape(nodes * cap, toks), rows_ref[...])
    out_ref[...] = out.astype(BF).reshape(nodes, cap, cols)
    for k in range(groups):
        mine = jnp.sum(jnp.where(picked[k], before, 0.0), axis=0, keepdims=True)
        slot_ref[k : k + 1, :] = mine.astype(jnp.int32)


def pack(ids, rows, nodes, cap):
    return pl.pallas_call(
        pack_kernel,
        out_shape=[
            jax.ShapeDtypeStruct((nodes, cap, rows.shape[1]), BF),
            jax.ShapeDtypeStruct(ids.shape, jnp.int32),
        ],
        compiler_params=pltpu.CompilerParams(vmem_limit_bytes=VMEM),
        name="pack",
    )(ids, rows)


def scale_kernel(shard_ref, saved_ref, gate_ref, hi_ref, lo_ref):
    shards, cap, wide = saved_ref.shape
    per_dev = gate_ref.shape[2]
    owner = lax.broadcasted_iota(jnp.int32, (cap, wide), 1) // (wide // per_dev)
    for at in range(shards):
        shard = shard_ref[at]
        scaled = saved_ref[shard].astype(F32) * spread(gate_ref[shard], owner)
        hi = scaled.astype(BF)
        hi_ref[at * cap : (at + 1) * cap] = hi
        lo_ref[at * cap : (at + 1) * cap] = (scaled - hi.astype(F32)).astype(BF)


def spread(gates, owner):
    gate = gates[:, 0:1]
    for j in range(1, gates.shape[1]):
        gate = jnp.where(owner == j, gates[:, j : j + 1], gate)
    return gate


def scale(order, saved, gates):
    shards, cap, wide = saved.shape
    vmem = pl.BlockSpec(memory_space=pltpu.VMEM)
    return pl.pallas_call(
        scale_kernel,
        in_specs=[pl.BlockSpec(memory_space=pltpu.SMEM), vmem, vmem],
        out_shape=[jax.ShapeDtypeStruct((shards * cap, wide), BF)] * 2,
        compiler_params=pltpu.CompilerParams(vmem_limit_bytes=VMEM),
        name="scale",
    )(order, saved, gates)


def up_kernel(*refs):
    *row_refs, w_ref, out_ref = refs
    rows = jnp.concatenate([r[...] for r in row_refs], axis=0)
    out_ref[...] = dot(rows, w_ref[...], (((1,), (1,)), ((), ())))


def up(blocks, w):
    slots, (units, width) = sum(b.shape[0] for b in blocks), w.shape
    return pl.pallas_call(
        up_kernel,
        out_shape=jax.ShapeDtypeStruct((slots, units), F32),
        compiler_params=pltpu.CompilerParams(vmem_limit_bytes=VMEM),
        cost_estimate=pl.CostEstimate(
            flops=2 * slots * units * width,
            bytes_accessed=2 * (slots + units) * width,
            transcendentals=0,
        ),
        name="up",
    )(*blocks, w)


def close_kernel(shard_ref, *refs):
    *up_refs, saved_ref, gate_ref, dh_ref, part_ref = refs
    _, per_dev, cap = part_ref.shape
    wide = saved_ref.shape[2]
    pick = jnp.where(
        lax.broadcasted_iota(jnp.int32, (8, wide), 0)
        == lax.broadcasted_iota(jnp.int32, (8, wide), 1) // (wide // per_dev),
        1.0,
        0.0,
    )
    left = lax.broadcasted_iota(jnp.int32, (cap, wide), 1) // (wide // per_dev)
    at = 0
    for ref in up_refs:
        for row in range(0, ref.shape[0], cap):
            shard = shard_ref[at]
            at += 1
            u = ref[row : row + cap, :]
            gate = spread(gate_ref[shard], left)
            dh_ref[shard] = (gate * u).astype(BF)
            sums = lax.dot_general(
                pick,
                saved_ref[shard].astype(F32) * u,
                (((1,), (1,)), ((), ())),
                precision=lax.Precision.HIGHEST,
                preferred_element_type=F32,
            )
            part_ref[shard] = sums[:per_dev]


def close(order, ups, saved, gates):
    shards, cap, per_dev = gates.shape
    vmem = pl.BlockSpec(memory_space=pltpu.VMEM)
    return pl.pallas_call(
        close_kernel,
        in_specs=[pl.BlockSpec(memory_space=pltpu.SMEM)] + [vmem] * (len(ups) + 2),
        out_shape=[
            jax.ShapeDtypeStruct(saved.shape, BF),
            jax.ShapeDtypeStruct((shards, per_dev, cap), F32),
        ],
        compiler_params=pltpu.CompilerParams(vmem_limit_bytes=VMEM),
        name="close",
    )(order, *ups, saved, gates)


def down_kernel(count, hi_ref, lo_ref, *refs):
    row_refs, rest = refs[:count], refs[count:]
    rows = jnp.concatenate([r[...] for r in row_refs], axis=0)
    out_ref = rest[-1]
    total = dot(
        jnp.concatenate([hi_ref[...], lo_ref[...]], axis=0),
        jnp.concatenate([rows, rows], axis=0),
        (((0,), (0,)), ((), ())),
    )
    if len(rest) == 2:
        total = total + rest[0][...]
    out_ref[...] = total.astype(out_ref.dtype)


def down(hi, lo, at, blocks, total, tile, kind):
    units = hi.shape[1]
    slots, width = sum(b.shape[0] for b in blocks), blocks[0].shape[1]
    tiled = lambda i: (0, i)
    mine = pl.BlockSpec((slots, units), lambda i: (at // slots, 0))
    whole = pl.BlockSpec((units, tile), tiled)
    return pl.pallas_call(
        lambda *refs: down_kernel(len(blocks), *refs),
        grid=(width // tile,),
        in_specs=[mine] * 2
        + [pl.BlockSpec((b.shape[0], tile), tiled) for b in blocks]
        + ([] if total is None else [whole]),
        out_specs=whole,
        out_shape=jax.ShapeDtypeStruct((units, width), kind),
        input_output_aliases={2 + len(blocks): 0} if total is not None and total.dtype == kind else {},
        compiler_params=pltpu.CompilerParams(vmem_limit_bytes=VMEM),
        cost_estimate=pl.CostEstimate(
            flops=4 * slots * units * width,
            bytes_accessed=2 * (slots + 4 * units) * width,
            transcendentals=0,
        ),
        name="down",
    )(hi, lo, *blocks, *([] if total is None else [total]))


def look_kernel(ids_ref, slot_ref, table_ref, out_ref):
    toks, groups = ids_ref.shape
    nodes, wide = table_ref.shape
    per_dev = out_ref.shape[1] // groups
    cap = wide // per_dev
    table = table_ref[...]
    node = lax.broadcasted_iota(jnp.int32, (toks, nodes), 1)
    lane = lax.broadcasted_iota(jnp.int32, (toks, wide), 1)
    found = []
    for k in range(groups):
        hot = jnp.where(ids_ref[:, k : k + 1] == node, 1.0, 0.0)
        line = lax.dot_general(
            hot,
            table,
            (((1,), (0,)), ((), ())),
            precision=lax.Precision.HIGHEST,
            preferred_element_type=F32,
        )
        for j in range(per_dev):
            mine = lane == slot_ref[:, k : k + 1] + j * cap
            found.append(jnp.sum(jnp.where(mine, line, 0.0), axis=1, keepdims=True))
    out_ref[...] = jnp.concatenate(found, axis=1)


def look(ids, slot, table, per_dev):
    return pl.pallas_call(
        look_kernel,
        out_shape=jax.ShapeDtypeStruct((ids.shape[0], ids.shape[1] * per_dev), F32),
        compiler_params=pltpu.CompilerParams(vmem_limit_bytes=VMEM),
        name="look",
    )(ids, slot, table)


def largest_tile(width, most):
    return max(t for t in range(128, most + 1, 128) if width % t == 0)


def per_device(d_out, node_ids, gates, hidden, w_down):
    nodes = lax.axis_size("node")
    local = lax.axis_size("local")
    cap, per_dev = gates.shape[2:]
    units = hidden.shape[4]
    width = d_out.shape[1] * nodes
    tile = largest_tile(width, 1024)

    packed, slot = pack(node_ids.T, d_out, nodes, cap)
    w = w_down.reshape(per_dev * units, width)
    saved = hidden.reshape(local, cap, per_dev * units)
    gate = gates.reshape(local, cap, per_dev)
    own_rows = lax.all_to_all(packed, "node", split_axis=0, concat_axis=2, tiled=True).reshape(cap, width)

    steps = local // 2
    right = [(i, (i + 1) % local) for i in range(local)]
    left = [(i, (i - 1) % local) for i in range(local)]
    order = [t for k in range(1, steps) for t in (-k, k)] + [0, steps]
    shards = ((lax.axis_index("local") + jnp.array(order, jnp.int32)) % local).astype(jnp.int32)
    hi, lo = scale(shards, saved, gate)
    block, place = [own_rows], (local - 2) * cap
    ups, total = [], None
    one, other = own_rows, own_rows
    for k in range(1, steps + 1):
        if k == steps:
            one, other = one[: cap // 2], other[cap // 2 :]
        if k > 1:
            one, ups[-1], total = lax.optimization_barrier((one, ups[-1], total))
        one, other = lax.ppermute(one, "local", right), lax.ppermute(other, "local", left)
        ups.append(up(block, w))
        total = down(hi, lo, place, block, total, tile, F32)
        block, place = [one, other], (2 * k - 2) * cap if k < steps else (local - 1) * cap
    ups.append(up(block, w))
    grad_h, part = close(shards, ups[1:-1] + [ups[0], ups[-1]], saved, gate)
    got = lax.all_to_all(part, "local", split_axis=0, concat_axis=0, tiled=True)
    grad_w = down(hi, lo, place, block, total, tile, BF)
    got, grad_w = lax.optimization_barrier((got, grad_w))
    own = jnp.sum(got, axis=0)
    table = lax.all_to_all(
        jnp.broadcast_to(own[None], (nodes, per_dev, cap)),
        "node",
        split_axis=0,
        concat_axis=0,
        tiled=True,
    )
    d_gates = look(node_ids, slot.T, table.reshape(nodes, per_dev * cap), per_dev)
    return (
        grad_h.reshape(1, local, cap, per_dev, units),
        grad_w.reshape(per_dev, units, width),
        d_gates.reshape(node_ids.shape + (per_dev,)),
    )


def solution(mesh):
    return jax.shard_map(
        per_device,
        mesh=mesh,
        in_specs=(
            P("local", "node"),
            P("local", None),
            P("node", None, None, None),
            P("node", None, None, None, "local"),
            P("node", "local", None),
        ),
        out_specs=(
            P("node", None, None, None, "local"),
            P("node", "local", None),
            P("local", None, None),
        ),
        check_vma=False,
    )
```

time: 191 us -> 189 us (0.990)
  waiting for transfers between devices: 96.6 us -> 22.9 us
  starting transfers between devices: 20.9 us -> 79.8 us
  Pallas kernels: 10.9 us -> 36.1 us
  between operations: 14.2 us -> 1.21 us
    all_gather x1 -> x0, waiting for transfers between devices: 83.6 us -> none  [per_device(): rows = lax.all_gather(arrived, 'local', axis=0, tiled=True)]
    ppermute x0 -> x16, starting transfers between devices: none -> 59.2 us  [the longest x8 43.9 us: per_device(): lax.ppermute(other, 'local', left)]
    pallas_call x3 -> x21, Pallas kernels: 9.19 us -> 34.3 us  [the longest x9 23.3 us: down(): pl.pallas_call(lambda *refs: down_kernel(len(blocks), *refs), grid=(width...]
    ppermute x0 -> x16, waiting for transfers between devices: none -> 9.96 us  [the longest x8 8.18 us: per_device(): lax.ppermute(one, 'local', right)]
    all_to_all x1, waiting for transfers between devices: 10.9 us -> 4.05 us  [per_device(): got = lax.all_to_all(part, 'local', split_axis=0, concat_axis=0, tiled=True)]
    all_to_all x1, waiting for transfers between devices: 2.2 us -> 8.93 us  [per_device(): lax.all_to_all(jnp.broadcast_to(own[None], (nodes, per_dev, cap)), 'node'...]
    all_to_all x1, starting transfers between devices: 9.08 us -> 6.03 us  [per_device(): got = lax.all_to_all(part, 'local', split_axis=0, concat_axis=0, tiled=True)]
    all_to_all x1, starting transfers between devices: 11.8 us -> 14.6 us  [per_device(): lax.all_to_all(jnp.broadcast_to(own[None], (nodes, per_dev, cap)), 'node'...]
  transfers between devices with their start and end apart: 3 -> 18, of which waited for: 3 -> 10; matrix products, arithmetic and copies ran while one was open for 1% -> 1% of each run, Pallas kernels for 2% -> 17%
where the time goes in v2:
time: 189 us; the launch traced here: 187 us
  starting transfers between devices  79.8 us (42%)
  Pallas kernels  36.1 us (19%)
  blocking collectives  35.2 us (19%)
  waiting for transfers between devices  22.9 us (12%)
  local copies, waits for them, and re-layouts  11.2 us (6%)
    ppermute x8, starting transfers between devices, per_device(): lax.ppermute(other, 'local', left)  43.9 us
    all_to_all x1, blocking collectives, per_device(): lax.all_to_all(packed, 'node', split_axis=0, concat_axis=2, tiled=True)  35.2 us
    pallas_call x9, Pallas kernels, down(): pl.pallas_call(lambda *refs: down_kernel(len(blocks), *refs), grid=(width...  23.3 us
    ppermute x8, starting transfers between devices, per_device(): lax.ppermute(one, 'local', right)  15.3 us
    all_to_all x1, starting transfers between devices, per_device(): lax.all_to_all(jnp.broadcast_to(own[None], (nodes, per_dev, cap)), 'node'...  14.6 us
    all_to_all x1, waiting for transfers between devices, per_device(): lax.all_to_all(jnp.broadcast_to(own[None], (nodes, per_dev, cap)), 'node'...  8.93 us
    ppermute x8, waiting for transfers between devices, per_device(): lax.ppermute(one, 'local', right)  8.18 us
    pallas_call x9, Pallas kernels, up(): pl.pallas_call(up_kernel, out_shape=jax.ShapeDtypeStruct((slots, units),...  7.94 us
  transfers between devices with their start and end apart: 18, of which 10 were waited for; matrix products, arithmetic and copies ran while one was open for 1% of the time, Pallas kernels for 17%

profile of v2, /device:TPU:1, one launch (start us, length us, event | category | flops | bytes accessed | tf_op | source)
XLA Modules:
  0.0 187.2 jit_solution(2514687861382729981)
XLA Ops:
  3.0 35.2 %all_to_all.25 = bf16[64,32,96]{2,1,0:T(8,128)(2,1)S(1)} all-to-all(bf16[64,32,96]{2,1,0:T(8,128)(2,1)S(1)} %get-tuple-element.32), channel_id=1, replica_groups=mesh['node'=64,'local'=16] {'node'}, dimensions={0} | all-to-all | bytes 786432 | tf_op jit(solution)/shard_map/all_to_all | solution.py:239
  41.8 11.9 %collective-permute-start.2 = (bf16[32,6144]{1,0:T(8,128)(2,1)}, bf16[32,6144]{1,0:T(8,128)(2,1)}, u32[]{:S(2)}, u32[]{:S(2)}) collective-permute-start(bf16[32,6144]{1,0:T(8,128)(2,1)} %reshape.32.refs_0_.refs_2_), channel_id=1, source_target_pairs={{0,15},{1,0},{2,1},{3,2},{4,3},{5,4},{6,5},{7,6},{8,7},{9,8},{10,9... | collective-permute-start | bytes 1179656 | tf_op jit(solution)/shard_map/ppermute | solution.py:255
  57.2 3.7 %down.9.refs_4_ = f32[128,6144]{1,0:T(8,128)S(1)} custom-call(bf16[512,128]{1,0:T(8,128)(2,1)S(1)} %get-tuple-element.33.refs_0_, bf16[512,128]{1,0:T(8,128)(2,1)S(1)} %get-tuple-element.34.refs_1_, bf16[32,6144]{1,0:T(8,128)(2,1)} %reshape.32.refs_0_.refs_2_), custom_call_target="tpu_custom_call" | custom-call | flops 100663296 | bytes 6684672 | tf_op jit(solution)/shard_map/down/pallas_call | solution.py:171
  63.2 4.6 %collective-permute-start.4 = (bf16[32,6144]{1,0:T(8,128)(2,1)}, bf16[32,6144]{1,0:T(8,128)(2,1)S(1)}, u32[]{:S(2)}, u32[]{:S(2)}) collective-permute-start(bf16[32,6144]{1,0:T(8,128)(2,1)} %collective-permute-done.2.refs_1_.refs_3_), channel_id=1, source_target_pairs={{0,15},{1,0},{2,1},{3,2},{4,3},{5,4},{6,5},{7,6},{8,7},{9,8},{10,9... | collective-permute-start | bytes 1179656 | tf_op jit(solution)/shard_map/ppermute | solution.py:255
  70.9 4.0 %down.10.refs_4_ = f32[128,6144]{1,0:T(8,128)S(1)} custom-call(bf16[512,128]{1,0:T(8,128)(2,1)S(1)} %get-tuple-element.33.refs_0_, bf16[512,128]{1,0:T(8,128)(2,1)S(1)} %get-tuple-element.34.refs_1_, bf16[32,6144]{1,0:T(8,128)(2,1)} %collective-permute-done.refs_0_.refs_2_, ...), custom_call_target="tpu_custom_call", output_to_operand_aliasing={{}: (4, {})} | custom-call | flops 201326592 | bytes 7077888 | tf_op jit(solution)/shard_map/down/pallas_call | solution.py:171
  76.9 4.6 %collective-permute-start.6 = (bf16[32,6144]{1,0:T(8,128)(2,1)S(1)}, bf16[32,6144]{1,0:T(8,128)(2,1)S(1)}, u32[]{:S(2)}, u32[]{:S(2)}) collective-permute-start(bf16[32,6144]{1,0:T(8,128)(2,1)S(1)} %collective-permute-done.4.refs_1_.refs_3_), channel_id=1, source_target_pairs={{0,15},{1,0},{2,1},{3,2},{4,3},{5,4},{6,5},{7,6},{8,7},{9,8},{10,9... | collective-permute-start | bytes 1179656 | tf_op jit(solution)/shard_map/ppermute | solution.py:255
  82.1 2.1 %down.11.refs_4_ = f32[128,6144]{1,0:T(8,128)S(1)} custom-call(bf16[512,128]{1,0:T(8,128)(2,1)S(1)} %get-tuple-element.33.refs_0_, bf16[512,128]{1,0:T(8,128)(2,1)S(1)} %get-tuple-element.34.refs_1_, bf16[32,6144]{1,0:T(8,128)(2,1)S(1)} %collective-permute-done.1.refs_0_.refs_2_, ...), custom_call_target="tpu_custom_call", output_to_operand_aliasing={{}: (4, {})} | custom-call | flops 201326592 | bytes 7077888 | tf_op jit(solution)/shard_map/down/pallas_call | solution.py:171
  84.2 3.0 %collective-permute-done.3.refs_0_.refs_2_ = bf16[32,6144]{1,0:T(8,128)(2,1)S(1)} collective-permute-done((bf16[32,6144]{1,0:T(8,128)(2,1)S(1)}, bf16[32,6144]{1,0:T(8,128)(2,1)S(1)}, u32[]{:S(2)}, u32[]{:S(2)}) %collective-permute-start.3) | collective-permute-done | bytes 393248 | tf_op jit(solution)/shard_map/ppermute | solution.py:255
  89.1 4.6 %collective-permute-start.8 = (bf16[32,6144]{1,0:T(8,128)(2,1)S(1)}, bf16[32,6144]{1,0:T(8,128)(2,1)S(1)}, u32[]{:S(2)}, u32[]{:S(2)}) collective-permute-start(bf16[32,6144]{1,0:T(8,128)(2,1)S(1)} %collective-permute-done.6.refs_1_.refs_3_), channel_id=1, source_target_pairs={{0,15},{1,0},{2,1},{3,2},{4,3},{5,4},{6,5},{7,6},{8,7},{9,8},{10,9... | collective-permute-start | bytes 1179656 | tf_op jit(solution)/shard_map/ppermute | solution.py:255
  94.4 2.1 %down.12.refs_4_ = f32[128,6144]{1,0:T(8,128)S(1)} custom-call(bf16[512,128]{1,0:T(8,128)(2,1)S(1)} %get-tuple-element.33.refs_0_, bf16[512,128]{1,0:T(8,128)(2,1)S(1)} %get-tuple-element.34.refs_1_, bf16[32,6144]{1,0:T(8,128)(2,1)S(1)} %collective-permute-done.3.refs_0_.refs_2_, ...), custom_call_target="tpu_custom_call", output_to_operand_aliasing={{}: (4, {})} | custom-call | flops 201326592 | bytes 7077888 | tf_op jit(solution)/shard_map/down/pallas_call | solution.py:171
  96.4 2.1 %collective-permute-done.5.refs_0_.refs_2_ = bf16[32,6144]{1,0:T(8,128)(2,1)S(1)} collective-permute-done((bf16[32,6144]{1,0:T(8,128)(2,1)S(1)}, bf16[32,6144]{1,0:T(8,128)(2,1)S(1)}, u32[]{:S(2)}, u32[]{:S(2)}) %collective-permute-start.5) | collective-permute-done | bytes 393248 | tf_op jit(solution)/shard_map/ppermute | solution.py:255
  100.4 4.6 %collective-permute-start.10 = (bf16[32,6144]{1,0:T(8,128)(2,1)S(1)}, bf16[32,6144]{1,0:T(8,128)(2,1)S(1)}, u32[]{:S(2)}, u32[]{:S(2)}) collective-permute-start(bf16[32,6144]{1,0:T(8,128)(2,1)S(1)} %collective-permute-done.8.refs_1_.refs_3_), channel_id=1, source_target_pairs={{0,15},{1,0},{2,1},{3,2},{4,3},{5,4},{6,5},{7,6},{8,7},{9,8},{10,9... | collective-permute-start | bytes 1179656 | tf_op jit(solution)/shard_map/ppermute | solution.py:255
  105.7 2.1 %down.13.refs_4_ = f32[128,6144]{1,0:T(8,128)S(1)} custom-call(bf16[512,128]{1,0:T(8,128)(2,1)S(1)} %get-tuple-element.33.refs_0_, bf16[512,128]{1,0:T(8,128)(2,1)S(1)} %get-tuple-element.34.refs_1_, bf16[32,6144]{1,0:T(8,128)(2,1)S(1)} %collective-permute-done.5.refs_0_.refs_2_, ...), custom_call_target="tpu_custom_call", output_to_operand_aliasing={{}: (4, {})} | custom-call | flops 201326592 | bytes 7077888 | tf_op jit(solution)/shard_map/down/pallas_call | solution.py:171
  110.8 4.6 %collective-permute-start.12 = (bf16[32,6144]{1,0:T(8,128)(2,1)S(1)}, bf16[32,6144]{1,0:T(8,128)(2,1)S(1)}, u32[]{:S(2)}, u32[]{:S(2)}) collective-permute-start(bf16[32,6144]{1,0:T(8,128)(2,1)S(1)} %collective-permute-done.10.refs_1_.refs_3_), channel_id=1, source_target_pairs={{0,15},{1,0},{2,1},{3,2},{4,3},{5,4},{6,5},{7,6},{8,7},{9,8},{10,9... | collective-permute-start | bytes 1179656 | tf_op jit(solution)/shard_map/ppermute | solution.py:255
  116.1 2.1 %down.14.refs_4_ = f32[128,6144]{1,0:T(8,128)S(1)} custom-call(bf16[512,128]{1,0:T(8,128)(2,1)S(1)} %get-tuple-element.33.refs_0_, bf16[512,128]{1,0:T(8,128)(2,1)S(1)} %get-tuple-element.34.refs_1_, bf16[32,6144]{1,0:T(8,128)(2,1)S(1)} %collective-permute-done.7.refs_0_.refs_2_, ...), custom_call_target="tpu_custom_call", output_to_operand_aliasing={{}: (4, {})} | custom-call | flops 201326592 | bytes 7077888 | tf_op jit(solution)/shard_map/down/pallas_call | solution.py:171
  120.5 4.6 %collective-permute-start.13 = (bf16[32,6144]{1,0:T(8,128)(2,1)S(1)}, bf16[32,6144]{1,0:T(8,128)(2,1)S(1)}, u32[]{:S(2)}, u32[]{:S(2)}) collective-permute-start(bf16[32,6144]{1,0:T(8,128)(2,1)S(1)} %collective-permute-done.12.refs_1_.refs_3_), channel_id=1, source_target_pairs={{0,15},{1,0},{2,1},{3,2},{4,3},{5,4},{6,5},{7,6},{8,7},{9,8},{10,9... | collective-permute-start | bytes 1179656 | tf_op jit(solution)/shard_map/ppermute | solution.py:255
  125.8 2.1 %down.15.refs_4_ = f32[128,6144]{1,0:T(8,128)S(1)} custom-call(bf16[512,128]{1,0:T(8,128)(2,1)S(1)} %get-tuple-element.33.refs_0_, bf16[512,128]{1,0:T(8,128)(2,1)S(1)} %get-tuple-element.34.refs_1_, bf16[32,6144]{1,0:T(8,128)(2,1)S(1)} %collective-permute-done.9.refs_0_.refs_2_, ...), custom_call_target="tpu_custom_call", output_to_operand_aliasing={{}: (4, {})} | custom-call | flops 201326592 | bytes 7077888 | tf_op jit(solution)/shard_map/down/pallas_call | solution.py:171
  130.3 4.6 %collective-permute-start.15 = (bf16[16,6144]{1,0:T(8,128)(2,1)S(1)}, bf16[16,6144]{1,0:T(8,128)(2,1)S(1)}, u32[]{:S(2)}, u32[]{:S(2)}) collective-permute-start(bf16[16,6144]{1,0:T(8,128)(2,1)S(1)} %slice.9), channel_id=1, source_target_pairs={{0,15},{1,0},{2,1},{3,2},{4,3},{5,4},{6,5},{7,6},{8,7},{9,8},{10,9... | collective-permute-start | bytes 589832 | tf_op jit(solution)/shard_map/ppermute | solution.py:255
  141.0 6.0 %all-to-all-start.1 = ((f32[16,2,32]{2,1,0:T(2,128)}), f32[16,2,32]{2,1,0:T(2,128)}, u32[]{:S(2)}, u32[]{:S(2)}) async-start(f32[16,2,32]{2,1,0:T(2,128)} %get-tuple-element.56), calls=%async_computation.1 | async-start | bytes 32768 | tf_op jit(solution)/shard_map/all_to_all | solution.py:261
  149.1 2.0 %down.16.refs_4_ = f32[128,6144]{1,0:T(8,128)S(1)} custom-call(bf16[512,128]{1,0:T(8,128)(2,1)S(1)} %get-tuple-element.33.refs_0_, bf16[512,128]{1,0:T(8,128)(2,1)S(1)} %get-tuple-element.34.refs_1_, bf16[32,6144]{1,0:T(8,128)(2,1)S(1)} %copy-done.4, bf16[32,6144]{1,0:T(8,128)(2,1)S(1)} %copy-done.6, ...), custom_call_target="tpu_custom_call", output_to_operand_aliasing={{}: (4, {})} | custom-call | flops 201326592 | bytes 7077888 | tf_op jit(solution)/shard_map/down/pallas_call | solution.py:171
  151.2 3.3 %down.17 = bf16[128,6144]{1,0:T(8,128)(2,1)} custom-call(bf16[512,128]{1,0:T(8,128)(2,1)S(1)} %get-tuple-element.33.refs_0_, bf16[512,128]{1,0:T(8,128)(2,1)S(1)} %get-tuple-element.34.refs_1_, bf16[16,6144]{1,0:T(8,128)(2,1)S(1)} %copy-done.10, bf16[16,6144]{1,0:T(8,128)(2,1)S(1)} %copy-done.12, f32[128,6144]{1,0:T(8,128)S(1)} %down.16.refs_4_), custom_call_target="tpu_custom_call" | custom-call | flops 100663296 | bytes 6684672 | tf_op jit(solution)/shard_map/down/pallas_call | solution.py:171
  154.5 4.1 %all-to-all-done.1 = f32[16,2,32]{2,1,0:T(2,128)} async-done(((f32[16,2,32]{2,1,0:T(2,128)}), f32[16,2,32]{2,1,0:T(2,128)}, u32[]{:S(2)}, u32[]{:S(2)}) %all-to-all-start.1) | async-done | bytes 4128 | tf_op jit(solution)/shard_map/all_to_all | solution.py:261
  159.9 14.6 %all-to-all-start.2 = ((f32[64,2,32]{2,1,0:T(2,128)}), f32[64,2,32]{2,1,0:T(2,128)S(1)}, u32[]{:S(2)}, u32[]{:S(2)}) async-start(f32[64,2,32]{2,1,0:T(2,128)} %broadcast_in_dim.2), calls=%async_computation.2 | async-start | bytes 131072 | tf_op jit(solution)/shard_map/all_to_all | solution.py:265
  175.7 8.9 %all-to-all-done.2 = f32[64,2,32]{2,1,0:T(2,128)S(1)} async-done(((f32[64,2,32]{2,1,0:T(2,128)}), f32[64,2,32]{2,1,0:T(2,128)S(1)}, u32[]{:S(2)}, u32[]{:S(2)}) %all-to-all-start.2) | async-done | bytes 16416 | tf_op jit(solution)/shard_map/all_to_all | solution.py:265
  (90 shorter events, 44.9 us)
Async XLA Ops:
  0.6 54.1 %copy-start.18 = (s32[16]{0:T(128)S(1)}, s32[16]{0:T(128)}, u32[]{:S(2)}) copy-start(s32[16]{0:T(128)} %constant.23.clone) | copy-start | bytes 196
  0.6 54.9 %copy-start = (bf16[2,64,6144]{2,1,0:T(8,128)(2,1)S(1)}, bf16[2,64,6144]{2,1,0:T(8,128)(2,1)}, u32[]{:S(2)}) copy-start(bf16[2,64,6144]{2,1,0:T(8,128)(2,1)} %param.10) | copy-start | bytes 4718596
  2.4 52.2 %copy-start.17 = (bf16[1,16,32,2,64]{4,3,2,1,0:T(2,128)(2,1)S(1)}, bf16[1,16,32,2,64]{4,3,2,1,0:T(2,128)(2,1)}, u32[]{:S(2)}) copy-start(bf16[1,16,32,2,64]{4,3,2,1,0:T(2,128)(2,1)} %param.9) | copy-start | bytes 393220
  39.9 21.3 %collective-permute-start = (bf16[32,6144]{1,0:T(8,128)(2,1)}, bf16[32,6144]{1,0:T(8,128)(2,1)}, u32[]{:S(2)}, u32[]{:S(2)}) collective-permute-start(bf16[32,6144]{1,0:T(8,128)(2,1)} %reshape.32.refs_0_.refs_2_), channel_id=1, source_target_pairs={{0,1},{1,2},{2,3},{3,4},{4,5},{5,6},{6,7},{7,8},{8,9},{9,10},{10,1... | collective-permute-start | bytes 1179656 | tf_op jit(solution)/shard_map/ppermute | solution.py:255
  41.8 21.3 %collective-permute-start.2 = (bf16[32,6144]{1,0:T(8,128)(2,1)}, bf16[32,6144]{1,0:T(8,128)(2,1)}, u32[]{:S(2)}, u32[]{:S(2)}) collective-permute-start(bf16[32,6144]{1,0:T(8,128)(2,1)} %reshape.32.refs_0_.refs_2_), channel_id=1, source_target_pairs={{0,15},{1,0},{2,1},{3,2},{4,3},{5,4},{6,5},{7,6},{8,7},{9,8},{10,9... | collective-permute-start | bytes 1179656 | tf_op jit(solution)/shard_map/ppermute | solution.py:255
  61.2 13.7 %collective-permute-start.1 = (bf16[32,6144]{1,0:T(8,128)(2,1)}, bf16[32,6144]{1,0:T(8,128)(2,1)S(1)}, u32[]{:S(2)}, u32[]{:S(2)}) collective-permute-start(bf16[32,6144]{1,0:T(8,128)(2,1)} %collective-permute-done.refs_0_.refs_2_), channel_id=1, source_target_pairs={{0,1},{1,2},{2,3},{3,4},{4,5},{5,6},{6,7},{7,8},{8,9},{9,10},{10,1... | collective-permute-start | bytes 1179656 | tf_op jit(solution)/shard_map/ppermute | solution.py:255
  63.2 13.7 %collective-permute-start.4 = (bf16[32,6144]{1,0:T(8,128)(2,1)}, bf16[32,6144]{1,0:T(8,128)(2,1)S(1)}, u32[]{:S(2)}, u32[]{:S(2)}) collective-permute-start(bf16[32,6144]{1,0:T(8,128)(2,1)} %collective-permute-done.2.refs_1_.refs_3_), channel_id=1, source_target_pairs={{0,15},{1,0},{2,1},{3,2},{4,3},{5,4},{6,5},{7,6},{8,7},{9,8},{10,9... | collective-permute-start | bytes 1179656 | tf_op jit(solution)/shard_map/ppermute | solution.py:255
  74.9 12.2 %collective-permute-start.3 = (bf16[32,6144]{1,0:T(8,128)(2,1)S(1)}, bf16[32,6144]{1,0:T(8,128)(2,1)S(1)}, u32[]{:S(2)}, u32[]{:S(2)}) collective-permute-start(bf16[32,6144]{1,0:T(8,128)(2,1)S(1)} %collective-permute-done.1.refs_0_.refs_2_), channel_id=1, source_target_pairs={{0,1},{1,2},{2,3},{3,4},{4,5},{5,6},{6,7},{7,8},{8,9},{9,10},{10,1... | collective-permute-start | bytes 1179656 | tf_op jit(solution)/shard_map/ppermute | solution.py:255
  76.9 12.2 %collective-permute-start.6 = (bf16[32,6144]{1,0:T(8,128)(2,1)S(1)}, bf16[32,6144]{1,0:T(8,128)(2,1)S(1)}, u32[]{:S(2)}, u32[]{:S(2)}) collective-permute-start(bf16[32,6144]{1,0:T(8,128)(2,1)S(1)} %collective-permute-done.4.refs_1_.refs_3_), channel_id=1, source_target_pairs={{0,15},{1,0},{2,1},{3,2},{4,3},{5,4},{6,5},{7,6},{8,7},{9,8},{10,9... | collective-permute-start | bytes 1179656 | tf_op jit(solution)/shard_map/ppermute | solution.py:255
  87.2 11.3 %collective-permute-start.5 = (bf16[32,6144]{1,0:T(8,128)(2,1)S(1)}, bf16[32,6144]{1,0:T(8,128)(2,1)S(1)}, u32[]{:S(2)}, u32[]{:S(2)}) collective-permute-start(bf16[32,6144]{1,0:T(8,128)(2,1)S(1)} %collective-permute-done.3.refs_0_.refs_2_), channel_id=1, source_target_pairs={{0,1},{1,2},{2,3},{3,4},{4,5},{5,6},{6,7},{7,8},{8,9},{9,10},{10,1... | collective-permute-start | bytes 1179656 | tf_op jit(solution)/shard_map/ppermute | solution.py:255
  89.1 11.3 %collective-permute-start.8 = (bf16[32,6144]{1,0:T(8,128)(2,1)S(1)}, bf16[32,6144]{1,0:T(8,128)(2,1)S(1)}, u32[]{:S(2)}, u32[]{:S(2)}) collective-permute-start(bf16[32,6144]{1,0:T(8,128)(2,1)S(1)} %collective-permute-done.6.refs_1_.refs_3_), channel_id=1, source_target_pairs={{0,15},{1,0},{2,1},{3,2},{4,3},{5,4},{6,5},{7,6},{8,7},{9,8},{10,9... | collective-permute-start | bytes 1179656 | tf_op jit(solution)/shard_map/ppermute | solution.py:255
  98.5 10.4 %collective-permute-start.7 = (bf16[32,6144]{1,0:T(8,128)(2,1)S(1)}, bf16[32,6144]{1,0:T(8,128)(2,1)S(1)}, u32[]{:S(2)}, u32[]{:S(2)}) collective-permute-start(bf16[32,6144]{1,0:T(8,128)(2,1)S(1)} %collective-permute-done.5.refs_0_.refs_2_), channel_id=1, source_target_pairs={{0,1},{1,2},{2,3},{3,4},{4,5},{5,6},{6,7},{7,8},{8,9},{9,10},{10,1... | collective-permute-start | bytes 1179656 | tf_op jit(solution)/shard_map/ppermute | solution.py:255
  100.4 10.4 %collective-permute-start.10 = (bf16[32,6144]{1,0:T(8,128)(2,1)S(1)}, bf16[32,6144]{1,0:T(8,128)(2,1)S(1)}, u32[]{:S(2)}, u32[]{:S(2)}) collective-permute-start(bf16[32,6144]{1,0:T(8,128)(2,1)S(1)} %collective-permute-done.8.refs_1_.refs_3_), channel_id=1, source_target_pairs={{0,15},{1,0},{2,1},{3,2},{4,3},{5,4},{6,5},{7,6},{8,7},{9,8},{10,9... | collective-permute-start | bytes 1179656 | tf_op jit(solution)/shard_map/ppermute | solution.py:255
  108.9 9.7 %collective-permute-start.9 = (bf16[32,6144]{1,0:T(8,128)(2,1)S(1)}, bf16[32,6144]{1,0:T(8,128)(2,1)S(1)}, u32[]{:S(2)}, u32[]{:S(2)}) collective-permute-start(bf16[32,6144]{1,0:T(8,128)(2,1)S(1)} %collective-permute-done.7.refs_0_.refs_2_), channel_id=1, source_target_pairs={{0,1},{1,2},{2,3},{3,4},{4,5},{5,6},{6,7},{7,8},{8,9},{9,10},{10,1... | collective-permute-start | bytes 1179656 | tf_op jit(solution)/shard_map/ppermute | solution.py:255
  110.8 9.7 %collective-permute-start.12 = (bf16[32,6144]{1,0:T(8,128)(2,1)S(1)}, bf16[32,6144]{1,0:T(8,128)(2,1)S(1)}, u32[]{:S(2)}, u32[]{:S(2)}) collective-permute-start(bf16[32,6144]{1,0:T(8,128)(2,1)S(1)} %collective-permute-done.10.refs_1_.refs_3_), channel_id=1, source_target_pairs={{0,15},{1,0},{2,1},{3,2},{4,3},{5,4},{6,5},{7,6},{8,7},{9,8},{10,9... | collective-permute-start | bytes 1179656 | tf_op jit(solution)/shard_map/ppermute | solution.py:255
  118.6 9.7 %collective-permute-start.11 = (bf16[32,6144]{1,0:T(8,128)(2,1)S(1)}, bf16[32,6144]{1,0:T(8,128)(2,1)S(1)}, u32[]{:S(2)}, u32[]{:S(2)}) collective-permute-start(bf16[32,6144]{1,0:T(8,128)(2,1)S(1)} %collective-permute-done.9.refs_0_.refs_2_), channel_id=1, source_target_pairs={{0,1},{1,2},{2,3},{3,4},{4,5},{5,6},{6,7},{7,8},{8,9},{9,10},{10,1... | collective-permute-start | bytes 1179656 | tf_op jit(solution)/shard_map/ppermute | solution.py:255
  120.5 9.7 %collective-permute-start.13 = (bf16[32,6144]{1,0:T(8,128)(2,1)S(1)}, bf16[32,6144]{1,0:T(8,128)(2,1)S(1)}, u32[]{:S(2)}, u32[]{:S(2)}) collective-permute-start(bf16[32,6144]{1,0:T(8,128)(2,1)S(1)} %collective-permute-done.12.refs_1_.refs_3_), channel_id=1, source_target_pairs={{0,15},{1,0},{2,1},{3,2},{4,3},{5,4},{6,5},{7,6},{8,7},{9,8},{10,9... | collective-permute-start | bytes 1179656 | tf_op jit(solution)/shard_map/ppermute | solution.py:255
  127.8 10.8 %copy-start.8 = (f32[1,16,32,2]{3,2,1,0:T(8,128)S(1)}, f32[1,16,32,2]{3,2,1,0:T(8,128)}, u32[]{:S(2)}) copy-start(f32[1,16,32,2]{3,2,1,0:T(8,128)} %copy-done.7) | copy-start | bytes 12292
  128.3 7.9 %collective-permute-start.14 = (bf16[16,6144]{1,0:T(8,128)(2,1)S(1)}, bf16[16,6144]{1,0:T(8,128)(2,1)S(1)}, u32[]{:S(2)}, u32[]{:S(2)}) collective-permute-start(bf16[16,6144]{1,0:T(8,128)(2,1)S(1)} %slice.8), channel_id=1, source_target_pairs={{0,1},{1,2},{2,3},{3,4},{4,5},{5,6},{6,7},{7,8},{8,9},{9,10},{10,1... | collective-permute-start | bytes 589832 | tf_op jit(solution)/shard_map/ppermute | solution.py:255
  130.3 7.7 %collective-permute-start.15 = (bf16[16,6144]{1,0:T(8,128)(2,1)S(1)}, bf16[16,6144]{1,0:T(8,128)(2,1)S(1)}, u32[]{:S(2)}, u32[]{:S(2)}) collective-permute-start(bf16[16,6144]{1,0:T(8,128)(2,1)S(1)} %slice.9), channel_id=1, source_target_pairs={{0,15},{1,0},{2,1},{3,2},{4,3},{5,4},{6,5},{7,6},{8,7},{9,8},{10,9... | collective-permute-start | bytes 589832 | tf_op jit(solution)/shard_map/ppermute | solution.py:255
  141.0 17.5 %all-to-all-start.1 = ((f32[16,2,32]{2,1,0:T(2,128)}), f32[16,2,32]{2,1,0:T(2,128)}, u32[]{:S(2)}, u32[]{:S(2)}) async-start(f32[16,2,32]{2,1,0:T(2,128)} %get-tuple-element.56), calls=%async_computation.1 | async-start | bytes 32768 | tf_op jit(solution)/shard_map/all_to_all | solution.py:261
  151.1 23.4 %copy-start.16 = (s32[256,4]{0,1:T(4,128)S(1)}, s32[256,4]{0,1:T(4,128)}, u32[]{:S(2)}) copy-start(s32[256,4]{0,1:T(4,128)} %param.7) | copy-start | bytes 12292
  151.1 23.7 %copy-start.14 = (bf16[16,32,128]{2,1,0:T(8,128)(2,1)S(1)}, bf16[16,32,128]{2,1,0:T(8,128)(2,1)}, u32[]{:S(2)}) copy-start(bf16[16,32,128]{2,1,0:T(8,128)(2,1)} %copy-done.13) | copy-start | bytes 393220
  159.9 24.7 %all-to-all-start.2 = ((f32[64,2,32]{2,1,0:T(2,128)}), f32[64,2,32]{2,1,0:T(2,128)S(1)}, u32[]{:S(2)}, u32[]{:S(2)}) async-start(f32[64,2,32]{2,1,0:T(2,128)} %broadcast_in_dim.2), calls=%async_computation.2 | async-start | bytes 131072 | tf_op jit(solution)/shard_map/all_to_all | solution.py:265
  (13 other events, 43.4 us)

commit v3 on v2

v3 whole, which is shorter than its diff:
```python
import functools

import jax
import jax.numpy as jnp
from jax import lax
from jax.experimental import pallas as pl
from jax.experimental.pallas import tpu as pltpu
from jax.sharding import PartitionSpec as P

BF = jnp.bfloat16
F32 = jnp.float32
VMEM = 16 * 1024 * 1024


def dot(a, b, dims=(((1,), (0,)), ((), ()))):
    return lax.dot_general(a, b, dims, preferred_element_type=F32)


CHUNK = 32
FOLD = 128 // CHUNK


def pack_kernel(ids_ref, rows_ref, out_ref, slot_ref):
    groups, toks = ids_ref.shape
    nodes, part, wide = out_ref.shape
    cols = rows_ref.shape[1]
    node = lax.broadcasted_iota(jnp.int32, (nodes, toks), 0)
    picked = [node == ids_ref[k : k + 1, :] for k in range(groups)]
    member = picked[0]
    for k in range(1, groups):
        member = member | picked[k]
    earlier = lax.broadcasted_iota(jnp.int32, (toks, toks), 0) < lax.broadcasted_iota(
        jnp.int32, (toks, toks), 1
    )
    before = dot(
        jnp.where(member, 1.0, 0.0).astype(BF), jnp.where(earlier, 1.0, 0.0).astype(BF)
    )
    code = jnp.where(member, before, -1.0).astype(jnp.int32)
    slot = lax.broadcasted_iota(jnp.int32, (nodes, part, toks), 1)
    col = lax.broadcasted_iota(jnp.int32, (cols, wide), 0)
    place = col // CHUNK * 128 + col % CHUNK
    lane = lax.broadcasted_iota(jnp.int32, (cols, wide), 1)
    rows = rows_ref[...]
    placed, spaced = [], []
    for at in range(FOLD):
        hit = jnp.where(code[:, None, :] == slot + at * part, 1.0, 0.0)
        placed.append(hit.reshape(nodes * part, toks).astype(BF))
        move = jnp.where(lane == place + at * CHUNK, 1.0, 0.0).astype(BF)
        spaced.append(dot(rows, move).astype(BF))
    out = dot(jnp.concatenate(placed, axis=1), jnp.concatenate(spaced, axis=0))
    out_ref[...] = out.reshape(nodes, part, wide).astype(BF)
    for k in range(groups):
        mine = jnp.sum(jnp.where(picked[k], before, 0.0), axis=0, keepdims=True)
        slot_ref[k : k + 1, :] = mine.astype(jnp.int32)


def pack(ids, rows, nodes, cap):
    return pl.pallas_call(
        pack_kernel,
        out_shape=[
            jax.ShapeDtypeStruct((nodes, cap // FOLD, rows.shape[1] * FOLD), BF),
            jax.ShapeDtypeStruct(ids.shape, jnp.int32),
        ],
        compiler_params=pltpu.CompilerParams(vmem_limit_bytes=VMEM),
        name="pack",
    )(ids, rows)


def unpack_kernel(got_ref, rows_ref):
    nodes, part, wide = got_ref.shape
    chunks = wide // 128
    sets = nodes // FOLD
    got = got_ref[...].astype(F32).reshape(sets, FOLD, part, wide)
    row = lax.broadcasted_iota(jnp.int32, (FOLD * 128, FOLD * 128), 0)
    lane = lax.broadcasted_iota(jnp.int32, (FOLD * 128, FOLD * 128), 1)
    to = row // CHUNK % FOLD * 128 + row // 128 * CHUNK + row % CHUNK
    move = jnp.where(lane == to, 1.0, 0.0).astype(BF)
    for tile in range(chunks):
        parts = []
        for at in range(FOLD * tile, FOLD * tile + FOLD):
            node, chunk = divmod(at, chunks)
            piece = got[:, node, :, chunk * 128 : chunk * 128 + 128]
            parts.append(piece.reshape(sets * part, 128).astype(BF))
        out = dot(jnp.concatenate(parts, axis=1), move)
        for m in range(sets):
            rows = out[m * part : (m + 1) * part]
            rows = jnp.concatenate([rows[:, i * 128 : i * 128 + 128] for i in range(FOLD)], axis=0)
            first = (m * chunks + tile) * 128
            rows_ref[:, first : first + 128] = rows.astype(BF)


def unpack(got):
    nodes, part, wide = got.shape
    return pl.pallas_call(
        unpack_kernel,
        out_shape=jax.ShapeDtypeStruct((part * FOLD, nodes * wide // FOLD), BF),
        compiler_params=pltpu.CompilerParams(vmem_limit_bytes=VMEM),
        name="unpack",
    )(got)


def scale_kernel(shard_ref, saved_ref, gate_ref, *out_refs):
    _, cap, wide = saved_ref.shape
    per_dev = gate_ref.shape[2]
    owner = lax.broadcasted_iota(jnp.int32, (cap, wide), 1) // (wide // per_dev)
    at = 0
    for ref in out_refs:
        rows = ref.shape[0] // 2
        for row in range(0, rows, cap):
            shard = shard_ref[at]
            at += 1
            scaled = saved_ref[shard].astype(F32) * spread(gate_ref[shard], owner)
            hi = scaled.astype(BF)
            ref[row : row + cap] = hi
            ref[rows + row : rows + row + cap] = (scaled - hi.astype(F32)).astype(BF)


def spread(gates, owner):
    gate = gates[:, 0:1]
    for j in range(1, gates.shape[1]):
        gate = jnp.where(owner == j, gates[:, j : j + 1], gate)
    return gate


def scale(order, saved, gates, counts):
    _, cap, wide = saved.shape
    vmem = pl.BlockSpec(memory_space=pltpu.VMEM)
    return pl.pallas_call(
        scale_kernel,
        in_specs=[pl.BlockSpec(memory_space=pltpu.SMEM), vmem, vmem],
        out_shape=[jax.ShapeDtypeStruct((2 * n * cap, wide), BF) for n in counts],
        compiler_params=pltpu.CompilerParams(vmem_limit_bytes=VMEM),
        name="scale",
    )(order, saved, gates)


def up_kernel(*refs):
    *row_refs, w_ref, out_ref = refs
    rows = jnp.concatenate([r[...] for r in row_refs], axis=0)
    out_ref[...] = dot(rows, w_ref[...], (((1,), (1,)), ((), ())))


def up(blocks, w):
    slots, (units, width) = sum(b.shape[0] for b in blocks), w.shape
    return pl.pallas_call(
        up_kernel,
        out_shape=jax.ShapeDtypeStruct((slots, units), F32),
        compiler_params=pltpu.CompilerParams(vmem_limit_bytes=VMEM),
        cost_estimate=pl.CostEstimate(
            flops=2 * slots * units * width,
            bytes_accessed=2 * (slots + units) * width,
            transcendentals=0,
        ),
        name="up",
    )(*blocks, w)


def close_kernel(shard_ref, *refs):
    *up_refs, saved_ref, gate_ref, dh_ref, part_ref = refs
    per_dev, cap = gate_ref.shape[2], gate_ref.shape[1]
    wide = saved_ref.shape[2]
    pick = jnp.where(
        lax.broadcasted_iota(jnp.int32, (8, wide), 0)
        == lax.broadcasted_iota(jnp.int32, (8, wide), 1) // (wide // per_dev),
        1.0,
        0.0,
    )
    left = lax.broadcasted_iota(jnp.int32, (cap, wide), 1) // (wide // per_dev)
    at = 0
    for ref in up_refs:
        for row in range(0, ref.shape[0], cap):
            shard = shard_ref[at]
            at += 1
            u = ref[row : row + cap, :]
            gate = spread(gate_ref[shard], left)
            dh_ref[shard] = (gate * u).astype(BF)
            sums = lax.dot_general(
                pick,
                saved_ref[shard].astype(F32) * u,
                (((1,), (1,)), ((), ())),
                precision=lax.Precision.HIGHEST,
                preferred_element_type=F32,
            )
            part_ref[shard] = jnp.concatenate([sums[j : j + 1] for j in range(per_dev)], axis=1)


def close(order, ups, saved, gates):
    shards, cap, per_dev = gates.shape
    vmem = pl.BlockSpec(memory_space=pltpu.VMEM)
    return pl.pallas_call(
        close_kernel,
        in_specs=[pl.BlockSpec(memory_space=pltpu.SMEM)] + [vmem] * (len(ups) + 2),
        out_shape=[
            jax.ShapeDtypeStruct(saved.shape, BF),
            jax.ShapeDtypeStruct((shards, 1, per_dev * cap), F32),
        ],
        compiler_params=pltpu.CompilerParams(vmem_limit_bytes=VMEM),
        name="close",
    )(order, *ups, saved, gates)


def down_kernel(count, scaled_ref, *refs):
    row_refs, rest = refs[:count], refs[count:]
    rows = jnp.concatenate([r[...] for r in row_refs], axis=0)
    out_ref = rest[-1]
    total = dot(
        scaled_ref[...], jnp.concatenate([rows, rows], axis=0), (((0,), (0,)), ((), ()))
    )
    if len(rest) == 2:
        total = total + rest[0][...]
    out_ref[...] = total.astype(out_ref.dtype)


def down(scaled, blocks, total, tile, kind):
    slots, units = scaled.shape
    width = blocks[0].shape[1]
    tiled = lambda i: (0, i)
    whole = pl.BlockSpec((units, tile), tiled)
    return pl.pallas_call(
        lambda *refs: down_kernel(len(blocks), *refs),
        grid=(width // tile,),
        in_specs=[pl.BlockSpec((slots, units), lambda i: (0, 0))]
        + [pl.BlockSpec((b.shape[0], tile), tiled) for b in blocks]
        + ([] if total is None else [whole]),
        out_specs=whole,
        out_shape=jax.ShapeDtypeStruct((units, width), kind),
        input_output_aliases={1 + len(blocks): 0} if total is not None and total.dtype == kind else {},
        compiler_params=pltpu.CompilerParams(vmem_limit_bytes=VMEM),
        cost_estimate=pl.CostEstimate(
            flops=2 * slots * units * width,
            bytes_accessed=(slots + 8 * units) * width,
            transcendentals=0,
        ),
        name="down",
    )(scaled, *blocks, *([] if total is None else [total]))


def total_kernel(got_ref, out_ref):
    out_ref[...] = jnp.broadcast_to(jnp.sum(got_ref[...], axis=0, keepdims=True), out_ref.shape)


def total_for(got, nodes):
    return pl.pallas_call(
        total_kernel, out_shape=jax.ShapeDtypeStruct((nodes,) + got.shape[1:], F32), name="total"
    )(got)


def look_kernel(ids_ref, slot_ref, table_ref, out_ref):
    groups, toks = ids_ref.shape
    nodes, _, wide = table_ref.shape
    per_dev = out_ref.shape[0] // groups
    cap = wide // per_dev
    node = lax.broadcasted_iota(jnp.int32, (nodes, toks), 0)
    hot = [jnp.where(node == ids_ref[k : k + 1, :], 1.0, 0.0) for k in range(groups)]
    lines = lax.dot_general(
        table_ref[:, 0, :],
        jnp.concatenate(hot, axis=1),
        (((0,), (0,)), ((), ())),
        precision=lax.Precision.HIGHEST,
        preferred_element_type=F32,
    )
    row = lax.broadcasted_iota(jnp.int32, (cap, toks), 0)
    for k in range(groups):
        mine = row == slot_ref[k : k + 1, :]
        for j in range(per_dev):
            part = lines[j * cap : (j + 1) * cap, k * toks : (k + 1) * toks]
            out_ref[k * per_dev + j : k * per_dev + j + 1, :] = jnp.sum(
                jnp.where(mine, part, 0.0), axis=0, keepdims=True
            )


def look(ids, slot, table, per_dev):
    return pl.pallas_call(
        look_kernel,
        out_shape=jax.ShapeDtypeStruct((ids.shape[0] * per_dev, ids.shape[1]), F32),
        compiler_params=pltpu.CompilerParams(vmem_limit_bytes=VMEM),
        name="look",
    )(ids, slot, table)


def largest_tile(width, most):
    return max(t for t in range(128, most + 1, 128) if width % t == 0)


def per_device(d_out, node_ids, gates, hidden, w_down):
    nodes = lax.axis_size("node")
    local = lax.axis_size("local")
    cap, per_dev = gates.shape[2:]
    units = hidden.shape[4]
    width = d_out.shape[1] * nodes
    tile = largest_tile(width, 1024)

    ids = node_ids.T
    packed, slot = pack(ids, d_out, nodes, cap)
    w = w_down.reshape(per_dev * units, width)
    saved = hidden.reshape(local, cap, per_dev * units)
    gate = gates.reshape(local, cap, per_dev)
    own_rows = unpack(lax.all_to_all(packed, "node", split_axis=0, concat_axis=0, tiled=True))

    steps = local // 2
    right = [(i, (i + 1) % local) for i in range(local)]
    left = [(i, (i - 1) % local) for i in range(local)]
    away = [[0]] + [[-k, k] for k in range(1, steps)] + [[steps]]
    order = jnp.array([t for step in away for t in step], jnp.int32)
    shards = ((lax.axis_index("local") + order) % local).astype(jnp.int32)
    groups = [range(k, min(k + 2, steps)) for k in range(0, steps, 2)] + [range(steps, steps + 1)]
    scaled = scale(shards, saved, gate, [sum(len(away[k]) for k in group) for group in groups])
    blocks, ups, total = [[own_rows]], [], None

    def add(at, kind):
        return down(scaled[at], [b for k in groups[at] for b in blocks[k]], total, tile, kind)

    one, other = own_rows, own_rows
    for k in range(1, steps + 1):
        if k == steps:
            one, other = one[: cap // 2], other[cap // 2 :]
        if k > 1:
            one, ups[-1], total = lax.optimization_barrier((one, ups[-1], total))
        one, other = lax.ppermute(one, "local", right), lax.ppermute(other, "local", left)
        ups.append(up(blocks[-1], w))
        for at, group in enumerate(groups):
            if group[-1] == k - 1:
                total = add(at, F32)
        blocks.append([one, other])
    blocks[-1][1], total = lax.optimization_barrier((blocks[-1][1], total))
    ups.append(up(blocks[-1], w))
    grad_h, part = close(shards, ups, saved, gate)
    got = lax.all_to_all(part, "local", split_axis=0, concat_axis=0, tiled=True)
    table = lax.all_to_all(total_for(got, nodes), "node", split_axis=0, concat_axis=0, tiled=True)
    grad_w = add(len(groups) - 1, BF)
    d_gates = look(ids, slot, table, per_dev)
    return (
        grad_h.reshape(1, local, cap, per_dev, units),
        grad_w.reshape(per_dev, units, width),
        d_gates.reshape(node_ids.shape[1], per_dev, -1).transpose(2, 0, 1),
    )


def solution(mesh):
    return jax.shard_map(
        per_device,
        mesh=mesh,
        in_specs=(
            P("local", "node"),
            P("local", None),
            P("node", None, None, None),
            P("node", None, None, None, "local"),
            P("node", "local", None),
        ),
        out_specs=(
            P("node", None, None, None, "local"),
            P("node", "local", None),
            P("local", None, None),
        ),
        check_vma=False,
    )
```

time: 189 us -> 184 us (0.974)
  blocking collectives: 35.2 us -> 47.9 us
  Pallas kernels: 36.1 us -> 25.2 us
  starting transfers between devices: 79.8 us -> 75.4 us
    all_to_all x1 -> x2, blocking collectives: 35.2 us -> 47.9 us  [the longest x1 32.6 us: per_device(): lax.all_to_all(packed, 'node', split_axis=0, concat_axis=0, tiled=True)]
    pallas_call x9 -> x5, Pallas kernels: 23.3 us -> 13.3 us  [down(): pl.pallas_call(lambda *refs: down_kernel(len(blocks), *refs), grid=(width...]
    all_to_all x2 -> x1, waiting for transfers between devices: 13 us -> 3.34 us  [per_device(): lax.all_to_all(total_for(got, nodes), 'node', split_axis=0, concat_axis=0...]
    ppermute x8, waiting for transfers between devices: 8.18 us -> 16 us  [per_device(): lax.ppermute(one, 'local', right)]
    all_to_all x2 -> x1, starting transfers between devices: 20.7 us -> 14.9 us  [per_device(): lax.all_to_all(total_for(got, nodes), 'node', split_axis=0, concat_axis=0...]
    unnamed x41 -> x24, local copies, waits for them, and re-layouts: 6.88 us -> 7.43 us
  transfers between devices with their start and end apart: 18 -> 17, of which waited for: 10 -> 10; matrix products, arithmetic and copies ran while one was open for 1% -> 2% of each run, Pallas kernels for 17% -> 11%
where the time goes in v3:
time: 184 us; the launch traced here: 183 us
  starting transfers between devices  75.4 us (41%)
  blocking collectives  47.9 us (26%)
  Pallas kernels  25.2 us (14%)
  waiting for transfers between devices  22.5 us (12%)
  local copies, waits for them, and re-layouts  10 us (5%)
    ppermute x8, starting transfers between devices, per_device(): lax.ppermute(other, 'local', left)  45.1 us
    all_to_all x1, blocking collectives, per_device(): lax.all_to_all(packed, 'node', split_axis=0, concat_axis=0, tiled=True)  32.6 us
    ppermute x8, waiting for transfers between devices, per_device(): lax.ppermute(one, 'local', right)  16 us
    all_to_all x1, blocking collectives, per_device(): got = lax.all_to_all(part, 'local', split_axis=0, concat_axis=0, tiled=True)  15.3 us
    ppermute x8, starting transfers between devices, per_device(): lax.ppermute(one, 'local', right)  15.3 us
    all_to_all x1, starting transfers between devices, per_device(): lax.all_to_all(total_for(got, nodes), 'node', split_axis=0, concat_axis=0...  14.9 us
    pallas_call x5, Pallas kernels, down(): pl.pallas_call(lambda *refs: down_kernel(len(blocks), *refs), grid=(width...  13.3 us
    unnamed x24, local copies, waits for them, and re-layouts  7.43 us
  transfers between devices with their start and end apart: 17, of which 10 were waited for; matrix products, arithmetic and copies ran while one was open for 2% of the time, Pallas kernels for 11%

profile of v3, /device:TPU:1, one launch (start us, length us, event | category | flops | bytes accessed | tf_op | source)
XLA Modules:
  0.0 182.7 jit_solution(6481714644527888265)
XLA Ops:
  3.9 32.6 %all_to_all.15.got_ref = bf16[64,8,384]{2,1,0:T(8,128)(2,1)S(1)} all-to-all(bf16[64,8,384]{2,1,0:T(8,128)(2,1)S(1)} %get-tuple-element.34), channel_id=1, replica_groups=mesh['node'=64,'local'=16] {'node'}, dimensions={0} | all-to-all | bytes 786432 | tf_op jit(solution)/shard_map/all_to_all | solution.py:298
  37.0 1.9 %collective-permute-start = (bf16[32,6144]{1,0:T(8,128)(2,1)S(1)}, bf16[32,6144]{1,0:T(8,128)(2,1)S(1)}, u32[]{:S(2)}, u32[]{:S(2)}) collective-permute-start(bf16[32,6144]{1,0:T(8,128)(2,1)S(1)} %unpack.1.refs_0_.refs_1_), channel_id=1, source_target_pairs={{0,1},{1,2},{2,3},{3,4},{4,5},{5,6},{6,7},{7,8},{8,9},{9,10},{10,1... | collective-permute-start | bytes 1179656 | tf_op jit(solution)/shard_map/ppermute | solution.py:319
  38.9 11.9 %collective-permute-start.2 = (bf16[32,6144]{1,0:T(8,128)(2,1)S(1)}, bf16[32,6144]{1,0:T(8,128)(2,1)S(1)}, u32[]{:S(2)}, u32[]{:S(2)}) collective-permute-start(bf16[32,6144]{1,0:T(8,128)(2,1)S(1)} %unpack.1.refs_0_.refs_1_), channel_id=1, source_target_pairs={{0,15},{1,0},{2,1},{3,2},{4,3},{5,4},{6,5},{7,6},{8,7},{9,8},{10,9... | collective-permute-start | bytes 1179656 | tf_op jit(solution)/shard_map/ppermute | solution.py:319
  52.8 5.3 %collective-permute-done.refs_0_.refs_2_ = bf16[32,6144]{1,0:T(8,128)(2,1)S(1)} collective-permute-done((bf16[32,6144]{1,0:T(8,128)(2,1)S(1)}, bf16[32,6144]{1,0:T(8,128)(2,1)S(1)}, u32[]{:S(2)}, u32[]{:S(2)}) %collective-permute-start) | collective-permute-done | bytes 393248 | tf_op jit(solution)/shard_map/ppermute | solution.py:319
  60.0 4.6 %collective-permute-start.4 = (bf16[32,6144]{1,0:T(8,128)(2,1)S(1)}, bf16[32,6144]{1,0:T(8,128)(2,1)}, u32[]{:S(2)}, u32[]{:S(2)}) collective-permute-start(bf16[32,6144]{1,0:T(8,128)(2,1)S(1)} %collective-permute-done.2.refs_1_.refs_3_), channel_id=1, source_target_pairs={{0,15},{1,0},{2,1},{3,2},{4,3},{5,4},{6,5},{7,6},{8,7},{9,8},{10,9... | collective-permute-start | bytes 1179656 | tf_op jit(solution)/shard_map/ppermute | solution.py:319
  73.0 4.6 %collective-permute-start.6 = (bf16[32,6144]{1,0:T(8,128)(2,1)}, bf16[32,6144]{1,0:T(8,128)(2,1)S(1)}, u32[]{:S(2)}, u32[]{:S(2)}) collective-permute-start(bf16[32,6144]{1,0:T(8,128)(2,1)} %collective-permute-done.4.refs_1_.refs_2_), channel_id=1, source_target_pairs={{0,15},{1,0},{2,1},{3,2},{4,3},{5,4},{6,5},{7,6},{8,7},{9,8},{10,9... | collective-permute-start | bytes 1179656 | tf_op jit(solution)/shard_map/ppermute | solution.py:319
  79.2 3.9 %collective-permute-done.3.refs_0_.refs_3_ = bf16[32,6144]{1,0:T(8,128)(2,1)S(1)} collective-permute-done((bf16[32,6144]{1,0:T(8,128)(2,1)S(1)}, bf16[32,6144]{1,0:T(8,128)(2,1)S(1)}, u32[]{:S(2)}, u32[]{:S(2)}) %collective-permute-start.3) | collective-permute-done | bytes 393248 | tf_op jit(solution)/shard_map/ppermute | solution.py:319
  85.0 4.6 %collective-permute-start.8 = (bf16[32,6144]{1,0:T(8,128)(2,1)S(1)}, bf16[32,6144]{1,0:T(8,128)(2,1)S(1)}, u32[]{:S(2)}, u32[]{:S(2)}) collective-permute-start(bf16[32,6144]{1,0:T(8,128)(2,1)S(1)} %collective-permute-done.6.refs_1_.refs_4_), channel_id=1, source_target_pairs={{0,15},{1,0},{2,1},{3,2},{4,3},{5,4},{6,5},{7,6},{8,7},{9,8},{10,9... | collective-permute-start | bytes 1179656 | tf_op jit(solution)/shard_map/ppermute | solution.py:319
  90.3 3.8 %down.6.refs_5_ = f32[128,6144]{1,0:T(8,128)S(1)} custom-call(bf16[256,128]{1,0:T(8,128)(2,1)S(1)} %get-tuple-element.43.refs_0_, bf16[32,6144]{1,0:T(8,128)(2,1)S(1)} %collective-permute-done.1.refs_0_.refs_1_, bf16[32,6144]{1,0:T(8,128)(2,1)} %collective-permute-done.4.refs_1_.refs_2_, ...), custom_call_target="tpu_custom_call", output_to_operand_aliasing={{}: (5, {})} | custom-call | flops 402653184 | bytes 7864320 | tf_op jit(solution)/shard_map/down/pallas_call | solution.py:219
  96.1 4.6 %collective-permute-start.10 = (bf16[32,6144]{1,0:T(8,128)(2,1)S(1)}, bf16[32,6144]{1,0:T(8,128)(2,1)S(1)}, u32[]{:S(2)}, u32[]{:S(2)}) collective-permute-start(bf16[32,6144]{1,0:T(8,128)(2,1)S(1)} %collective-permute-done.8.refs_1_.refs_2_), channel_id=1, source_target_pairs={{0,15},{1,0},{2,1},{3,2},{4,3},{5,4},{6,5},{7,6},{8,7},{9,8},{10,9... | collective-permute-start | bytes 1179656 | tf_op jit(solution)/shard_map/ppermute | solution.py:319
  101.4 3.0 %collective-permute-done.7.refs_0_.refs_3_ = bf16[32,6144]{1,0:T(8,128)(2,1)S(1)} collective-permute-done((bf16[32,6144]{1,0:T(8,128)(2,1)S(1)}, bf16[32,6144]{1,0:T(8,128)(2,1)S(1)}, u32[]{:S(2)}, u32[]{:S(2)}) %collective-permute-start.7) | collective-permute-done | bytes 393248 | tf_op jit(solution)/shard_map/ppermute | solution.py:319
  105.4 5.0 %collective-permute-start.12 = (bf16[32,6144]{1,0:T(8,128)(2,1)S(1)}, bf16[32,6144]{1,0:T(8,128)(2,1)S(1)}, u32[]{:S(2)}, u32[]{:S(2)}) collective-permute-start(bf16[32,6144]{1,0:T(8,128)(2,1)S(1)} %collective-permute-done.10.refs_1_.refs_4_), channel_id=1, source_target_pairs={{0,15},{1,0},{2,1},{3,2},{4,3},{5,4},{6,5},{7,6},{8,7},{9,8},{10,9... | collective-permute-start | bytes 1179656 | tf_op jit(solution)/shard_map/ppermute | solution.py:319
  110.4 1.9 %collective-permute-start.9 = (bf16[32,6144]{1,0:T(8,128)(2,1)S(1)}, bf16[32,6144]{1,0:T(8,128)(2,1)S(1)}, u32[]{:S(2)}, u32[]{:S(2)}) collective-permute-start(bf16[32,6144]{1,0:T(8,128)(2,1)S(1)} %collective-permute-done.7.refs_0_.refs_3_), channel_id=1, source_target_pairs={{0,1},{1,2},{2,3},{3,4},{4,5},{5,6},{6,7},{7,8},{8,9},{9,10},{10,1... | collective-permute-start | bytes 1179656 | tf_op jit(solution)/shard_map/ppermute | solution.py:319
  113.0 2.2 %down.7.refs_5_ = f32[128,6144]{1,0:T(8,128)S(1)} custom-call(bf16[256,128]{1,0:T(8,128)(2,1)S(1)} %get-tuple-element.50.refs_0_, bf16[32,6144]{1,0:T(8,128)(2,1)S(1)} %collective-permute-done.5.refs_0_.refs_1_, bf16[32,6144]{1,0:T(8,128)(2,1)S(1)} %collective-permute-done.8.refs_1_.refs_2_, ...), custom_call_target="tpu_custom_call", output_to_operand_aliasing={{}: (5, {})} | custom-call | flops 402653184 | bytes 7864320 | tf_op jit(solution)/shard_map/down/pallas_call | solution.py:219
  115.2 4.9 %collective-permute-start.13 = (bf16[32,6144]{1,0:T(8,128)(2,1)S(1)}, bf16[32,6144]{1,0:T(8,128)(2,1)S(1)}, u32[]{:S(2)}, u32[]{:S(2)}) collective-permute-start(bf16[32,6144]{1,0:T(8,128)(2,1)S(1)} %collective-permute-done.12.refs_1_.refs_2_), channel_id=1, source_target_pairs={{0,15},{1,0},{2,1},{3,2},{4,3},{5,4},{6,5},{7,6},{8,7},{9,8},{10,9... | collective-permute-start | bytes 1179656 | tf_op jit(solution)/shard_map/ppermute | solution.py:319
  122.8 2.1 %collective-permute-done.13.refs_1_.refs_4_ = bf16[32,6144]{1,0:T(8,128)(2,1)S(1)} collective-permute-done((bf16[32,6144]{1,0:T(8,128)(2,1)S(1)}, bf16[32,6144]{1,0:T(8,128)(2,1)S(1)}, u32[]{:S(2)}, u32[]{:S(2)}) %collective-permute-start.13) | collective-permute-done | bytes 393248 | tf_op jit(solution)/shard_map/ppermute | solution.py:319
  124.9 5.0 %collective-permute-start.15 = (bf16[16,6144]{1,0:T(8,128)(2,1)S(1)}, bf16[16,6144]{1,0:T(8,128)(2,1)S(1)}, u32[]{:S(2)}, u32[]{:S(2)}) collective-permute-start(bf16[16,6144]{1,0:T(8,128)(2,1)S(1)} %slice.9), channel_id=1, source_target_pairs={{0,15},{1,0},{2,1},{3,2},{4,3},{5,4},{6,5},{7,6},{8,7},{9,8},{10,9... | collective-permute-start | bytes 589832 | tf_op jit(solution)/shard_map/ppermute | solution.py:319
  130.1 1.9 %collective-permute-start.14 = (bf16[16,6144]{1,0:T(8,128)(2,1)S(1)}, bf16[16,6144]{1,0:T(8,128)(2,1)S(1)}, u32[]{:S(2)}, u32[]{:S(2)}) collective-permute-start(bf16[16,6144]{1,0:T(8,128)(2,1)S(1)} %slice.8), channel_id=1, source_target_pairs={{0,1},{1,2},{2,3},{3,4},{4,5},{5,6},{6,7},{7,8},{8,9},{9,10},{10,1... | collective-permute-start | bytes 589832 | tf_op jit(solution)/shard_map/ppermute | solution.py:319
  132.7 2.2 %down.8.refs_3_ = f32[128,6144]{1,0:T(8,128)S(1)} custom-call(bf16[256,128]{1,0:T(8,128)(2,1)S(1)} %get-tuple-element.57.refs_0_, bf16[32,6144]{1,0:T(8,128)(2,1)S(1)} %collective-permute-done.9.refs_0_.refs_1_, bf16[32,6144]{1,0:T(8,128)(2,1)S(1)} %collective-permute-done.12.refs_1_.refs_2_, ...), custom_call_target="tpu_custom_call", output_to_operand_aliasing={{}: (5, {})} | custom-call | flops 402653184 | bytes 7864320 | tf_op jit(solution)/shard_map/down/pallas_call | solution.py:219
  136.5 2.4 %collective-permute-done.14.refs_0_.refs_1_ = bf16[16,6144]{1,0:T(8,128)(2,1)S(1)} collective-permute-done((bf16[16,6144]{1,0:T(8,128)(2,1)S(1)}, bf16[16,6144]{1,0:T(8,128)(2,1)S(1)}, u32[]{:S(2)}, u32[]{:S(2)}) %collective-permute-start.14) | collective-permute-done | bytes 196640 | tf_op jit(solution)/shard_map/ppermute | solution.py:319
  140.7 15.3 %all_to_all.16.got_ref = f32[16,1,64]{2,1,0:T(1,128)} all-to-all(f32[16,1,64]{2,1,0:T(1,128)S(1)} %get-tuple-element.64), channel_id=1, replica_groups=mesh['node'=64,'local'=16] {'local'}, dimensions={0} | all-to-all | bytes 8192 | tf_op jit(solution)/shard_map/all_to_all | solution.py:328
  157.4 14.9 %all-to-all-start.2 = ((f32[64,1,64]{2,1,0:T(1,128)}), f32[64,1,64]{2,1,0:T(1,128)S(1)}, u32[]{:S(2)}, u32[]{:S(2)}) async-start(f32[64,1,64]{2,1,0:T(1,128)} %total.1), calls=%async_computation.2 | async-start | bytes 65536 | tf_op jit(solution)/shard_map/all_to_all | solution.py:329
  175.0 3.3 %down.9 = bf16[128,6144]{1,0:T(8,128)(2,1)} custom-call(bf16[64,128]{1,0:T(8,128)(2,1)S(1)} %copy-done.5, bf16[16,6144]{1,0:T(8,128)(2,1)S(1)} %collective-permute-done.14.refs_0_.refs_1_, bf16[16,6144]{1,0:T(8,128)(2,1)S(1)} %collective-permute-done.15.refs_1_.refs_2_, f32[128,6144]{1,0:T(8,128)S(1)} %copy-done.3), custom_call_target="tpu_custom_call" | custom-call | flops 100663296 | bytes 6684672 | tf_op jit(solution)/shard_map/down/pallas_call | solution.py:219
  178.3 3.3 %all-to-all-done.2.table_ref = f32[64,1,64]{2,1,0:T(1,128)S(1)} async-done(((f32[64,1,64]{2,1,0:T(1,128)}), f32[64,1,64]{2,1,0:T(1,128)S(1)}, u32[]{:S(2)}, u32[]{:S(2)}) %all-to-all-start.2) | async-done | bytes 16416 | tf_op jit(solution)/shard_map/all_to_all | solution.py:329
  (62 shorter events, 36.5 us)
Async XLA Ops:
  0.6 66.8 %copy-start.1 = (bf16[2,64,6144]{2,1,0:T(8,128)(2,1)S(1)}, bf16[2,64,6144]{2,1,0:T(8,128)(2,1)}, u32[]{:S(2)}) copy-start(bf16[2,64,6144]{2,1,0:T(8,128)(2,1)} %param.10) | copy-start | bytes 4718596
  2.4 62.2 %copy-start.10 = (f32[1,16,32,2]{2,3,1,0:T(2,128)S(1)}, f32[1,16,32,2]{2,3,1,0:T(2,128)}, u32[]{:S(2)}) copy-start(f32[1,16,32,2]{2,3,1,0:T(2,128)} %param.8) | copy-start | bytes 12292
  37.0 21.1 %collective-permute-start = (bf16[32,6144]{1,0:T(8,128)(2,1)S(1)}, bf16[32,6144]{1,0:T(8,128)(2,1)S(1)}, u32[]{:S(2)}, u32[]{:S(2)}) collective-permute-start(bf16[32,6144]{1,0:T(8,128)(2,1)S(1)} %unpack.1.refs_0_.refs_1_), channel_id=1, source_target_pairs={{0,1},{1,2},{2,3},{3,4},{4,5},{5,6},{6,7},{7,8},{8,9},{9,10},{10,1... | collective-permute-start | bytes 1179656 | tf_op jit(solution)/shard_map/ppermute | solution.py:319
  38.9 21.1 %collective-permute-start.2 = (bf16[32,6144]{1,0:T(8,128)(2,1)S(1)}, bf16[32,6144]{1,0:T(8,128)(2,1)S(1)}, u32[]{:S(2)}, u32[]{:S(2)}) collective-permute-start(bf16[32,6144]{1,0:T(8,128)(2,1)S(1)} %unpack.1.refs_0_.refs_1_), channel_id=1, source_target_pairs={{0,15},{1,0},{2,1},{3,2},{4,3},{5,4},{6,5},{7,6},{8,7},{9,8},{10,9... | collective-permute-start | bytes 1179656 | tf_op jit(solution)/shard_map/ppermute | solution.py:319
  58.1 13.0 %collective-permute-start.1 = (bf16[32,6144]{1,0:T(8,128)(2,1)S(1)}, bf16[32,6144]{1,0:T(8,128)(2,1)S(1)}, u32[]{:S(2)}, u32[]{:S(2)}) collective-permute-start(bf16[32,6144]{1,0:T(8,128)(2,1)S(1)} %collective-permute-done.refs_0_.refs_2_), channel_id=1, source_target_pairs={{0,1},{1,2},{2,3},{3,4},{4,5},{5,6},{6,7},{7,8},{8,9},{9,10},{10,1... | collective-permute-start | bytes 1179656 | tf_op jit(solution)/shard_map/ppermute | solution.py:319
  60.0 13.0 %collective-permute-start.4 = (bf16[32,6144]{1,0:T(8,128)(2,1)S(1)}, bf16[32,6144]{1,0:T(8,128)(2,1)}, u32[]{:S(2)}, u32[]{:S(2)}) collective-permute-start(bf16[32,6144]{1,0:T(8,128)(2,1)S(1)} %collective-permute-done.2.refs_1_.refs_3_), channel_id=1, source_target_pairs={{0,15},{1,0},{2,1},{3,2},{4,3},{5,4},{6,5},{7,6},{8,7},{9,8},{10,9... | collective-permute-start | bytes 1179656 | tf_op jit(solution)/shard_map/ppermute | solution.py:319
  67.4 2.5 %copy-start.4 = (bf16[64,128]{1,0:T(8,128)(2,1)}, bf16[64,128]{1,0:T(8,128)(2,1)S(1)}, u32[]{:S(2)}) copy-start(bf16[64,128]{1,0:T(8,128)(2,1)S(1)} %get-tuple-element.61.refs_0_) | copy-start | bytes 49156
  71.1 12.0 %collective-permute-start.3 = (bf16[32,6144]{1,0:T(8,128)(2,1)S(1)}, bf16[32,6144]{1,0:T(8,128)(2,1)S(1)}, u32[]{:S(2)}, u32[]{:S(2)}) collective-permute-start(bf16[32,6144]{1,0:T(8,128)(2,1)S(1)} %collective-permute-done.1.refs_0_.refs_1_), channel_id=1, source_target_pairs={{0,1},{1,2},{2,3},{3,4},{4,5},{5,6},{6,7},{7,8},{8,9},{9,10},{10,1... | collective-permute-start | bytes 1179656 | tf_op jit(solution)/shard_map/ppermute | solution.py:319
  73.0 12.0 %collective-permute-start.6 = (bf16[32,6144]{1,0:T(8,128)(2,1)}, bf16[32,6144]{1,0:T(8,128)(2,1)S(1)}, u32[]{:S(2)}, u32[]{:S(2)}) collective-permute-start(bf16[32,6144]{1,0:T(8,128)(2,1)} %collective-permute-done.4.refs_1_.refs_2_), channel_id=1, source_target_pairs={{0,15},{1,0},{2,1},{3,2},{4,3},{5,4},{6,5},{7,6},{8,7},{9,8},{10,9... | collective-permute-start | bytes 1179656 | tf_op jit(solution)/shard_map/ppermute | solution.py:319
  83.1 11.1 %collective-permute-start.5 = (bf16[32,6144]{1,0:T(8,128)(2,1)S(1)}, bf16[32,6144]{1,0:T(8,128)(2,1)S(1)}, u32[]{:S(2)}, u32[]{:S(2)}) collective-permute-start(bf16[32,6144]{1,0:T(8,128)(2,1)S(1)} %collective-permute-done.3.refs_0_.refs_3_), channel_id=1, source_target_pairs={{0,1},{1,2},{2,3},{3,4},{4,5},{5,6},{6,7},{7,8},{8,9},{9,10},{10,1... | collective-permute-start | bytes 1179656 | tf_op jit(solution)/shard_map/ppermute | solution.py:319
  85.0 11.1 %collective-permute-start.8 = (bf16[32,6144]{1,0:T(8,128)(2,1)S(1)}, bf16[32,6144]{1,0:T(8,128)(2,1)S(1)}, u32[]{:S(2)}, u32[]{:S(2)}) collective-permute-start(bf16[32,6144]{1,0:T(8,128)(2,1)S(1)} %collective-permute-done.6.refs_1_.refs_4_), channel_id=1, source_target_pairs={{0,15},{1,0},{2,1},{3,2},{4,3},{5,4},{6,5},{7,6},{8,7},{9,8},{10,9... | collective-permute-start | bytes 1179656 | tf_op jit(solution)/shard_map/ppermute | solution.py:319
  94.2 10.2 %collective-permute-start.7 = (bf16[32,6144]{1,0:T(8,128)(2,1)S(1)}, bf16[32,6144]{1,0:T(8,128)(2,1)S(1)}, u32[]{:S(2)}, u32[]{:S(2)}) collective-permute-start(bf16[32,6144]{1,0:T(8,128)(2,1)S(1)} %collective-permute-done.5.refs_0_.refs_1_), channel_id=1, source_target_pairs={{0,1},{1,2},{2,3},{3,4},{4,5},{5,6},{6,7},{7,8},{8,9},{9,10},{10,1... | collective-permute-start | bytes 1179656 | tf_op jit(solution)/shard_map/ppermute | solution.py:319
  96.1 9.3 %collective-permute-start.10 = (bf16[32,6144]{1,0:T(8,128)(2,1)S(1)}, bf16[32,6144]{1,0:T(8,128)(2,1)S(1)}, u32[]{:S(2)}, u32[]{:S(2)}) collective-permute-start(bf16[32,6144]{1,0:T(8,128)(2,1)S(1)} %collective-permute-done.8.refs_1_.refs_2_), channel_id=1, source_target_pairs={{0,15},{1,0},{2,1},{3,2},{4,3},{5,4},{6,5},{7,6},{8,7},{9,8},{10,9... | collective-permute-start | bytes 1179656 | tf_op jit(solution)/shard_map/ppermute | solution.py:319
  105.4 9.8 %collective-permute-start.12 = (bf16[32,6144]{1,0:T(8,128)(2,1)S(1)}, bf16[32,6144]{1,0:T(8,128)(2,1)S(1)}, u32[]{:S(2)}, u32[]{:S(2)}) collective-permute-start(bf16[32,6144]{1,0:T(8,128)(2,1)S(1)} %collective-permute-done.10.refs_1_.refs_4_), channel_id=1, source_target_pairs={{0,15},{1,0},{2,1},{3,2},{4,3},{5,4},{6,5},{7,6},{8,7},{9,8},{10,9... | collective-permute-start | bytes 1179656 | tf_op jit(solution)/shard_map/ppermute | solution.py:319
  110.4 9.7 %collective-permute-start.9 = (bf16[32,6144]{1,0:T(8,128)(2,1)S(1)}, bf16[32,6144]{1,0:T(8,128)(2,1)S(1)}, u32[]{:S(2)}, u32[]{:S(2)}) collective-permute-start(bf16[32,6144]{1,0:T(8,128)(2,1)S(1)} %collective-permute-done.7.refs_0_.refs_3_), channel_id=1, source_target_pairs={{0,1},{1,2},{2,3},{3,4},{4,5},{5,6},{6,7},{7,8},{8,9},{9,10},{10,1... | collective-permute-start | bytes 1179656 | tf_op jit(solution)/shard_map/ppermute | solution.py:319
  115.2 9.6 %collective-permute-start.13 = (bf16[32,6144]{1,0:T(8,128)(2,1)S(1)}, bf16[32,6144]{1,0:T(8,128)(2,1)S(1)}, u32[]{:S(2)}, u32[]{:S(2)}) collective-permute-start(bf16[32,6144]{1,0:T(8,128)(2,1)S(1)} %collective-permute-done.12.refs_1_.refs_2_), channel_id=1, source_target_pairs={{0,15},{1,0},{2,1},{3,2},{4,3},{5,4},{6,5},{7,6},{8,7},{9,8},{10,9... | collective-permute-start | bytes 1179656 | tf_op jit(solution)/shard_map/ppermute | solution.py:319
  120.2 9.9 %collective-permute-start.11 = (bf16[32,6144]{1,0:T(8,128)(2,1)S(1)}, bf16[32,6144]{1,0:T(8,128)(2,1)S(1)}, u32[]{:S(2)}, u32[]{:S(2)}) collective-permute-start(bf16[32,6144]{1,0:T(8,128)(2,1)S(1)} %collective-permute-done.9.refs_0_.refs_1_), channel_id=1, source_target_pairs={{0,1},{1,2},{2,3},{3,4},{4,5},{5,6},{6,7},{7,8},{8,9},{9,10},{10,1... | collective-permute-start | bytes 1179656 | tf_op jit(solution)/shard_map/ppermute | solution.py:319
  124.9 11.6 %collective-permute-start.15 = (bf16[16,6144]{1,0:T(8,128)(2,1)S(1)}, bf16[16,6144]{1,0:T(8,128)(2,1)S(1)}, u32[]{:S(2)}, u32[]{:S(2)}) collective-permute-start(bf16[16,6144]{1,0:T(8,128)(2,1)S(1)} %slice.9), channel_id=1, source_target_pairs={{0,15},{1,0},{2,1},{3,2},{4,3},{5,4},{6,5},{7,6},{8,7},{9,8},{10,9... | collective-permute-start | bytes 589832 | tf_op jit(solution)/shard_map/ppermute | solution.py:319
  130.1 8.8 %collective-permute-start.14 = (bf16[16,6144]{1,0:T(8,128)(2,1)S(1)}, bf16[16,6144]{1,0:T(8,128)(2,1)S(1)}, u32[]{:S(2)}, u32[]{:S(2)}) collective-permute-start(bf16[16,6144]{1,0:T(8,128)(2,1)S(1)} %slice.8), channel_id=1, source_target_pairs={{0,1},{1,2},{2,3},{3,4},{4,5},{5,6},{6,7},{7,8},{8,9},{9,10},{10,1... | collective-permute-start | bytes 589832 | tf_op jit(solution)/shard_map/ppermute | solution.py:319
  136.5 36.6 %copy-start.5 = (bf16[64,128]{1,0:T(8,128)(2,1)S(1)}, bf16[64,128]{1,0:T(8,128)(2,1)}, u32[]{:S(2)}) copy-start(bf16[64,128]{1,0:T(8,128)(2,1)} %copy-done.4) | copy-start | bytes 49156
  139.5 42.1 %copy-start.7 = (s32[256,4]{0,1:T(4,128)S(1)}, s32[256,4]{0,1:T(4,128)}, u32[]{:S(2)}) copy-start(s32[256,4]{0,1:T(4,128)} %param.7) | copy-start | bytes 12292
  139.5 42.1 %copy-start.9 = (s32[4,256]{1,0:T(4,128)S(1)}, s32[4,256]{1,0:T(4,128)}, u32[]{:S(2)}) copy-start(s32[4,256]{1,0:T(4,128)} %copy-done.8) | copy-start | bytes 12292
  157.4 24.3 %all-to-all-start.2 = ((f32[64,1,64]{2,1,0:T(1,128)}), f32[64,1,64]{2,1,0:T(1,128)S(1)}, u32[]{:S(2)}, u32[]{:S(2)}) async-start(f32[64,1,64]{2,1,0:T(1,128)} %total.1), calls=%async_computation.2 | async-start | bytes 65536 | tf_op jit(solution)/shard_map/all_to_all | solution.py:329
  173.1 1.9 %copy-start.3 = (f32[128,6144]{1,0:T(8,128)S(1)}, f32[128,6144]{1,0:T(8,128)}, u32[]{:S(2)}) copy-start(f32[128,6144]{1,0:T(8,128)} %copy-done.2) | copy-start | bytes 9437188
  (4 other events, 4.3 us)

commit v4 on v3

--- a/solution.py
+++ b/solution.py
@@ -314,8 +314,11 @@
     for k in range(1, steps + 1):
         if k == steps:
             one, other = one[: cap // 2], other[cap // 2 :]
+        if k == 2:
+            one, *scaled = lax.optimization_barrier((one, *scaled))
         if k > 1:
             one, ups[-1], total = lax.optimization_barrier((one, ups[-1], total))
+            other, ups[-1] = lax.optimization_barrier((other, ups[-1]))
         one, other = lax.ppermute(one, "local", right), lax.ppermute(other, "local", left)
         ups.append(up(blocks[-1], w))
         for at, group in enumerate(groups):
@@ -326,11 +329,13 @@
     ups.append(up(blocks[-1], w))
     grad_h, part = close(shards, ups, saved, gate)
     got = lax.all_to_all(part, "local", split_axis=0, concat_axis=0, tiled=True)
+    grad_h = grad_h.reshape(1, local, cap, per_dev, units)
+    grad_w = add(len(groups) - 1, BF)
+    got, grad_w, grad_h = lax.optimization_barrier((got, grad_w, grad_h))
     table = lax.all_to_all(total_for(got, nodes), "node", split_axis=0, concat_axis=0, tiled=True)
-    grad_w = add(len(groups) - 1, BF)
     d_gates = look(ids, slot, table, per_dev)
     return (
-        grad_h.reshape(1, local, cap, per_dev, units),
+        grad_h,
         grad_w.reshape(per_dev, units, width),
         d_gates.reshape(node_ids.shape[1], per_dev, -1).transpose(2, 0, 1),
     )

time: 184 us -> 184 us (level)
  starting transfers between devices: 75.4 us -> 63.2 us
  blocking collectives: 47.9 us -> 58.3 us
  waiting for transfers between devices: 22.5 us -> 27.6 us
  Pallas kernels: 25.2 us -> 23.3 us
    all_to_all x1, starting transfers between devices: 14.9 us -> 3.59 us  [per_device(): got = lax.all_to_all(part, 'local', split_axis=0, concat_axis=0, tiled=True)]
    all_to_all x1, blocking collectives: 15.3 us -> 25.8 us  [per_device(): lax.all_to_all(total_for(got, nodes), 'node', split_axis=0, concat_axis=0...]
    ppermute x8, waiting for transfers between devices: 16 us -> 20.9 us  [per_device(): lax.ppermute(one, 'local', right)]
    all_to_all x1, waiting for transfers between devices: 3.34 us -> 5.18 us  [per_device(): got = lax.all_to_all(part, 'local', split_axis=0, concat_axis=0, tiled=True)]
    unnamed x24 -> x14, local copies, waits for them, and re-layouts: 7.43 us -> 6.71 us
  transfers between devices with their start and end apart: 17 -> 17, of which waited for: 10 -> 10; matrix products, arithmetic and copies ran while one was open for 2% -> 2% of each run, Pallas kernels for 11% -> 10%
where the time goes in v4:
time: 184 us; the launch traced here: 183 us
  starting transfers between devices  63.2 us (34%)
  blocking collectives  58.3 us (32%)
  waiting for transfers between devices  27.6 us (15%)
  Pallas kernels  23.3 us (13%)
  local copies, waits for them, and re-layouts  9.33 us (5%)
    ppermute x8, starting transfers between devices, per_device(): lax.ppermute(other, 'local', left)  44.3 us
    all_to_all x1, blocking collectives, per_device(): lax.all_to_all(packed, 'node', split_axis=0, concat_axis=0, tiled=True)  32.6 us
    all_to_all x1, blocking collectives, per_device(): lax.all_to_all(total_for(got, nodes), 'node', split_axis=0, concat_axis=0...  25.8 us
    ppermute x8, waiting for transfers between devices, per_device(): lax.ppermute(one, 'local', right)  20.9 us
    ppermute x8, starting transfers between devices, per_device(): lax.ppermute(one, 'local', right)  15.3 us
    pallas_call x5, Pallas kernels, down(): pl.pallas_call(lambda *refs: down_kernel(len(blocks), *refs), grid=(width...  11.7 us
    unnamed x14, local copies, waits for them, and re-layouts  6.71 us
    pallas_call x9, Pallas kernels, up(): pl.pallas_call(up_kernel, out_shape=jax.ShapeDtypeStruct((slots, units),...  5.9 us
  transfers between devices with their start and end apart: 17, of which 10 were waited for; matrix products, arithmetic and copies ran while one was open for 2% of the time, Pallas kernels for 10%

profile of v4, /device:TPU:1, one launch (start us, length us, event | category | flops | bytes accessed | tf_op | source)
XLA Modules:
  0.0 183.4 jit_solution(17027923565088237499)
XLA Ops:
  3.3 32.6 %all_to_all.15.got_ref = bf16[64,8,384]{2,1,0:T(8,128)(2,1)S(1)} all-to-all(bf16[64,8,384]{2,1,0:T(8,128)(2,1)S(1)} %get-tuple-element.57), channel_id=1, replica_groups=mesh['node'=64,'local'=16] {'node'}, dimensions={0} | all-to-all | bytes 786432 | tf_op jit(solution)/shard_map/all_to_all | solution.py:298
  36.4 1.9 %collective-permute-start.1 = (bf16[32,6144]{1,0:T(8,128)(2,1)S(1)}, bf16[32,6144]{1,0:T(8,128)(2,1)S(1)}, u32[]{:S(2)}, u32[]{:S(2)}) collective-permute-start(bf16[32,6144]{1,0:T(8,128)(2,1)S(1)} %unpack.1.refs_0_.refs_1_), channel_id=1, source_target_pairs={{0,1},{1,2},{2,3},{3,4},{4,5},{5,6},{6,7},{7,8},{8,9},{9,10},{10,1... | collective-permute-start | bytes 1179656 | tf_op jit(solution)/shard_map/ppermute | solution.py:322
  38.3 11.9 %collective-permute-start = (bf16[32,6144]{1,0:T(8,128)(2,1)S(1)}, bf16[32,6144]{1,0:T(8,128)(2,1)S(1)}, u32[]{:S(2)}, u32[]{:S(2)}) collective-permute-start(bf16[32,6144]{1,0:T(8,128)(2,1)S(1)} %unpack.1.refs_0_.refs_1_), channel_id=1, source_target_pairs={{0,15},{1,0},{2,1},{3,2},{4,3},{5,4},{6,5},{7,6},{8,7},{9,8},{10,9... | collective-permute-start | bytes 1179656 | tf_op jit(solution)/shard_map/ppermute | solution.py:322
  54.3 3.2 %collective-permute-done.1.refs_0_.refs_2_ = bf16[32,6144]{1,0:T(8,128)(2,1)S(1)} collective-permute-done((bf16[32,6144]{1,0:T(8,128)(2,1)S(1)}, bf16[32,6144]{1,0:T(8,128)(2,1)S(1)}, u32[]{:S(2)}, u32[]{:S(2)}) %collective-permute-start.1) | collective-permute-done | bytes 393248 | tf_op jit(solution)/shard_map/ppermute | solution.py:322
  57.5 1.9 %collective-permute-start.3 = (bf16[32,6144]{1,0:T(8,128)(2,1)S(1)}, bf16[32,6144]{1,0:T(8,128)(2,1)S(1)}, u32[]{:S(2)}, u32[]{:S(2)}) collective-permute-start(bf16[32,6144]{1,0:T(8,128)(2,1)S(1)} %collective-permute-done.1.refs_0_.refs_2_), channel_id=1, source_target_pairs={{0,1},{1,2},{2,3},{3,4},{4,5},{5,6},{6,7},{7,8},{8,9},{9,10},{10,1... | collective-permute-start | bytes 1179656 | tf_op jit(solution)/shard_map/ppermute | solution.py:322
  59.4 4.6 %collective-permute-start.2 = (bf16[32,6144]{1,0:T(8,128)(2,1)S(1)}, bf16[32,6144]{1,0:T(8,128)(2,1)S(1)}, u32[]{:S(2)}, u32[]{:S(2)}) collective-permute-start(bf16[32,6144]{1,0:T(8,128)(2,1)S(1)} %collective-permute-done.refs_1_.refs_3_), channel_id=1, source_target_pairs={{0,15},{1,0},{2,1},{3,2},{4,3},{5,4},{6,5},{7,6},{8,7},{9,8},{10,9... | collective-permute-start | bytes 1179656 | tf_op jit(solution)/shard_map/ppermute | solution.py:322
  66.5 3.9 %collective-permute-done.3.refs_0_.refs_1_ = bf16[32,6144]{1,0:T(8,128)(2,1)S(1)} collective-permute-done((bf16[32,6144]{1,0:T(8,128)(2,1)S(1)}, bf16[32,6144]{1,0:T(8,128)(2,1)S(1)}, u32[]{:S(2)}, u32[]{:S(2)}) %collective-permute-start.3) | collective-permute-done | bytes 393248 | tf_op jit(solution)/shard_map/ppermute | solution.py:322
  72.4 4.6 %collective-permute-start.4 = (bf16[32,6144]{1,0:T(8,128)(2,1)S(1)}, bf16[32,6144]{1,0:T(8,128)(2,1)S(1)}, u32[]{:S(2)}, u32[]{:S(2)}) collective-permute-start(bf16[32,6144]{1,0:T(8,128)(2,1)S(1)} %collective-permute-done.2.refs_1_.refs_2_), channel_id=1, source_target_pairs={{0,15},{1,0},{2,1},{3,2},{4,3},{5,4},{6,5},{7,6},{8,7},{9,8},{10,9... | collective-permute-start | bytes 1179656 | tf_op jit(solution)/shard_map/ppermute | solution.py:322
  77.7 4.9 %collective-permute-done.5.refs_0_.refs_3_ = bf16[32,6144]{1,0:T(8,128)(2,1)S(1)} collective-permute-done((bf16[32,6144]{1,0:T(8,128)(2,1)S(1)}, bf16[32,6144]{1,0:T(8,128)(2,1)S(1)}, u32[]{:S(2)}, u32[]{:S(2)}) %collective-permute-start.5) | collective-permute-done | bytes 393248 | tf_op jit(solution)/shard_map/ppermute | solution.py:322
  84.4 4.6 %collective-permute-start.6 = (bf16[32,6144]{1,0:T(8,128)(2,1)S(1)}, bf16[32,6144]{1,0:T(8,128)(2,1)S(1)}, u32[]{:S(2)}, u32[]{:S(2)}) collective-permute-start(bf16[32,6144]{1,0:T(8,128)(2,1)S(1)} %collective-permute-done.4.refs_1_.refs_4_), channel_id=1, source_target_pairs={{0,15},{1,0},{2,1},{3,2},{4,3},{5,4},{6,5},{7,6},{8,7},{9,8},{10,9... | collective-permute-start | bytes 1179656 | tf_op jit(solution)/shard_map/ppermute | solution.py:322
  89.7 2.2 %down.6.refs_5_ = f32[128,6144]{1,0:T(8,128)S(1)} custom-call(bf16[256,128]{1,0:T(8,128)(2,1)S(1)} %get-tuple-element.78.refs_0_, bf16[32,6144]{1,0:T(8,128)(2,1)S(1)} %collective-permute-done.3.refs_0_.refs_1_, bf16[32,6144]{1,0:T(8,128)(2,1)S(1)} %collective-permute-done.2.refs_1_.refs_2_, ...), custom_call_target="tpu_custom_call", output_to_operand_aliasing={{}: (5, {})} | custom-call | flops 402653184 | bytes 7864320 | tf_op jit(solution)/shard_map/down/pallas_call | solution.py:219
  95.6 4.6 %collective-permute-start.8 = (bf16[32,6144]{1,0:T(8,128)(2,1)S(1)}, bf16[32,6144]{1,0:T(8,128)(2,1)S(1)}, u32[]{:S(2)}, u32[]{:S(2)}) collective-permute-start(bf16[32,6144]{1,0:T(8,128)(2,1)S(1)} %collective-permute-done.6.refs_1_.refs_2_), channel_id=1, source_target_pairs={{0,15},{1,0},{2,1},{3,2},{4,3},{5,4},{6,5},{7,6},{8,7},{9,8},{10,9... | collective-permute-start | bytes 1179656 | tf_op jit(solution)/shard_map/ppermute | solution.py:322
  100.8 3.0 %collective-permute-done.9.refs_0_.refs_3_ = bf16[32,6144]{1,0:T(8,128)(2,1)S(1)} collective-permute-done((bf16[32,6144]{1,0:T(8,128)(2,1)S(1)}, bf16[32,6144]{1,0:T(8,128)(2,1)S(1)}, u32[]{:S(2)}, u32[]{:S(2)}) %collective-permute-start.9) | collective-permute-done | bytes 393248 | tf_op jit(solution)/shard_map/ppermute | solution.py:322
  105.8 4.6 %collective-permute-start.10 = (bf16[32,6144]{1,0:T(8,128)(2,1)S(1)}, bf16[32,6144]{1,0:T(8,128)(2,1)S(1)}, u32[]{:S(2)}, u32[]{:S(2)}) collective-permute-start(bf16[32,6144]{1,0:T(8,128)(2,1)S(1)} %collective-permute-done.8.refs_1_.refs_4_), channel_id=1, source_target_pairs={{0,15},{1,0},{2,1},{3,2},{4,3},{5,4},{6,5},{7,6},{8,7},{9,8},{10,9... | collective-permute-start | bytes 1179656 | tf_op jit(solution)/shard_map/ppermute | solution.py:322
  111.0 2.2 %down.7.refs_5_ = f32[128,6144]{1,0:T(8,128)S(1)} custom-call(bf16[256,128]{1,0:T(8,128)(2,1)S(1)} %get-tuple-element.89.refs_0_, bf16[32,6144]{1,0:T(8,128)(2,1)S(1)} %collective-permute-done.7.refs_0_.refs_1_, bf16[32,6144]{1,0:T(8,128)(2,1)S(1)} %collective-permute-done.6.refs_1_.refs_2_, ...), custom_call_target="tpu_custom_call", output_to_operand_aliasing={{}: (5, {})} | custom-call | flops 402653184 | bytes 7864320 | tf_op jit(solution)/shard_map/down/pallas_call | solution.py:219
  115.5 4.6 %collective-permute-start.12 = (bf16[32,6144]{1,0:T(8,128)(2,1)S(1)}, bf16[32,6144]{1,0:T(8,128)(2,1)S(1)}, u32[]{:S(2)}, u32[]{:S(2)}) collective-permute-start(bf16[32,6144]{1,0:T(8,128)(2,1)S(1)} %collective-permute-done.10.refs_1_.refs_2_), channel_id=1, source_target_pairs={{0,15},{1,0},{2,1},{3,2},{4,3},{5,4},{6,5},{7,6},{8,7},{9,8},{10,9... | collective-permute-start | bytes 1179656 | tf_op jit(solution)/shard_map/ppermute | solution.py:322
  120.7 2.5 %collective-permute-done.13.refs_0_.refs_3_ = bf16[32,6144]{1,0:T(8,128)(2,1)S(1)} collective-permute-done((bf16[32,6144]{1,0:T(8,128)(2,1)S(1)}, bf16[32,6144]{1,0:T(8,128)(2,1)S(1)}, u32[]{:S(2)}, u32[]{:S(2)}) %collective-permute-start.13) | collective-permute-done | bytes 393248 | tf_op jit(solution)/shard_map/ppermute | solution.py:322
  124.8 5.0 %collective-permute-start.15 = (bf16[16,6144]{1,0:T(8,128)(2,1)S(1)}, bf16[16,6144]{1,0:T(8,128)(2,1)S(1)}, u32[]{:S(2)}, u32[]{:S(2)}) collective-permute-start(bf16[16,6144]{1,0:T(8,128)(2,1)S(1)} %slice.8), channel_id=1, source_target_pairs={{0,15},{1,0},{2,1},{3,2},{4,3},{5,4},{6,5},{7,6},{8,7},{9,8},{10,9... | collective-permute-start | bytes 589832 | tf_op jit(solution)/shard_map/ppermute | solution.py:322
  129.8 1.9 %collective-permute-start.14 = (bf16[16,6144]{1,0:T(8,128)(2,1)S(1)}, bf16[16,6144]{1,0:T(8,128)(2,1)S(1)}, u32[]{:S(2)}, u32[]{:S(2)}) collective-permute-start(bf16[16,6144]{1,0:T(8,128)(2,1)S(1)} %slice.9), channel_id=1, source_target_pairs={{0,1},{1,2},{2,3},{3,4},{4,5},{5,6},{6,7},{7,8},{8,9},{9,10},{10,1... | collective-permute-start | bytes 589832 | tf_op jit(solution)/shard_map/ppermute | solution.py:322
  132.4 2.2 %down.8.refs_3_ = f32[128,6144]{1,0:T(8,128)S(1)} custom-call(bf16[256,128]{1,0:T(8,128)(2,1)S(1)} %get-tuple-element.100.refs_0_, bf16[32,6144]{1,0:T(8,128)(2,1)S(1)} %collective-permute-done.11.refs_0_.refs_1_, bf16[32,6144]{1,0:T(8,128)(2,1)S(1)} %collective-permute-done.10.refs_1_.refs_2_, ...), custom_call_target="tpu_custom_call", output_to_operand_aliasing={{}: (5, {})} | custom-call | flops 402653184 | bytes 7864320 | tf_op jit(solution)/shard_map/down/pallas_call | solution.py:219
  139.8 3.6 %all-to-all-start.1 = ((f32[16,1,64]{2,1,0:T(1,128)}), f32[16,1,64]{2,1,0:T(1,128)S(1)}, u32[]{:S(2)}, u32[]{:S(2)}) async-start(f32[16,1,64]{2,1,0:T(1,128)} %get-tuple-element.103), calls=%async_computation.1 | async-start | bytes 16384 | tf_op jit(solution)/shard_map/all_to_all | solution.py:331
  146.2 3.3 %down.9 = bf16[128,6144]{1,0:T(8,128)(2,1)} custom-call(bf16[64,128]{1,0:T(8,128)(2,1)S(1)} %get-tuple-element.104.refs_0_, bf16[16,6144]{1,0:T(8,128)(2,1)S(1)} %collective-permute-done.14.refs_0_.refs_1_, bf16[16,6144]{1,0:T(8,128)(2,1)S(1)} %collective-permute-done.15.refs_1_.refs_2_, f32[128,6144]{1,0:T(8,128)S(1)} %copy-done.2), custom_call_target="tpu_custom_call" | custom-call | flops 100663296 | bytes 6684672 | tf_op jit(solution)/shard_map/down/pallas_call | solution.py:219
  149.5 5.2 %all-to-all-done.1.got_ref = f32[16,1,64]{2,1,0:T(1,128)S(1)} async-done(((f32[16,1,64]{2,1,0:T(1,128)}), f32[16,1,64]{2,1,0:T(1,128)S(1)}, u32[]{:S(2)}, u32[]{:S(2)}) %all-to-all-start.1) | async-done | bytes 4128 | tf_op jit(solution)/shard_map/all_to_all | solution.py:331
  156.6 25.8 %all_to_all.16.table_ref = f32[64,1,64]{2,1,0:T(1,128)S(1)} all-to-all(f32[64,1,64]{2,1,0:T(1,128)} %total.1), channel_id=1, replica_groups=mesh['node'=64,'local'=16] {'node'}, dimensions={0} | all-to-all | bytes 32768 | tf_op jit(solution)/shard_map/all_to_all | solution.py:335
  (52 shorter events, 37.9 us)
Async XLA Ops:
  0.6 53.0 %copy-start = (bf16[2,64,6144]{2,1,0:T(8,128)(2,1)S(1)}, bf16[2,64,6144]{2,1,0:T(8,128)(2,1)}, u32[]{:S(2)}) copy-start(bf16[2,64,6144]{2,1,0:T(8,128)(2,1)} %param.10) | copy-start | bytes 4718596
  1.7 0.7 copy-start.3
  36.4 21.1 %collective-permute-start.1 = (bf16[32,6144]{1,0:T(8,128)(2,1)S(1)}, bf16[32,6144]{1,0:T(8,128)(2,1)S(1)}, u32[]{:S(2)}, u32[]{:S(2)}) collective-permute-start(bf16[32,6144]{1,0:T(8,128)(2,1)S(1)} %unpack.1.refs_0_.refs_1_), channel_id=1, source_target_pairs={{0,1},{1,2},{2,3},{3,4},{4,5},{5,6},{6,7},{7,8},{8,9},{9,10},{10,1... | collective-permute-start | bytes 1179656 | tf_op jit(solution)/shard_map/ppermute | solution.py:322
  38.3 21.1 %collective-permute-start = (bf16[32,6144]{1,0:T(8,128)(2,1)S(1)}, bf16[32,6144]{1,0:T(8,128)(2,1)S(1)}, u32[]{:S(2)}, u32[]{:S(2)}) collective-permute-start(bf16[32,6144]{1,0:T(8,128)(2,1)S(1)} %unpack.1.refs_0_.refs_1_), channel_id=1, source_target_pairs={{0,15},{1,0},{2,1},{3,2},{4,3},{5,4},{6,5},{7,6},{8,7},{9,8},{10,9... | collective-permute-start | bytes 1179656 | tf_op jit(solution)/shard_map/ppermute | solution.py:322
  57.5 13.0 %collective-permute-start.3 = (bf16[32,6144]{1,0:T(8,128)(2,1)S(1)}, bf16[32,6144]{1,0:T(8,128)(2,1)S(1)}, u32[]{:S(2)}, u32[]{:S(2)}) collective-permute-start(bf16[32,6144]{1,0:T(8,128)(2,1)S(1)} %collective-permute-done.1.refs_0_.refs_2_), channel_id=1, source_target_pairs={{0,1},{1,2},{2,3},{3,4},{4,5},{5,6},{6,7},{7,8},{8,9},{9,10},{10,1... | collective-permute-start | bytes 1179656 | tf_op jit(solution)/shard_map/ppermute | solution.py:322
  59.4 13.0 %collective-permute-start.2 = (bf16[32,6144]{1,0:T(8,128)(2,1)S(1)}, bf16[32,6144]{1,0:T(8,128)(2,1)S(1)}, u32[]{:S(2)}, u32[]{:S(2)}) collective-permute-start(bf16[32,6144]{1,0:T(8,128)(2,1)S(1)} %collective-permute-done.refs_1_.refs_3_), channel_id=1, source_target_pairs={{0,15},{1,0},{2,1},{3,2},{4,3},{5,4},{6,5},{7,6},{8,7},{9,8},{10,9... | collective-permute-start | bytes 1179656 | tf_op jit(solution)/shard_map/ppermute | solution.py:322
  70.5 12.0 %collective-permute-start.5 = (bf16[32,6144]{1,0:T(8,128)(2,1)S(1)}, bf16[32,6144]{1,0:T(8,128)(2,1)S(1)}, u32[]{:S(2)}, u32[]{:S(2)}) collective-permute-start(bf16[32,6144]{1,0:T(8,128)(2,1)S(1)} %collective-permute-done.3.refs_0_.refs_1_), channel_id=1, source_target_pairs={{0,1},{1,2},{2,3},{3,4},{4,5},{5,6},{6,7},{7,8},{8,9},{9,10},{10,1... | collective-permute-start | bytes 1179656 | tf_op jit(solution)/shard_map/ppermute | solution.py:322
  72.4 12.0 %collective-permute-start.4 = (bf16[32,6144]{1,0:T(8,128)(2,1)S(1)}, bf16[32,6144]{1,0:T(8,128)(2,1)S(1)}, u32[]{:S(2)}, u32[]{:S(2)}) collective-permute-start(bf16[32,6144]{1,0:T(8,128)(2,1)S(1)} %collective-permute-done.2.refs_1_.refs_2_), channel_id=1, source_target_pairs={{0,15},{1,0},{2,1},{3,2},{4,3},{5,4},{6,5},{7,6},{8,7},{9,8},{10,9... | collective-permute-start | bytes 1179656 | tf_op jit(solution)/shard_map/ppermute | solution.py:322
  82.5 11.1 %collective-permute-start.7 = (bf16[32,6144]{1,0:T(8,128)(2,1)S(1)}, bf16[32,6144]{1,0:T(8,128)(2,1)S(1)}, u32[]{:S(2)}, u32[]{:S(2)}) collective-permute-start(bf16[32,6144]{1,0:T(8,128)(2,1)S(1)} %collective-permute-done.5.refs_0_.refs_3_), channel_id=1, source_target_pairs={{0,1},{1,2},{2,3},{3,4},{4,5},{5,6},{6,7},{7,8},{8,9},{9,10},{10,1... | collective-permute-start | bytes 1179656 | tf_op jit(solution)/shard_map/ppermute | solution.py:322
  84.4 11.1 %collective-permute-start.6 = (bf16[32,6144]{1,0:T(8,128)(2,1)S(1)}, bf16[32,6144]{1,0:T(8,128)(2,1)S(1)}, u32[]{:S(2)}, u32[]{:S(2)}) collective-permute-start(bf16[32,6144]{1,0:T(8,128)(2,1)S(1)} %collective-permute-done.4.refs_1_.refs_4_), channel_id=1, source_target_pairs={{0,15},{1,0},{2,1},{3,2},{4,3},{5,4},{6,5},{7,6},{8,7},{9,8},{10,9... | collective-permute-start | bytes 1179656 | tf_op jit(solution)/shard_map/ppermute | solution.py:322
  93.6 10.2 %collective-permute-start.9 = (bf16[32,6144]{1,0:T(8,128)(2,1)S(1)}, bf16[32,6144]{1,0:T(8,128)(2,1)S(1)}, u32[]{:S(2)}, u32[]{:S(2)}) collective-permute-start(bf16[32,6144]{1,0:T(8,128)(2,1)S(1)} %collective-permute-done.7.refs_0_.refs_1_), channel_id=1, source_target_pairs={{0,1},{1,2},{2,3},{3,4},{4,5},{5,6},{6,7},{7,8},{8,9},{9,10},{10,1... | collective-permute-start | bytes 1179656 | tf_op jit(solution)/shard_map/ppermute | solution.py:322
  95.6 10.2 %collective-permute-start.8 = (bf16[32,6144]{1,0:T(8,128)(2,1)S(1)}, bf16[32,6144]{1,0:T(8,128)(2,1)S(1)}, u32[]{:S(2)}, u32[]{:S(2)}) collective-permute-start(bf16[32,6144]{1,0:T(8,128)(2,1)S(1)} %collective-permute-done.6.refs_1_.refs_2_), channel_id=1, source_target_pairs={{0,15},{1,0},{2,1},{3,2},{4,3},{5,4},{6,5},{7,6},{8,7},{9,8},{10,9... | collective-permute-start | bytes 1179656 | tf_op jit(solution)/shard_map/ppermute | solution.py:322
  103.8 9.7 %collective-permute-start.11 = (bf16[32,6144]{1,0:T(8,128)(2,1)S(1)}, bf16[32,6144]{1,0:T(8,128)(2,1)S(1)}, u32[]{:S(2)}, u32[]{:S(2)}) collective-permute-start(bf16[32,6144]{1,0:T(8,128)(2,1)S(1)} %collective-permute-done.9.refs_0_.refs_3_), channel_id=1, source_target_pairs={{0,1},{1,2},{2,3},{3,4},{4,5},{5,6},{6,7},{7,8},{8,9},{9,10},{10,1... | collective-permute-start | bytes 1179656 | tf_op jit(solution)/shard_map/ppermute | solution.py:322
  105.8 9.7 %collective-permute-start.10 = (bf16[32,6144]{1,0:T(8,128)(2,1)S(1)}, bf16[32,6144]{1,0:T(8,128)(2,1)S(1)}, u32[]{:S(2)}, u32[]{:S(2)}) collective-permute-start(bf16[32,6144]{1,0:T(8,128)(2,1)S(1)} %collective-permute-done.8.refs_1_.refs_4_), channel_id=1, source_target_pairs={{0,15},{1,0},{2,1},{3,2},{4,3},{5,4},{6,5},{7,6},{8,7},{9,8},{10,9... | collective-permute-start | bytes 1179656 | tf_op jit(solution)/shard_map/ppermute | solution.py:322
  113.5 9.7 %collective-permute-start.13 = (bf16[32,6144]{1,0:T(8,128)(2,1)S(1)}, bf16[32,6144]{1,0:T(8,128)(2,1)S(1)}, u32[]{:S(2)}, u32[]{:S(2)}) collective-permute-start(bf16[32,6144]{1,0:T(8,128)(2,1)S(1)} %collective-permute-done.11.refs_0_.refs_1_), channel_id=1, source_target_pairs={{0,1},{1,2},{2,3},{3,4},{4,5},{5,6},{6,7},{7,8},{8,9},{9,10},{10,1... | collective-permute-start | bytes 1179656 | tf_op jit(solution)/shard_map/ppermute | solution.py:322
  115.5 9.3 %collective-permute-start.12 = (bf16[32,6144]{1,0:T(8,128)(2,1)S(1)}, bf16[32,6144]{1,0:T(8,128)(2,1)S(1)}, u32[]{:S(2)}, u32[]{:S(2)}) collective-permute-start(bf16[32,6144]{1,0:T(8,128)(2,1)S(1)} %collective-permute-done.10.refs_1_.refs_2_), channel_id=1, source_target_pairs={{0,15},{1,0},{2,1},{3,2},{4,3},{5,4},{6,5},{7,6},{8,7},{9,8},{10,9... | collective-permute-start | bytes 1179656 | tf_op jit(solution)/shard_map/ppermute | solution.py:322
  124.8 11.4 %collective-permute-start.15 = (bf16[16,6144]{1,0:T(8,128)(2,1)S(1)}, bf16[16,6144]{1,0:T(8,128)(2,1)S(1)}, u32[]{:S(2)}, u32[]{:S(2)}) collective-permute-start(bf16[16,6144]{1,0:T(8,128)(2,1)S(1)} %slice.8), channel_id=1, source_target_pairs={{0,15},{1,0},{2,1},{3,2},{4,3},{5,4},{6,5},{7,6},{8,7},{9,8},{10,9... | collective-permute-start | bytes 589832 | tf_op jit(solution)/shard_map/ppermute | solution.py:322
  129.8 7.6 %collective-permute-start.14 = (bf16[16,6144]{1,0:T(8,128)(2,1)S(1)}, bf16[16,6144]{1,0:T(8,128)(2,1)S(1)}, u32[]{:S(2)}, u32[]{:S(2)}) collective-permute-start(bf16[16,6144]{1,0:T(8,128)(2,1)S(1)} %slice.9), channel_id=1, source_target_pairs={{0,1},{1,2},{2,3},{3,4},{4,5},{5,6},{6,7},{7,8},{8,9},{9,10},{10,1... | collective-permute-start | bytes 589832 | tf_op jit(solution)/shard_map/ppermute | solution.py:322
  134.6 1.6 copy-start.1
  138.1 44.3 %copy-start.4 = (s32[256,4]{0,1:T(4,128)S(1)}, s32[256,4]{0,1:T(4,128)}, u32[]{:S(2)}) copy-start(s32[256,4]{0,1:T(4,128)} %param.7) | copy-start | bytes 12292
  139.8 14.8 %all-to-all-start.1 = ((f32[16,1,64]{2,1,0:T(1,128)}), f32[16,1,64]{2,1,0:T(1,128)S(1)}, u32[]{:S(2)}, u32[]{:S(2)}) async-start(f32[16,1,64]{2,1,0:T(1,128)} %get-tuple-element.103), calls=%async_computation.1 | async-start | bytes 16384 | tf_op jit(solution)/shard_map/all_to_all | solution.py:331
  144.3 1.9 %copy-start.2 = (f32[128,6144]{1,0:T(8,128)S(1)}, f32[128,6144]{1,0:T(8,128)}, u32[]{:S(2)}) copy-start(f32[128,6144]{1,0:T(8,128)} %copy-done.1) | copy-start | bytes 9437188
  154.6 0.6 copy-start.5

commit v5 on v4

--- a/solution.py
+++ b/solution.py
@@ -312,20 +312,20 @@
 
     one, other = own_rows, own_rows
     for k in range(1, steps + 1):
-        if k == steps:
-            one, other = one[: cap // 2], other[cap // 2 :]
         if k == 2:
             one, *scaled = lax.optimization_barrier((one, *scaled))
         if k > 1:
             one, ups[-1], total = lax.optimization_barrier((one, ups[-1], total))
             other, ups[-1] = lax.optimization_barrier((other, ups[-1]))
-        one, other = lax.ppermute(one, "local", right), lax.ppermute(other, "local", left)
+        one = lax.ppermute(one, "local", right)
+        if k < steps:
+            other = lax.ppermute(other, "local", left)
         ups.append(up(blocks[-1], w))
         for at, group in enumerate(groups):
             if group[-1] == k - 1:
                 total = add(at, F32)
-        blocks.append([one, other])
-    blocks[-1][1], total = lax.optimization_barrier((blocks[-1][1], total))
+        blocks.append([one, other] if k < steps else [one])
+    blocks[-1][0], total = lax.optimization_barrier((blocks[-1][0], total))
     ups.append(up(blocks[-1], w))
     grad_h, part = close(shards, ups, saved, gate)
     got = lax.all_to_all(part, "local", split_axis=0, concat_axis=0, tiled=True)

time: 184 us -> 179 us (0.973)
  starting transfers between devices: 63.2 us -> 58.5 us
    ppermute x16 -> x15, starting transfers between devices: 59.6 us -> 54.6 us  [the longest x7 39.3 us: per_device(): other = lax.ppermute(other, 'local', left)]
    all_to_all x1, blocking collectives: 25.8 us -> 23.9 us  [per_device(): lax.all_to_all(total_for(got, nodes), 'node', split_axis=0, concat_axis=0...]
    ppermute x16 -> x15, waiting for transfers between devices: 22.4 us -> 23.5 us  [the longest x8 23.5 us: per_device(): one = lax.ppermute(one, 'local', right)]
  transfers between devices with their start and end apart: 17 -> 16, of which waited for: 10 -> 9; matrix products, arithmetic and copies ran while one was open for 2% -> 2% of each run, Pallas kernels for 10% -> 10%
where the time goes in v5:
time: 179 us; the launch traced here: 178 us
  starting transfers between devices  58.5 us (33%)
  blocking collectives  56.5 us (32%)
  waiting for transfers between devices  28.7 us (16%)
  Pallas kernels  23.3 us (13%)
  local copies, waits for them, and re-layouts  9.31 us (5%)
    ppermute x7, starting transfers between devices, per_device(): other = lax.ppermute(other, 'local', left)  39.3 us
    all_to_all x1, blocking collectives, per_device(): lax.all_to_all(packed, 'node', split_axis=0, concat_axis=0, tiled=True)  32.6 us
    all_to_all x1, blocking collectives, per_device(): lax.all_to_all(total_for(got, nodes), 'node', split_axis=0, concat_axis=0...  23.9 us
    ppermute x8, waiting for transfers between devices, per_device(): one = lax.ppermute(one, 'local', right)  23.5 us
    ppermute x8, starting transfers between devices, per_device(): one = lax.ppermute(one, 'local', right)  15.3 us
    pallas_call x5, Pallas kernels, down(): pl.pallas_call(lambda *refs: down_kernel(len(blocks), *refs), grid=(width...  11.6 us
    unnamed x14, local copies, waits for them, and re-layouts  6.72 us
    pallas_call x9, Pallas kernels, up(): pl.pallas_call(up_kernel, out_shape=jax.ShapeDtypeStruct((slots, units),...  5.91 us
  transfers between devices with their start and end apart: 16, of which 9 were waited for; matrix products, arithmetic and copies ran while one was open for 2% of the time, Pallas kernels for 10%

profile of v5, /device:TPU:1, one launch (start us, length us, event | category | flops | bytes accessed | tf_op | source)
XLA Modules:
  0.0 178.0 jit_solution(1345947929481508199)
XLA Ops:
  3.3 32.6 %all_to_all.15.got_ref = bf16[64,8,384]{2,1,0:T(8,128)(2,1)S(1)} all-to-all(bf16[64,8,384]{2,1,0:T(8,128)(2,1)S(1)} %get-tuple-element.56), channel_id=1, replica_groups=mesh['node'=64,'local'=16] {'node'}, dimensions={0} | all-to-all | bytes 786432 | tf_op jit(solution)/shard_map/all_to_all | solution.py:298
  36.4 1.9 %collective-permute-start.1 = (bf16[32,6144]{1,0:T(8,128)(2,1)S(1)}, bf16[32,6144]{1,0:T(8,128)(2,1)S(1)}, u32[]{:S(2)}, u32[]{:S(2)}) collective-permute-start(bf16[32,6144]{1,0:T(8,128)(2,1)S(1)} %unpack.1.refs_0_.refs_1_), channel_id=1, source_target_pairs={{0,1},{1,2},{2,3},{3,4},{4,5},{5,6},{6,7},{7,8},{8,9},{9,10},{10,1... | collective-permute-start | bytes 1179656 | tf_op jit(solution)/shard_map/ppermute | solution.py:320
  38.3 11.9 %collective-permute-start = (bf16[32,6144]{1,0:T(8,128)(2,1)S(1)}, bf16[32,6144]{1,0:T(8,128)(2,1)S(1)}, u32[]{:S(2)}, u32[]{:S(2)}) collective-permute-start(bf16[32,6144]{1,0:T(8,128)(2,1)S(1)} %unpack.1.refs_0_.refs_1_), channel_id=1, source_target_pairs={{0,15},{1,0},{2,1},{3,2},{4,3},{5,4},{6,5},{7,6},{8,7},{9,8},{10,9... | collective-permute-start | bytes 1179656 | tf_op jit(solution)/shard_map/ppermute | solution.py:322
  54.3 3.2 %collective-permute-done.1.refs_0_.refs_2_ = bf16[32,6144]{1,0:T(8,128)(2,1)S(1)} collective-permute-done((bf16[32,6144]{1,0:T(8,128)(2,1)S(1)}, bf16[32,6144]{1,0:T(8,128)(2,1)S(1)}, u32[]{:S(2)}, u32[]{:S(2)}) %collective-permute-start.1) | collective-permute-done | bytes 393248 | tf_op jit(solution)/shard_map/ppermute | solution.py:320
  57.5 1.9 %collective-permute-start.3 = (bf16[32,6144]{1,0:T(8,128)(2,1)S(1)}, bf16[32,6144]{1,0:T(8,128)(2,1)S(1)}, u32[]{:S(2)}, u32[]{:S(2)}) collective-permute-start(bf16[32,6144]{1,0:T(8,128)(2,1)S(1)} %collective-permute-done.1.refs_0_.refs_2_), channel_id=1, source_target_pairs={{0,1},{1,2},{2,3},{3,4},{4,5},{5,6},{6,7},{7,8},{8,9},{9,10},{10,1... | collective-permute-start | bytes 1179656 | tf_op jit(solution)/shard_map/ppermute | solution.py:320
  59.4 4.6 %collective-permute-start.2 = (bf16[32,6144]{1,0:T(8,128)(2,1)S(1)}, bf16[32,6144]{1,0:T(8,128)(2,1)S(1)}, u32[]{:S(2)}, u32[]{:S(2)}) collective-permute-start(bf16[32,6144]{1,0:T(8,128)(2,1)S(1)} %collective-permute-done.refs_1_.refs_3_), channel_id=1, source_target_pairs={{0,15},{1,0},{2,1},{3,2},{4,3},{5,4},{6,5},{7,6},{8,7},{9,8},{10,9... | collective-permute-start | bytes 1179656 | tf_op jit(solution)/shard_map/ppermute | solution.py:322
  66.5 3.9 %collective-permute-done.3.refs_0_.refs_1_ = bf16[32,6144]{1,0:T(8,128)(2,1)S(1)} collective-permute-done((bf16[32,6144]{1,0:T(8,128)(2,1)S(1)}, bf16[32,6144]{1,0:T(8,128)(2,1)S(1)}, u32[]{:S(2)}, u32[]{:S(2)}) %collective-permute-start.3) | collective-permute-done | bytes 393248 | tf_op jit(solution)/shard_map/ppermute | solution.py:320
  72.4 4.6 %collective-permute-start.4 = (bf16[32,6144]{1,0:T(8,128)(2,1)S(1)}, bf16[32,6144]{1,0:T(8,128)(2,1)S(1)}, u32[]{:S(2)}, u32[]{:S(2)}) collective-permute-start(bf16[32,6144]{1,0:T(8,128)(2,1)S(1)} %collective-permute-done.2.refs_1_.refs_2_), channel_id=1, source_target_pairs={{0,15},{1,0},{2,1},{3,2},{4,3},{5,4},{6,5},{7,6},{8,7},{9,8},{10,9... | collective-permute-start | bytes 1179656 | tf_op jit(solution)/shard_map/ppermute | solution.py:322
  77.7 4.9 %collective-permute-done.5.refs_0_.refs_3_ = bf16[32,6144]{1,0:T(8,128)(2,1)S(1)} collective-permute-done((bf16[32,6144]{1,0:T(8,128)(2,1)S(1)}, bf16[32,6144]{1,0:T(8,128)(2,1)S(1)}, u32[]{:S(2)}, u32[]{:S(2)}) %collective-permute-start.5) | collective-permute-done | bytes 393248 | tf_op jit(solution)/shard_map/ppermute | solution.py:320
  84.4 4.6 %collective-permute-start.6 = (bf16[32,6144]{1,0:T(8,128)(2,1)S(1)}, bf16[32,6144]{1,0:T(8,128)(2,1)S(1)}, u32[]{:S(2)}, u32[]{:S(2)}) collective-permute-start(bf16[32,6144]{1,0:T(8,128)(2,1)S(1)} %collective-permute-done.4.refs_1_.refs_4_), channel_id=1, source_target_pairs={{0,15},{1,0},{2,1},{3,2},{4,3},{5,4},{6,5},{7,6},{8,7},{9,8},{10,9... | collective-permute-start | bytes 1179656 | tf_op jit(solution)/shard_map/ppermute | solution.py:322
  89.7 2.2 %down.6.refs_5_ = f32[128,6144]{1,0:T(8,128)S(1)} custom-call(bf16[256,128]{1,0:T(8,128)(2,1)S(1)} %get-tuple-element.77.refs_0_, bf16[32,6144]{1,0:T(8,128)(2,1)S(1)} %collective-permute-done.3.refs_0_.refs_1_, bf16[32,6144]{1,0:T(8,128)(2,1)S(1)} %collective-permute-done.2.refs_1_.refs_2_, ...), custom_call_target="tpu_custom_call", output_to_operand_aliasing={{}: (5, {})} | custom-call | flops 402653184 | bytes 7864320 | tf_op jit(solution)/shard_map/down/pallas_call | solution.py:219
  93.6 1.9 %collective-permute-start.9 = (bf16[32,6144]{1,0:T(8,128)(2,1)S(1)}, bf16[32,6144]{1,0:T(8,128)(2,1)S(1)}, u32[]{:S(2)}, u32[]{:S(2)}) collective-permute-start(bf16[32,6144]{1,0:T(8,128)(2,1)S(1)} %collective-permute-done.7.refs_0_.refs_1_), channel_id=1, source_target_pairs={{0,1},{1,2},{2,3},{3,4},{4,5},{5,6},{6,7},{7,8},{8,9},{9,10},{10,1... | collective-permute-start | bytes 1179656 | tf_op jit(solution)/shard_map/ppermute | solution.py:320
  95.6 4.6 %collective-permute-start.8 = (bf16[32,6144]{1,0:T(8,128)(2,1)S(1)}, bf16[32,6144]{1,0:T(8,128)(2,1)S(1)}, u32[]{:S(2)}, u32[]{:S(2)}) collective-permute-start(bf16[32,6144]{1,0:T(8,128)(2,1)S(1)} %collective-permute-done.6.refs_1_.refs_2_), channel_id=1, source_target_pairs={{0,15},{1,0},{2,1},{3,2},{4,3},{5,4},{6,5},{7,6},{8,7},{9,8},{10,9... | collective-permute-start | bytes 1179656 | tf_op jit(solution)/shard_map/ppermute | solution.py:322
  100.8 3.0 %collective-permute-done.9.refs_0_.refs_3_ = bf16[32,6144]{1,0:T(8,128)(2,1)S(1)} collective-permute-done((bf16[32,6144]{1,0:T(8,128)(2,1)S(1)}, bf16[32,6144]{1,0:T(8,128)(2,1)S(1)}, u32[]{:S(2)}, u32[]{:S(2)}) %collective-permute-start.9) | collective-permute-done | bytes 393248 | tf_op jit(solution)/shard_map/ppermute | solution.py:320
  105.8 4.6 %collective-permute-start.10 = (bf16[32,6144]{1,0:T(8,128)(2,1)S(1)}, bf16[32,6144]{1,0:T(8,128)(2,1)S(1)}, u32[]{:S(2)}, u32[]{:S(2)}) collective-permute-start(bf16[32,6144]{1,0:T(8,128)(2,1)S(1)} %collective-permute-done.8.refs_1_.refs_4_), channel_id=1, source_target_pairs={{0,15},{1,0},{2,1},{3,2},{4,3},{5,4},{6,5},{7,6},{8,7},{9,8},{10,9... | collective-permute-start | bytes 1179656 | tf_op jit(solution)/shard_map/ppermute | solution.py:322
  111.0 2.2 %down.7.refs_5_ = f32[128,6144]{1,0:T(8,128)S(1)} custom-call(bf16[256,128]{1,0:T(8,128)(2,1)S(1)} %get-tuple-element.88.refs_0_, bf16[32,6144]{1,0:T(8,128)(2,1)S(1)} %collective-permute-done.7.refs_0_.refs_1_, bf16[32,6144]{1,0:T(8,128)(2,1)S(1)} %collective-permute-done.6.refs_1_.refs_2_, ...), custom_call_target="tpu_custom_call", output_to_operand_aliasing={{}: (5, {})} | custom-call | flops 402653184 | bytes 7864320 | tf_op jit(solution)/shard_map/down/pallas_call | solution.py:219
  115.5 4.6 %collective-permute-start.12 = (bf16[32,6144]{1,0:T(8,128)(2,1)S(1)}, bf16[32,6144]{1,0:T(8,128)(2,1)S(1)}, u32[]{:S(2)}, u32[]{:S(2)}) collective-permute-start(bf16[32,6144]{1,0:T(8,128)(2,1)S(1)} %collective-permute-done.10.refs_1_.refs_2_), channel_id=1, source_target_pairs={{0,15},{1,0},{2,1},{3,2},{4,3},{5,4},{6,5},{7,6},{8,7},{9,8},{10,9... | collective-permute-start | bytes 1179656 | tf_op jit(solution)/shard_map/ppermute | solution.py:322
  120.7 2.5 %collective-permute-done.13.refs_0_.refs_3_ = bf16[32,6144]{1,0:T(8,128)(2,1)S(1)} collective-permute-done((bf16[32,6144]{1,0:T(8,128)(2,1)S(1)}, bf16[32,6144]{1,0:T(8,128)(2,1)S(1)}, u32[]{:S(2)}, u32[]{:S(2)}) %collective-permute-start.13) | collective-permute-done | bytes 393248 | tf_op jit(solution)/shard_map/ppermute | solution.py:320
  125.9 2.2 %down.8.refs_2_ = f32[128,6144]{1,0:T(8,128)S(1)} custom-call(bf16[256,128]{1,0:T(8,128)(2,1)S(1)} %get-tuple-element.98.refs_0_, bf16[32,6144]{1,0:T(8,128)(2,1)S(1)} %collective-permute-done.11.refs_0_.refs_1_, bf16[32,6144]{1,0:T(8,128)(2,1)S(1)} %collective-permute-done.10.refs_1_.refs_2_, ...), custom_call_target="tpu_custom_call", output_to_operand_aliasing={{}: (5, {})} | custom-call | flops 402653184 | bytes 7864320 | tf_op jit(solution)/shard_map/down/pallas_call | solution.py:219
  129.7 3.8 %collective-permute-done.14.refs_0_.refs_1_ = bf16[32,6144]{1,0:T(8,128)(2,1)S(1)} collective-permute-done((bf16[32,6144]{1,0:T(8,128)(2,1)S(1)}, bf16[32,6144]{1,0:T(8,128)(2,1)S(1)}, u32[]{:S(2)}, u32[]{:S(2)}) %collective-permute-start.14) | collective-permute-done | bytes 393248 | tf_op jit(solution)/shard_map/ppermute | solution.py:320
  135.9 3.9 %all-to-all-start.1 = ((f32[16,1,64]{2,1,0:T(1,128)}), f32[16,1,64]{2,1,0:T(1,128)S(1)}, u32[]{:S(2)}, u32[]{:S(2)}) async-start(f32[16,1,64]{2,1,0:T(1,128)} %get-tuple-element.101), calls=%async_computation.1 | async-start | bytes 16384 | tf_op jit(solution)/shard_map/all_to_all | solution.py:331
  142.6 3.3 %down.9 = bf16[128,6144]{1,0:T(8,128)(2,1)} custom-call(bf16[64,128]{1,0:T(8,128)(2,1)S(1)} %get-tuple-element.102.refs_0_, bf16[32,6144]{1,0:T(8,128)(2,1)S(1)} %collective-permute-done.14.refs_0_.refs_1_, f32[128,6144]{1,0:T(8,128)S(1)} %copy-done.2), custom_call_target="tpu_custom_call" | custom-call | flops 100663296 | bytes 6684672 | tf_op jit(solution)/shard_map/down/pallas_call | solution.py:219
  145.9 5.2 %all-to-all-done.1.got_ref = f32[16,1,64]{2,1,0:T(1,128)S(1)} async-done(((f32[16,1,64]{2,1,0:T(1,128)}), f32[16,1,64]{2,1,0:T(1,128)S(1)}, u32[]{:S(2)}, u32[]{:S(2)}) %all-to-all-start.1) | async-done | bytes 4128 | tf_op jit(solution)/shard_map/all_to_all | solution.py:331
  153.0 23.9 %all_to_all.16.table_ref = f32[64,1,64]{2,1,0:T(1,128)S(1)} all-to-all(f32[64,1,64]{2,1,0:T(1,128)} %total.1), channel_id=1, replica_groups=mesh['node'=64,'local'=16] {'node'}, dimensions={0} | all-to-all | bytes 32768 | tf_op jit(solution)/shard_map/all_to_all | solution.py:335
  (48 shorter events, 35.1 us)
Async XLA Ops:
  0.6 53.0 %copy-start = (bf16[2,64,6144]{2,1,0:T(8,128)(2,1)S(1)}, bf16[2,64,6144]{2,1,0:T(8,128)(2,1)}, u32[]{:S(2)}) copy-start(bf16[2,64,6144]{2,1,0:T(8,128)(2,1)} %param.10) | copy-start | bytes 4718596
  1.7 0.7 copy-start.3
  36.4 21.1 %collective-permute-start.1 = (bf16[32,6144]{1,0:T(8,128)(2,1)S(1)}, bf16[32,6144]{1,0:T(8,128)(2,1)S(1)}, u32[]{:S(2)}, u32[]{:S(2)}) collective-permute-start(bf16[32,6144]{1,0:T(8,128)(2,1)S(1)} %unpack.1.refs_0_.refs_1_), channel_id=1, source_target_pairs={{0,1},{1,2},{2,3},{3,4},{4,5},{5,6},{6,7},{7,8},{8,9},{9,10},{10,1... | collective-permute-start | bytes 1179656 | tf_op jit(solution)/shard_map/ppermute | solution.py:320
  38.3 21.1 %collective-permute-start = (bf16[32,6144]{1,0:T(8,128)(2,1)S(1)}, bf16[32,6144]{1,0:T(8,128)(2,1)S(1)}, u32[]{:S(2)}, u32[]{:S(2)}) collective-permute-start(bf16[32,6144]{1,0:T(8,128)(2,1)S(1)} %unpack.1.refs_0_.refs_1_), channel_id=1, source_target_pairs={{0,15},{1,0},{2,1},{3,2},{4,3},{5,4},{6,5},{7,6},{8,7},{9,8},{10,9... | collective-permute-start | bytes 1179656 | tf_op jit(solution)/shard_map/ppermute | solution.py:322
  57.5 13.0 %collective-permute-start.3 = (bf16[32,6144]{1,0:T(8,128)(2,1)S(1)}, bf16[32,6144]{1,0:T(8,128)(2,1)S(1)}, u32[]{:S(2)}, u32[]{:S(2)}) collective-permute-start(bf16[32,6144]{1,0:T(8,128)(2,1)S(1)} %collective-permute-done.1.refs_0_.refs_2_), channel_id=1, source_target_pairs={{0,1},{1,2},{2,3},{3,4},{4,5},{5,6},{6,7},{7,8},{8,9},{9,10},{10,1... | collective-permute-start | bytes 1179656 | tf_op jit(solution)/shard_map/ppermute | solution.py:320
  59.4 13.0 %collective-permute-start.2 = (bf16[32,6144]{1,0:T(8,128)(2,1)S(1)}, bf16[32,6144]{1,0:T(8,128)(2,1)S(1)}, u32[]{:S(2)}, u32[]{:S(2)}) collective-permute-start(bf16[32,6144]{1,0:T(8,128)(2,1)S(1)} %collective-permute-done.refs_1_.refs_3_), channel_id=1, source_target_pairs={{0,15},{1,0},{2,1},{3,2},{4,3},{5,4},{6,5},{7,6},{8,7},{9,8},{10,9... | collective-permute-start | bytes 1179656 | tf_op jit(solution)/shard_map/ppermute | solution.py:322
  70.5 12.0 %collective-permute-start.5 = (bf16[32,6144]{1,0:T(8,128)(2,1)S(1)}, bf16[32,6144]{1,0:T(8,128)(2,1)S(1)}, u32[]{:S(2)}, u32[]{:S(2)}) collective-permute-start(bf16[32,6144]{1,0:T(8,128)(2,1)S(1)} %collective-permute-done.3.refs_0_.refs_1_), channel_id=1, source_target_pairs={{0,1},{1,2},{2,3},{3,4},{4,5},{5,6},{6,7},{7,8},{8,9},{9,10},{10,1... | collective-permute-start | bytes 1179656 | tf_op jit(solution)/shard_map/ppermute | solution.py:320
  72.4 12.0 %collective-permute-start.4 = (bf16[32,6144]{1,0:T(8,128)(2,1)S(1)}, bf16[32,6144]{1,0:T(8,128)(2,1)S(1)}, u32[]{:S(2)}, u32[]{:S(2)}) collective-permute-start(bf16[32,6144]{1,0:T(8,128)(2,1)S(1)} %collective-permute-done.2.refs_1_.refs_2_), channel_id=1, source_target_pairs={{0,15},{1,0},{2,1},{3,2},{4,3},{5,4},{6,5},{7,6},{8,7},{9,8},{10,9... | collective-permute-start | bytes 1179656 | tf_op jit(solution)/shard_map/ppermute | solution.py:322
  82.5 11.1 %collective-permute-start.7 = (bf16[32,6144]{1,0:T(8,128)(2,1)S(1)}, bf16[32,6144]{1,0:T(8,128)(2,1)S(1)}, u32[]{:S(2)}, u32[]{:S(2)}) collective-permute-start(bf16[32,6144]{1,0:T(8,128)(2,1)S(1)} %collective-permute-done.5.refs_0_.refs_3_), channel_id=1, source_target_pairs={{0,1},{1,2},{2,3},{3,4},{4,5},{5,6},{6,7},{7,8},{8,9},{9,10},{10,1... | collective-permute-start | bytes 1179656 | tf_op jit(solution)/shard_map/ppermute | solution.py:320
  84.4 11.1 %collective-permute-start.6 = (bf16[32,6144]{1,0:T(8,128)(2,1)S(1)}, bf16[32,6144]{1,0:T(8,128)(2,1)S(1)}, u32[]{:S(2)}, u32[]{:S(2)}) collective-permute-start(bf16[32,6144]{1,0:T(8,128)(2,1)S(1)} %collective-permute-done.4.refs_1_.refs_4_), channel_id=1, source_target_pairs={{0,15},{1,0},{2,1},{3,2},{4,3},{5,4},{6,5},{7,6},{8,7},{9,8},{10,9... | collective-permute-start | bytes 1179656 | tf_op jit(solution)/shard_map/ppermute | solution.py:322
  93.6 10.2 %collective-permute-start.9 = (bf16[32,6144]{1,0:T(8,128)(2,1)S(1)}, bf16[32,6144]{1,0:T(8,128)(2,1)S(1)}, u32[]{:S(2)}, u32[]{:S(2)}) collective-permute-start(bf16[32,6144]{1,0:T(8,128)(2,1)S(1)} %collective-permute-done.7.refs_0_.refs_1_), channel_id=1, source_target_pairs={{0,1},{1,2},{2,3},{3,4},{4,5},{5,6},{6,7},{7,8},{8,9},{9,10},{10,1... | collective-permute-start | bytes 1179656 | tf_op jit(solution)/shard_map/ppermute | solution.py:320
  95.6 10.2 %collective-permute-start.8 = (bf16[32,6144]{1,0:T(8,128)(2,1)S(1)}, bf16[32,6144]{1,0:T(8,128)(2,1)S(1)}, u32[]{:S(2)}, u32[]{:S(2)}) collective-permute-start(bf16[32,6144]{1,0:T(8,128)(2,1)S(1)} %collective-permute-done.6.refs_1_.refs_2_), channel_id=1, source_target_pairs={{0,15},{1,0},{2,1},{3,2},{4,3},{5,4},{6,5},{7,6},{8,7},{9,8},{10,9... | collective-permute-start | bytes 1179656 | tf_op jit(solution)/shard_map/ppermute | solution.py:322
  103.8 9.7 %collective-permute-start.11 = (bf16[32,6144]{1,0:T(8,128)(2,1)S(1)}, bf16[32,6144]{1,0:T(8,128)(2,1)S(1)}, u32[]{:S(2)}, u32[]{:S(2)}) collective-permute-start(bf16[32,6144]{1,0:T(8,128)(2,1)S(1)} %collective-permute-done.9.refs_0_.refs_3_), channel_id=1, source_target_pairs={{0,1},{1,2},{2,3},{3,4},{4,5},{5,6},{6,7},{7,8},{8,9},{9,10},{10,1... | collective-permute-start | bytes 1179656 | tf_op jit(solution)/shard_map/ppermute | solution.py:320
  105.8 9.7 %collective-permute-start.10 = (bf16[32,6144]{1,0:T(8,128)(2,1)S(1)}, bf16[32,6144]{1,0:T(8,128)(2,1)S(1)}, u32[]{:S(2)}, u32[]{:S(2)}) collective-permute-start(bf16[32,6144]{1,0:T(8,128)(2,1)S(1)} %collective-permute-done.8.refs_1_.refs_4_), channel_id=1, source_target_pairs={{0,15},{1,0},{2,1},{3,2},{4,3},{5,4},{6,5},{7,6},{8,7},{9,8},{10,9... | collective-permute-start | bytes 1179656 | tf_op jit(solution)/shard_map/ppermute | solution.py:322
  113.5 9.7 %collective-permute-start.13 = (bf16[32,6144]{1,0:T(8,128)(2,1)S(1)}, bf16[32,6144]{1,0:T(8,128)(2,1)S(1)}, u32[]{:S(2)}, u32[]{:S(2)}) collective-permute-start(bf16[32,6144]{1,0:T(8,128)(2,1)S(1)} %collective-permute-done.11.refs_0_.refs_1_), channel_id=1, source_target_pairs={{0,1},{1,2},{2,3},{3,4},{4,5},{5,6},{6,7},{7,8},{8,9},{9,10},{10,1... | collective-permute-start | bytes 1179656 | tf_op jit(solution)/shard_map/ppermute | solution.py:320
  115.5 9.7 %collective-permute-start.12 = (bf16[32,6144]{1,0:T(8,128)(2,1)S(1)}, bf16[32,6144]{1,0:T(8,128)(2,1)S(1)}, u32[]{:S(2)}, u32[]{:S(2)}) collective-permute-start(bf16[32,6144]{1,0:T(8,128)(2,1)S(1)} %collective-permute-done.10.refs_1_.refs_2_), channel_id=1, source_target_pairs={{0,15},{1,0},{2,1},{3,2},{4,3},{5,4},{6,5},{7,6},{8,7},{9,8},{10,9... | collective-permute-start | bytes 1179656 | tf_op jit(solution)/shard_map/ppermute | solution.py:322
  123.3 10.2 %collective-permute-start.14 = (bf16[32,6144]{1,0:T(8,128)(2,1)S(1)}, bf16[32,6144]{1,0:T(8,128)(2,1)S(1)}, u32[]{:S(2)}, u32[]{:S(2)}) collective-permute-start(bf16[32,6144]{1,0:T(8,128)(2,1)S(1)} %collective-permute-done.13.refs_0_.refs_3_), channel_id=1, source_target_pairs={{0,1},{1,2},{2,3},{3,4},{4,5},{5,6},{6,7},{7,8},{8,9},{9,10},{10,1... | collective-permute-start | bytes 1179656 | tf_op jit(solution)/shard_map/ppermute | solution.py:320
  128.0 1.6 copy-start.1
  134.1 42.8 %copy-start.4 = (s32[256,4]{0,1:T(4,128)S(1)}, s32[256,4]{0,1:T(4,128)}, u32[]{:S(2)}) copy-start(s32[256,4]{0,1:T(4,128)} %param.7) | copy-start | bytes 12292
  135.9 15.2 %all-to-all-start.1 = ((f32[16,1,64]{2,1,0:T(1,128)}), f32[16,1,64]{2,1,0:T(1,128)S(1)}, u32[]{:S(2)}, u32[]{:S(2)}) async-start(f32[16,1,64]{2,1,0:T(1,128)} %get-tuple-element.101), calls=%async_computation.1 | async-start | bytes 16384 | tf_op jit(solution)/shard_map/all_to_all | solution.py:331
  140.7 1.9 %copy-start.2 = (f32[128,6144]{1,0:T(8,128)S(1)}, f32[128,6144]{1,0:T(8,128)}, u32[]{:S(2)}) copy-start(f32[128,6144]{1,0:T(8,128)} %copy-done.1) | copy-start | bytes 9437188
  151.1 0.6 copy-start.5

commit v6 on v5

--- a/solution.py
+++ b/solution.py
@@ -325,7 +325,7 @@
             if group[-1] == k - 1:
                 total = add(at, F32)
         blocks.append([one, other] if k < steps else [one])
-    blocks[-1][0], total = lax.optimization_barrier((blocks[-1][0], total))
+    ups[-1], total = lax.optimization_barrier((ups[-1], total))
     ups.append(up(blocks[-1], w))
     grad_h, part = close(shards, ups, saved, gate)
     got = lax.all_to_all(part, "local", split_axis=0, concat_axis=0, tiled=True)

time: 179 us -> 179 us (level)
  no operation moved by 1% of the time
where the time goes in v6:
time: 179 us; the launch traced here: 178 us
  starting transfers between devices  58.5 us (33%)
  blocking collectives  56.5 us (32%)
  waiting for transfers between devices  28.7 us (16%)
  Pallas kernels  23.3 us (13%)
  local copies, waits for them, and re-layouts  9.31 us (5%)
    ppermute x7, starting transfers between devices, per_device(): other = lax.ppermute(other, 'local', left)  39.3 us
    all_to_all x1, blocking collectives, per_device(): lax.all_to_all(packed, 'node', split_axis=0, concat_axis=0, tiled=True)  32.6 us
    all_to_all x1, blocking collectives, per_device(): lax.all_to_all(total_for(got, nodes), 'node', split_axis=0, concat_axis=0...  23.9 us
    ppermute x8, waiting for transfers between devices, per_device(): one = lax.ppermute(one, 'local', right)  23.5 us
    ppermute x8, starting transfers between devices, per_device(): one = lax.ppermute(one, 'local', right)  15.3 us
    pallas_call x5, Pallas kernels, down(): pl.pallas_call(lambda *refs: down_kernel(len(blocks), *refs), grid=(width...  11.6 us
    unnamed x14, local copies, waits for them, and re-layouts  6.72 us
    pallas_call x9, Pallas kernels, up(): pl.pallas_call(up_kernel, out_shape=jax.ShapeDtypeStruct((slots, units),...  5.91 us
  transfers between devices with their start and end apart: 16, of which 9 were waited for; matrix products, arithmetic and copies ran while one was open for 2% of the time, Pallas kernels for 10%

profile of v6, /device:TPU:1, one launch (start us, length us, event | category | flops | bytes accessed | tf_op | source)
XLA Modules:
  0.0 178.0 jit_solution(1345947929481508199)
XLA Ops:
  3.3 32.6 %all_to_all.15.got_ref = bf16[64,8,384]{2,1,0:T(8,128)(2,1)S(1)} all-to-all(bf16[64,8,384]{2,1,0:T(8,128)(2,1)S(1)} %get-tuple-element.56), channel_id=1, replica_groups=mesh['node'=64,'local'=16] {'node'}, dimensions={0} | all-to-all | bytes 786432 | tf_op jit(solution)/shard_map/all_to_all | solution.py:298
  36.4 1.9 %collective-permute-start.1 = (bf16[32,6144]{1,0:T(8,128)(2,1)S(1)}, bf16[32,6144]{1,0:T(8,128)(2,1)S(1)}, u32[]{:S(2)}, u32[]{:S(2)}) collective-permute-start(bf16[32,6144]{1,0:T(8,128)(2,1)S(1)} %unpack.1.refs_0_.refs_1_), channel_id=1, source_target_pairs={{0,1},{1,2},{2,3},{3,4},{4,5},{5,6},{6,7},{7,8},{8,9},{9,10},{10,1... | collective-permute-start | bytes 1179656 | tf_op jit(solution)/shard_map/ppermute | solution.py:320
  38.3 11.9 %collective-permute-start = (bf16[32,6144]{1,0:T(8,128)(2,1)S(1)}, bf16[32,6144]{1,0:T(8,128)(2,1)S(1)}, u32[]{:S(2)}, u32[]{:S(2)}) collective-permute-start(bf16[32,6144]{1,0:T(8,128)(2,1)S(1)} %unpack.1.refs_0_.refs_1_), channel_id=1, source_target_pairs={{0,15},{1,0},{2,1},{3,2},{4,3},{5,4},{6,5},{7,6},{8,7},{9,8},{10,9... | collective-permute-start | bytes 1179656 | tf_op jit(solution)/shard_map/ppermute | solution.py:322
  54.3 3.2 %collective-permute-done.1.refs_0_.refs_2_ = bf16[32,6144]{1,0:T(8,128)(2,1)S(1)} collective-permute-done((bf16[32,6144]{1,0:T(8,128)(2,1)S(1)}, bf16[32,6144]{1,0:T(8,128)(2,1)S(1)}, u32[]{:S(2)}, u32[]{:S(2)}) %collective-permute-start.1) | collective-permute-done | bytes 393248 | tf_op jit(solution)/shard_map/ppermute | solution.py:320
  57.5 1.9 %collective-permute-start.3 = (bf16[32,6144]{1,0:T(8,128)(2,1)S(1)}, bf16[32,6144]{1,0:T(8,128)(2,1)S(1)}, u32[]{:S(2)}, u32[]{:S(2)}) collective-permute-start(bf16[32,6144]{1,0:T(8,128)(2,1)S(1)} %collective-permute-done.1.refs_0_.refs_2_), channel_id=1, source_target_pairs={{0,1},{1,2},{2,3},{3,4},{4,5},{5,6},{6,7},{7,8},{8,9},{9,10},{10,1... | collective-permute-start | bytes 1179656 | tf_op jit(solution)/shard_map/ppermute | solution.py:320
  59.4 4.6 %collective-permute-start.2 = (bf16[32,6144]{1,0:T(8,128)(2,1)S(1)}, bf16[32,6144]{1,0:T(8,128)(2,1)S(1)}, u32[]{:S(2)}, u32[]{:S(2)}) collective-permute-start(bf16[32,6144]{1,0:T(8,128)(2,1)S(1)} %collective-permute-done.refs_1_.refs_3_), channel_id=1, source_target_pairs={{0,15},{1,0},{2,1},{3,2},{4,3},{5,4},{6,5},{7,6},{8,7},{9,8},{10,9... | collective-permute-start | bytes 1179656 | tf_op jit(solution)/shard_map/ppermute | solution.py:322
  66.5 3.9 %collective-permute-done.3.refs_0_.refs_1_ = bf16[32,6144]{1,0:T(8,128)(2,1)S(1)} collective-permute-done((bf16[32,6144]{1,0:T(8,128)(2,1)S(1)}, bf16[32,6144]{1,0:T(8,128)(2,1)S(1)}, u32[]{:S(2)}, u32[]{:S(2)}) %collective-permute-start.3) | collective-permute-done | bytes 393248 | tf_op jit(solution)/shard_map/ppermute | solution.py:320
  72.4 4.6 %collective-permute-start.4 = (bf16[32,6144]{1,0:T(8,128)(2,1)S(1)}, bf16[32,6144]{1,0:T(8,128)(2,1)S(1)}, u32[]{:S(2)}, u32[]{:S(2)}) collective-permute-start(bf16[32,6144]{1,0:T(8,128)(2,1)S(1)} %collective-permute-done.2.refs_1_.refs_2_), channel_id=1, source_target_pairs={{0,15},{1,0},{2,1},{3,2},{4,3},{5,4},{6,5},{7,6},{8,7},{9,8},{10,9... | collective-permute-start | bytes 1179656 | tf_op jit(solution)/shard_map/ppermute | solution.py:322
  77.7 4.9 %collective-permute-done.5.refs_0_.refs_3_ = bf16[32,6144]{1,0:T(8,128)(2,1)S(1)} collective-permute-done((bf16[32,6144]{1,0:T(8,128)(2,1)S(1)}, bf16[32,6144]{1,0:T(8,128)(2,1)S(1)}, u32[]{:S(2)}, u32[]{:S(2)}) %collective-permute-start.5) | collective-permute-done | bytes 393248 | tf_op jit(solution)/shard_map/ppermute | solution.py:320
  84.4 4.6 %collective-permute-start.6 = (bf16[32,6144]{1,0:T(8,128)(2,1)S(1)}, bf16[32,6144]{1,0:T(8,128)(2,1)S(1)}, u32[]{:S(2)}, u32[]{:S(2)}) collective-permute-start(bf16[32,6144]{1,0:T(8,128)(2,1)S(1)} %collective-permute-done.4.refs_1_.refs_4_), channel_id=1, source_target_pairs={{0,15},{1,0},{2,1},{3,2},{4,3},{5,4},{6,5},{7,6},{8,7},{9,8},{10,9... | collective-permute-start | bytes 1179656 | tf_op jit(solution)/shard_map/ppermute | solution.py:322
  89.7 2.2 %down.6.refs_5_ = f32[128,6144]{1,0:T(8,128)S(1)} custom-call(bf16[256,128]{1,0:T(8,128)(2,1)S(1)} %get-tuple-element.77.refs_0_, bf16[32,6144]{1,0:T(8,128)(2,1)S(1)} %collective-permute-done.3.refs_0_.refs_1_, bf16[32,6144]{1,0:T(8,128)(2,1)S(1)} %collective-permute-done.2.refs_1_.refs_2_, ...), custom_call_target="tpu_custom_call", output_to_operand_aliasing={{}: (5, {})} | custom-call | flops 402653184 | bytes 7864320 | tf_op jit(solution)/shard_map/down/pallas_call | solution.py:219
  93.6 1.9 %collective-permute-start.9 = (bf16[32,6144]{1,0:T(8,128)(2,1)S(1)}, bf16[32,6144]{1,0:T(8,128)(2,1)S(1)}, u32[]{:S(2)}, u32[]{:S(2)}) collective-permute-start(bf16[32,6144]{1,0:T(8,128)(2,1)S(1)} %collective-permute-done.7.refs_0_.refs_1_), channel_id=1, source_target_pairs={{0,1},{1,2},{2,3},{3,4},{4,5},{5,6},{6,7},{7,8},{8,9},{9,10},{10,1... | collective-permute-start | bytes 1179656 | tf_op jit(solution)/shard_map/ppermute | solution.py:320
  95.6 4.6 %collective-permute-start.8 = (bf16[32,6144]{1,0:T(8,128)(2,1)S(1)}, bf16[32,6144]{1,0:T(8,128)(2,1)S(1)}, u32[]{:S(2)}, u32[]{:S(2)}) collective-permute-start(bf16[32,6144]{1,0:T(8,128)(2,1)S(1)} %collective-permute-done.6.refs_1_.refs_2_), channel_id=1, source_target_pairs={{0,15},{1,0},{2,1},{3,2},{4,3},{5,4},{6,5},{7,6},{8,7},{9,8},{10,9... | collective-permute-start | bytes 1179656 | tf_op jit(solution)/shard_map/ppermute | solution.py:322
  100.8 3.0 %collective-permute-done.9.refs_0_.refs_3_ = bf16[32,6144]{1,0:T(8,128)(2,1)S(1)} collective-permute-done((bf16[32,6144]{1,0:T(8,128)(2,1)S(1)}, bf16[32,6144]{1,0:T(8,128)(2,1)S(1)}, u32[]{:S(2)}, u32[]{:S(2)}) %collective-permute-start.9) | collective-permute-done | bytes 393248 | tf_op jit(solution)/shard_map/ppermute | solution.py:320
  105.8 4.6 %collective-permute-start.10 = (bf16[32,6144]{1,0:T(8,128)(2,1)S(1)}, bf16[32,6144]{1,0:T(8,128)(2,1)S(1)}, u32[]{:S(2)}, u32[]{:S(2)}) collective-permute-start(bf16[32,6144]{1,0:T(8,128)(2,1)S(1)} %collective-permute-done.8.refs_1_.refs_4_), channel_id=1, source_target_pairs={{0,15},{1,0},{2,1},{3,2},{4,3},{5,4},{6,5},{7,6},{8,7},{9,8},{10,9... | collective-permute-start | bytes 1179656 | tf_op jit(solution)/shard_map/ppermute | solution.py:322
  111.0 2.2 %down.7.refs_5_ = f32[128,6144]{1,0:T(8,128)S(1)} custom-call(bf16[256,128]{1,0:T(8,128)(2,1)S(1)} %get-tuple-element.88.refs_0_, bf16[32,6144]{1,0:T(8,128)(2,1)S(1)} %collective-permute-done.7.refs_0_.refs_1_, bf16[32,6144]{1,0:T(8,128)(2,1)S(1)} %collective-permute-done.6.refs_1_.refs_2_, ...), custom_call_target="tpu_custom_call", output_to_operand_aliasing={{}: (5, {})} | custom-call | flops 402653184 | bytes 7864320 | tf_op jit(solution)/shard_map/down/pallas_call | solution.py:219
  115.5 4.6 %collective-permute-start.12 = (bf16[32,6144]{1,0:T(8,128)(2,1)S(1)}, bf16[32,6144]{1,0:T(8,128)(2,1)S(1)}, u32[]{:S(2)}, u32[]{:S(2)}) collective-permute-start(bf16[32,6144]{1,0:T(8,128)(2,1)S(1)} %collective-permute-done.10.refs_1_.refs_2_), channel_id=1, source_target_pairs={{0,15},{1,0},{2,1},{3,2},{4,3},{5,4},{6,5},{7,6},{8,7},{9,8},{10,9... | collective-permute-start | bytes 1179656 | tf_op jit(solution)/shard_map/ppermute | solution.py:322
  120.7 2.5 %collective-permute-done.13.refs_0_.refs_3_ = bf16[32,6144]{1,0:T(8,128)(2,1)S(1)} collective-permute-done((bf16[32,6144]{1,0:T(8,128)(2,1)S(1)}, bf16[32,6144]{1,0:T(8,128)(2,1)S(1)}, u32[]{:S(2)}, u32[]{:S(2)}) %collective-permute-start.13) | collective-permute-done | bytes 393248 | tf_op jit(solution)/shard_map/ppermute | solution.py:320
  125.9 2.2 %down.8.refs_2_ = f32[128,6144]{1,0:T(8,128)S(1)} custom-call(bf16[256,128]{1,0:T(8,128)(2,1)S(1)} %get-tuple-element.97.refs_0_, bf16[32,6144]{1,0:T(8,128)(2,1)S(1)} %collective-permute-done.11.refs_0_.refs_1_, bf16[32,6144]{1,0:T(8,128)(2,1)S(1)} %collective-permute-done.10.refs_1_.refs_2_, ...), custom_call_target="tpu_custom_call", output_to_operand_aliasing={{}: (5, {})} | custom-call | flops 402653184 | bytes 7864320 | tf_op jit(solution)/shard_map/down/pallas_call | solution.py:219
  129.7 3.8 %collective-permute-done.14.refs_0_.refs_1_ = bf16[32,6144]{1,0:T(8,128)(2,1)S(1)} collective-permute-done((bf16[32,6144]{1,0:T(8,128)(2,1)S(1)}, bf16[32,6144]{1,0:T(8,128)(2,1)S(1)}, u32[]{:S(2)}, u32[]{:S(2)}) %collective-permute-start.14) | collective-permute-done | bytes 393248 | tf_op jit(solution)/shard_map/ppermute | solution.py:320
  135.9 3.9 %all-to-all-start.1 = ((f32[16,1,64]{2,1,0:T(1,128)}), f32[16,1,64]{2,1,0:T(1,128)S(1)}, u32[]{:S(2)}, u32[]{:S(2)}) async-start(f32[16,1,64]{2,1,0:T(1,128)} %get-tuple-element.101), calls=%async_computation.1 | async-start | bytes 16384 | tf_op jit(solution)/shard_map/all_to_all | solution.py:331
  142.6 3.3 %down.9 = bf16[128,6144]{1,0:T(8,128)(2,1)} custom-call(bf16[64,128]{1,0:T(8,128)(2,1)S(1)} %get-tuple-element.102.refs_0_, bf16[32,6144]{1,0:T(8,128)(2,1)S(1)} %collective-permute-done.14.refs_0_.refs_1_, f32[128,6144]{1,0:T(8,128)S(1)} %copy-done.2), custom_call_target="tpu_custom_call" | custom-call | flops 100663296 | bytes 6684672 | tf_op jit(solution)/shard_map/down/pallas_call | solution.py:219
  145.9 5.2 %all-to-all-done.1.got_ref = f32[16,1,64]{2,1,0:T(1,128)S(1)} async-done(((f32[16,1,64]{2,1,0:T(1,128)}), f32[16,1,64]{2,1,0:T(1,128)S(1)}, u32[]{:S(2)}, u32[]{:S(2)}) %all-to-all-start.1) | async-done | bytes 4128 | tf_op jit(solution)/shard_map/all_to_all | solution.py:331
  153.0 23.9 %all_to_all.16.table_ref = f32[64,1,64]{2,1,0:T(1,128)S(1)} all-to-all(f32[64,1,64]{2,1,0:T(1,128)} %total.1), channel_id=1, replica_groups=mesh['node'=64,'local'=16] {'node'}, dimensions={0} | all-to-all | bytes 32768 | tf_op jit(solution)/shard_map/all_to_all | solution.py:335
  (48 shorter events, 35.1 us)
Async XLA Ops:
  0.6 53.0 %copy-start = (bf16[2,64,6144]{2,1,0:T(8,128)(2,1)S(1)}, bf16[2,64,6144]{2,1,0:T(8,128)(2,1)}, u32[]{:S(2)}) copy-start(bf16[2,64,6144]{2,1,0:T(8,128)(2,1)} %param.10) | copy-start | bytes 4718596
  1.7 0.7 copy-start.3
  36.4 21.1 %collective-permute-start.1 = (bf16[32,6144]{1,0:T(8,128)(2,1)S(1)}, bf16[32,6144]{1,0:T(8,128)(2,1)S(1)}, u32[]{:S(2)}, u32[]{:S(2)}) collective-permute-start(bf16[32,6144]{1,0:T(8,128)(2,1)S(1)} %unpack.1.refs_0_.refs_1_), channel_id=1, source_target_pairs={{0,1},{1,2},{2,3},{3,4},{4,5},{5,6},{6,7},{7,8},{8,9},{9,10},{10,1... | collective-permute-start | bytes 1179656 | tf_op jit(solution)/shard_map/ppermute | solution.py:320
  38.3 21.1 %collective-permute-start = (bf16[32,6144]{1,0:T(8,128)(2,1)S(1)}, bf16[32,6144]{1,0:T(8,128)(2,1)S(1)}, u32[]{:S(2)}, u32[]{:S(2)}) collective-permute-start(bf16[32,6144]{1,0:T(8,128)(2,1)S(1)} %unpack.1.refs_0_.refs_1_), channel_id=1, source_target_pairs={{0,15},{1,0},{2,1},{3,2},{4,3},{5,4},{6,5},{7,6},{8,7},{9,8},{10,9... | collective-permute-start | bytes 1179656 | tf_op jit(solution)/shard_map/ppermute | solution.py:322
  57.5 13.0 %collective-permute-start.3 = (bf16[32,6144]{1,0:T(8,128)(2,1)S(1)}, bf16[32,6144]{1,0:T(8,128)(2,1)S(1)}, u32[]{:S(2)}, u32[]{:S(2)}) collective-permute-start(bf16[32,6144]{1,0:T(8,128)(2,1)S(1)} %collective-permute-done.1.refs_0_.refs_2_), channel_id=1, source_target_pairs={{0,1},{1,2},{2,3},{3,4},{4,5},{5,6},{6,7},{7,8},{8,9},{9,10},{10,1... | collective-permute-start | bytes 1179656 | tf_op jit(solution)/shard_map/ppermute | solution.py:320
  59.4 13.0 %collective-permute-start.2 = (bf16[32,6144]{1,0:T(8,128)(2,1)S(1)}, bf16[32,6144]{1,0:T(8,128)(2,1)S(1)}, u32[]{:S(2)}, u32[]{:S(2)}) collective-permute-start(bf16[32,6144]{1,0:T(8,128)(2,1)S(1)} %collective-permute-done.refs_1_.refs_3_), channel_id=1, source_target_pairs={{0,15},{1,0},{2,1},{3,2},{4,3},{5,4},{6,5},{7,6},{8,7},{9,8},{10,9... | collective-permute-start | bytes 1179656 | tf_op jit(solution)/shard_map/ppermute | solution.py:322
  70.5 12.0 %collective-permute-start.5 = (bf16[32,6144]{1,0:T(8,128)(2,1)S(1)}, bf16[32,6144]{1,0:T(8,128)(2,1)S(1)}, u32[]{:S(2)}, u32[]{:S(2)}) collective-permute-start(bf16[32,6144]{1,0:T(8,128)(2,1)S(1)} %collective-permute-done.3.refs_0_.refs_1_), channel_id=1, source_target_pairs={{0,1},{1,2},{2,3},{3,4},{4,5},{5,6},{6,7},{7,8},{8,9},{9,10},{10,1... | collective-permute-start | bytes 1179656 | tf_op jit(solution)/shard_map/ppermute | solution.py:320
  72.4 12.0 %collective-permute-start.4 = (bf16[32,6144]{1,0:T(8,128)(2,1)S(1)}, bf16[32,6144]{1,0:T(8,128)(2,1)S(1)}, u32[]{:S(2)}, u32[]{:S(2)}) collective-permute-start(bf16[32,6144]{1,0:T(8,128)(2,1)S(1)} %collective-permute-done.2.refs_1_.refs_2_), channel_id=1, source_target_pairs={{0,15},{1,0},{2,1},{3,2},{4,3},{5,4},{6,5},{7,6},{8,7},{9,8},{10,9... | collective-permute-start | bytes 1179656 | tf_op jit(solution)/shard_map/ppermute | solution.py:322
  82.5 11.1 %collective-permute-start.7 = (bf16[32,6144]{1,0:T(8,128)(2,1)S(1)}, bf16[32,6144]{1,0:T(8,128)(2,1)S(1)}, u32[]{:S(2)}, u32[]{:S(2)}) collective-permute-start(bf16[32,6144]{1,0:T(8,128)(2,1)S(1)} %collective-permute-done.5.refs_0_.refs_3_), channel_id=1, source_target_pairs={{0,1},{1,2},{2,3},{3,4},{4,5},{5,6},{6,7},{7,8},{8,9},{9,10},{10,1... | collective-permute-start | bytes 1179656 | tf_op jit(solution)/shard_map/ppermute | solution.py:320
  84.4 11.1 %collective-permute-start.6 = (bf16[32,6144]{1,0:T(8,128)(2,1)S(1)}, bf16[32,6144]{1,0:T(8,128)(2,1)S(1)}, u32[]{:S(2)}, u32[]{:S(2)}) collective-permute-start(bf16[32,6144]{1,0:T(8,128)(2,1)S(1)} %collective-permute-done.4.refs_1_.refs_4_), channel_id=1, source_target_pairs={{0,15},{1,0},{2,1},{3,2},{4,3},{5,4},{6,5},{7,6},{8,7},{9,8},{10,9... | collective-permute-start | bytes 1179656 | tf_op jit(solution)/shard_map/ppermute | solution.py:322
  93.6 10.2 %collective-permute-start.9 = (bf16[32,6144]{1,0:T(8,128)(2,1)S(1)}, bf16[32,6144]{1,0:T(8,128)(2,1)S(1)}, u32[]{:S(2)}, u32[]{:S(2)}) collective-permute-start(bf16[32,6144]{1,0:T(8,128)(2,1)S(1)} %collective-permute-done.7.refs_0_.refs_1_), channel_id=1, source_target_pairs={{0,1},{1,2},{2,3},{3,4},{4,5},{5,6},{6,7},{7,8},{8,9},{9,10},{10,1... | collective-permute-start | bytes 1179656 | tf_op jit(solution)/shard_map/ppermute | solution.py:320
  95.6 10.2 %collective-permute-start.8 = (bf16[32,6144]{1,0:T(8,128)(2,1)S(1)}, bf16[32,6144]{1,0:T(8,128)(2,1)S(1)}, u32[]{:S(2)}, u32[]{:S(2)}) collective-permute-start(bf16[32,6144]{1,0:T(8,128)(2,1)S(1)} %collective-permute-done.6.refs_1_.refs_2_), channel_id=1, source_target_pairs={{0,15},{1,0},{2,1},{3,2},{4,3},{5,4},{6,5},{7,6},{8,7},{9,8},{10,9... | collective-permute-start | bytes 1179656 | tf_op jit(solution)/shard_map/ppermute | solution.py:322
  103.8 9.7 %collective-permute-start.11 = (bf16[32,6144]{1,0:T(8,128)(2,1)S(1)}, bf16[32,6144]{1,0:T(8,128)(2,1)S(1)}, u32[]{:S(2)}, u32[]{:S(2)}) collective-permute-start(bf16[32,6144]{1,0:T(8,128)(2,1)S(1)} %collective-permute-done.9.refs_0_.refs_3_), channel_id=1, source_target_pairs={{0,1},{1,2},{2,3},{3,4},{4,5},{5,6},{6,7},{7,8},{8,9},{9,10},{10,1... | collective-permute-start | bytes 1179656 | tf_op jit(solution)/shard_map/ppermute | solution.py:320
  105.8 9.7 %collective-permute-start.10 = (bf16[32,6144]{1,0:T(8,128)(2,1)S(1)}, bf16[32,6144]{1,0:T(8,128)(2,1)S(1)}, u32[]{:S(2)}, u32[]{:S(2)}) collective-permute-start(bf16[32,6144]{1,0:T(8,128)(2,1)S(1)} %collective-permute-done.8.refs_1_.refs_4_), channel_id=1, source_target_pairs={{0,15},{1,0},{2,1},{3,2},{4,3},{5,4},{6,5},{7,6},{8,7},{9,8},{10,9... | collective-permute-start | bytes 1179656 | tf_op jit(solution)/shard_map/ppermute | solution.py:322
  113.5 9.7 %collective-permute-start.13 = (bf16[32,6144]{1,0:T(8,128)(2,1)S(1)}, bf16[32,6144]{1,0:T(8,128)(2,1)S(1)}, u32[]{:S(2)}, u32[]{:S(2)}) collective-permute-start(bf16[32,6144]{1,0:T(8,128)(2,1)S(1)} %collective-permute-done.11.refs_0_.refs_1_), channel_id=1, source_target_pairs={{0,1},{1,2},{2,3},{3,4},{4,5},{5,6},{6,7},{7,8},{8,9},{9,10},{10,1... | collective-permute-start | bytes 1179656 | tf_op jit(solution)/shard_map/ppermute | solution.py:320
  115.5 9.7 %collective-permute-start.12 = (bf16[32,6144]{1,0:T(8,128)(2,1)S(1)}, bf16[32,6144]{1,0:T(8,128)(2,1)S(1)}, u32[]{:S(2)}, u32[]{:S(2)}) collective-permute-start(bf16[32,6144]{1,0:T(8,128)(2,1)S(1)} %collective-permute-done.10.refs_1_.refs_2_), channel_id=1, source_target_pairs={{0,15},{1,0},{2,1},{3,2},{4,3},{5,4},{6,5},{7,6},{8,7},{9,8},{10,9... | collective-permute-start | bytes 1179656 | tf_op jit(solution)/shard_map/ppermute | solution.py:322
  123.3 10.2 %collective-permute-start.14 = (bf16[32,6144]{1,0:T(8,128)(2,1)S(1)}, bf16[32,6144]{1,0:T(8,128)(2,1)S(1)}, u32[]{:S(2)}, u32[]{:S(2)}) collective-permute-start(bf16[32,6144]{1,0:T(8,128)(2,1)S(1)} %collective-permute-done.13.refs_0_.refs_3_), channel_id=1, source_target_pairs={{0,1},{1,2},{2,3},{3,4},{4,5},{5,6},{6,7},{7,8},{8,9},{9,10},{10,1... | collective-permute-start | bytes 1179656 | tf_op jit(solution)/shard_map/ppermute | solution.py:320
  128.0 1.6 copy-start.1
  134.1 42.8 %copy-start.4 = (s32[256,4]{0,1:T(4,128)S(1)}, s32[256,4]{0,1:T(4,128)}, u32[]{:S(2)}) copy-start(s32[256,4]{0,1:T(4,128)} %param.7) | copy-start | bytes 12292
  135.9 15.2 %all-to-all-start.1 = ((f32[16,1,64]{2,1,0:T(1,128)}), f32[16,1,64]{2,1,0:T(1,128)S(1)}, u32[]{:S(2)}, u32[]{:S(2)}) async-start(f32[16,1,64]{2,1,0:T(1,128)} %get-tuple-element.101), calls=%async_computation.1 | async-start | bytes 16384 | tf_op jit(solution)/shard_map/all_to_all | solution.py:331
  140.7 1.9 %copy-start.2 = (f32[128,6144]{1,0:T(8,128)S(1)}, f32[128,6144]{1,0:T(8,128)}, u32[]{:S(2)}) copy-start(f32[128,6144]{1,0:T(8,128)} %copy-done.1) | copy-start | bytes 9437188
  151.1 0.6 copy-start.5
